TPU v7x, 32 devices: a whole 2x2x4 slice. The times are simulated.
32 devices in a mesh: pipe: 4 (over y, x), dp: 8 (over z, core).
Axes of the slice: x: 2, y: 2, z: 4, core: 2. Of those that a mesh axis runs over, the one named last changes fastest.
Arguments:
- video: bfloat16 [4, 8, 3, 16, 8, 128], P(None, 'dp'), may hold values from -6 to 6
- cotangent: bfloat16 [4, 8, 3, 16, 8, 128], P(None, 'dp'), may hold values from -6 to 6
- weights: bfloat16 [4, 3456, 128], P('pipe'), may hold values from -0.109375 to 0.109375
- gains: float32 [4, 128], P('pipe'), may hold values from 0.1 to 1.9
Outputs:
- segment_out: bfloat16 [4, 4, 8, 3, 16, 8, 128], P('pipe', None, 'dp')
- in_grad: bfloat16 [4, 4, 8, 3, 16, 8, 128], P('pipe', None, 'dp')
- weight_grad: float32 [4, 442368], P('pipe', 'dp')
All inputs are finite; a program needn't handle non-finite values.
Results may differ from a plain program's by a relative error of at most 0.025.
Values may be sent and summed in bfloat16 or wider, within the bound.
No kernel may reach another device: no remote copies, remote signals or barrier semaphores. Data moves between devices by JAX's collectives and lax.ppermute only.
A program may use at most 64 MiB of HBM per device.

v0:
```python
import math

import jax
import jax.numpy as jnp
from jax import lax
from jax.sharding import PartitionSpec as P

GROUPS = 32


def shifted(value, axis, steps):
    count = lax.axis_size(axis)
    initial, last = (max(0, -steps), min(count, count - steps))
    return lax.ppermute(value, axis, [(source, source + steps) for source in range(initial, last)])


def norm_act(values, gain):
    batch, frames, rows, cols, chans = values.shape
    grouped = values.reshape(batch, frames, rows, cols, GROUPS, chans // GROUPS)
    mean = jnp.mean(grouped, axis=(1, 2, 3, 5), keepdims=True)
    centred = grouped - mean
    var = jnp.mean(centred * centred, axis=(1, 2, 3, 5), keepdims=True)
    normed = (centred * lax.rsqrt(var + 1e-06)).reshape(values.shape) * gain
    return jax.nn.silu(normed)


def patches(act):
    frames, rows, cols = (act.shape[1], act.shape[2], act.shape[3])
    leading = act[:, :1]
    padded = jnp.concatenate([leading, leading, act], axis=1)
    padded = jnp.pad(padded, ((0, 0), (0, 0), (1, 1), (1, 1), (0, 0)))
    pieces = [
        padded[
            :, frame_off : frame_off + frames, row_off : row_off + rows, col_off : col_off + cols, :
        ]
        for frame_off in range(3)
        for row_off in range(3)
        for col_off in range(3)
    ]
    return jnp.concatenate(pieces, axis=-1).reshape(-1, 27 * act.shape[-1])


def forward(inputs, weight, gain):
    values = inputs.astype(jnp.float32)
    act = norm_act(values, gain).astype(jnp.bfloat16)
    cols_mat = patches(act)
    branch = jnp.dot(cols_mat, weight, preferred_element_type=jnp.float32).reshape(inputs.shape)
    return ((values + branch).astype(jnp.bfloat16), cols_mat)


def backward(inputs, grad, weight, gain, cols_mat):
    values = inputs.astype(jnp.float32)
    flat_grad = grad.reshape(-1, grad.shape[-1])
    term = lax.dot_general(
        cols_mat, flat_grad, (((0,), (0,)), ((), ())), preferred_element_type=jnp.float32
    )
    grad_cols = lax.dot_general(
        flat_grad, weight, (((1,), (1,)), ((), ())), preferred_element_type=jnp.float32
    )
    _, pull_cols = jax.vjp(patches, jnp.zeros(inputs.shape, jnp.float32))
    grad_act = pull_cols(grad_cols)[0]
    _, pull_norm = jax.vjp(lambda field: norm_act(field, gain), values)
    grad_in = grad.astype(jnp.float32) + pull_norm(grad_act)[0]
    return (grad_in.astype(jnp.bfloat16), term)


def place(buffer, slot, value, valid):
    older = lax.dynamic_index_in_dim(buffer, slot, 0, False)
    return lax.dynamic_update_index_in_dim(buffer, jnp.where(valid, value, older), slot, 0)


def body(video, cotangent, weights, gains):
    segment = lax.axis_index("pipe")
    sections = lax.axis_size("pipe")
    micro = video.shape[0]
    ticks = micro + sections - 1
    weight = weights[0]
    gain = gains[0]
    is_first = segment == 0
    is_last = segment == sections - 1
    unit_shape = video.shape[1:]
    kept_init = jnp.zeros((1, 1), jnp.bfloat16)

    def forward_tick(carry, tick):
        received, saved, outputs, kept = carry
        index = tick - segment
        valid = (index >= 0) & (index < micro)
        slot = jnp.clip(index, 0, micro - 1)
        unit_in = jnp.where(is_first, lax.dynamic_index_in_dim(video, slot, 0, False), received)
        result, cols_mat = forward(unit_in, weight, gain)
        saved = place(saved, slot, unit_in, valid)
        outputs = place(outputs, slot, result, valid)
        received = shifted(result, "pipe", 1)
        return ((received, saved, outputs, kept), None)

    empty = jnp.zeros(video.shape, jnp.bfloat16)
    start = (jnp.zeros(unit_shape, jnp.bfloat16), empty, empty, kept_init)
    (_, saved, outputs, kept), _ = lax.scan(forward_tick, start, jnp.arange(ticks, dtype=jnp.int32))
    total_init = jnp.zeros(weight.shape, jnp.float32)

    def backward_tick(carry, tick):
        received, grads_out, total = carry
        index = tick - (sections - 1 - segment)
        valid = (index >= 0) & (index < micro)
        slot = jnp.clip(index, 0, micro - 1)
        grad = jnp.where(is_last, lax.dynamic_index_in_dim(cotangent, slot, 0, False), received)
        unit_in = lax.dynamic_index_in_dim(saved, slot, 0, False)
        cols_mat = patches(norm_act(unit_in.astype(jnp.float32), gain).astype(jnp.bfloat16))
        grad_in, term = backward(unit_in, grad, weight, gain, cols_mat)
        term = jnp.where(valid, term, 0.0)
        total = total + term
        grads_out = place(grads_out, slot, grad_in, valid)
        received = shifted(grad_in, "pipe", -1)
        return ((received, grads_out, total), None)

    start_back = (jnp.zeros(unit_shape, jnp.bfloat16), empty, total_init)
    (_, grads_out, total), _ = lax.scan(
        backward_tick, start_back, jnp.arange(ticks, dtype=jnp.int32)
    )
    share = lax.psum_scatter(
        total.reshape(-1).astype(jnp.bfloat16), "dp", scatter_dimension=0, tiled=True
    ).astype(jnp.float32)
    clip_total = unit_shape[0] * lax.axis_size("dp")
    scale = 1.0 / math.sqrt(micro * clip_total * unit_shape[1] * unit_shape[2] * unit_shape[3])
    return (outputs[None], grads_out[None], (share * scale)[None])


def solution(mesh):
    in_specs = (
        P(None, "dp", None, None, None, None),
        P(None, "dp", None, None, None, None),
        P("pipe", None, None),
        P("pipe", None),
    )
    out_specs = (
        P("pipe", None, "dp", None, None, None, None),
        P("pipe", None, "dp", None, None, None, None),
        P("pipe", "dp"),
    )
    return jax.shard_map(body, mesh=mesh, in_specs=in_specs, out_specs=out_specs, check_vma=False)
```

profile of v0, /device:TPU:0, one launch (start us, length us, event | category | flops | bytes accessed | tf_op | source)
XLA Modules:
  0.0 314.2 jit_solution(17953913452624108127)
XLA Ops:
  7.4 94.1 %while.33 = (s32[]{:T(128)}, bf16[1,3,16,8,128]{4,3,2,1,0:T(8,128)(2,1)S(1)}, bf16[4,1,3,16,8,128]{5,4,3,2,1,0:T(8,128)(2,1)S(1)}, bf16[4,1,3,16,8,128]{5,4,3,2,...) while((s32[]{:T(128)}, ...), condition=%wide.region_5.6_spmd, body=%wide.region_0.5_spmd.sunk | while | flops 341573664 | bytes 16430921 | solution.py:98
  8.7 1.0 bitcast_dynamic-update-slice_fusion.6
  13.8 4.8 %collective-permute-start = (bf16[1,3,16,8,128]{4,3,2,1,0:T(8,128)(2,1)S(1)}, bf16[1,3,16,8,128]{4,3,2,1,0:T(8,128)(2,1)S(1)}, u32[]{:S(2)}, u32[]{:S(2)}) collective-permute-start(bf16[1,3,16,8,128]{4,3,2,1,0:T(8,128)(2,1)S(1)} %get-tuple-element.544), channel_id=1, source_target_pairs={{0,8},{8,16},{16,24},{1,9},{9,17},{17,25},{2,10},{10,18},{18,26},{... | collective-permute-start | bytes 294920 | tf_op jit(solution)/shard_map/while/body/eval_jaxpr/ppermute | solution.py:14
  18.6 2.2 collective-permute-done
  22.1 1.0 bitcast_dynamic-update-slice_fusion.6
  27.2 4.3 %collective-permute-start = (bf16[1,3,16,8,128]{4,3,2,1,0:T(8,128)(2,1)S(1)}, bf16[1,3,16,8,128]{4,3,2,1,0:T(8,128)(2,1)S(1)}, u32[]{:S(2)}, u32[]{:S(2)}) collective-permute-start(bf16[1,3,16,8,128]{4,3,2,1,0:T(8,128)(2,1)S(1)} %get-tuple-element.544), channel_id=1, source_target_pairs={{0,8},{8,16},{16,24},{1,9},{9,17},{17,25},{2,10},{10,18},{18,26},{... | collective-permute-start | bytes 294920 | tf_op jit(solution)/shard_map/while/body/eval_jaxpr/ppermute | solution.py:14
  31.5 2.2 collective-permute-done
  35.0 1.0 bitcast_dynamic-update-slice_fusion.6
  40.0 4.3 %collective-permute-start = (bf16[1,3,16,8,128]{4,3,2,1,0:T(8,128)(2,1)S(1)}, bf16[1,3,16,8,128]{4,3,2,1,0:T(8,128)(2,1)S(1)}, u32[]{:S(2)}, u32[]{:S(2)}) collective-permute-start(bf16[1,3,16,8,128]{4,3,2,1,0:T(8,128)(2,1)S(1)} %get-tuple-element.544), channel_id=1, source_target_pairs={{0,8},{8,16},{16,24},{1,9},{9,17},{17,25},{2,10},{10,18},{18,26},{... | collective-permute-start | bytes 294920 | tf_op jit(solution)/shard_map/while/body/eval_jaxpr/ppermute | solution.py:14
  44.3 2.2 collective-permute-done
  52.9 5.2 %collective-permute-start = (bf16[1,3,16,8,128]{4,3,2,1,0:T(8,128)(2,1)S(1)}, bf16[1,3,16,8,128]{4,3,2,1,0:T(8,128)(2,1)S(1)}, u32[]{:S(2)}, u32[]{:S(2)}) collective-permute-start(bf16[1,3,16,8,128]{4,3,2,1,0:T(8,128)(2,1)S(1)} %get-tuple-element.544), channel_id=1, source_target_pairs={{0,8},{8,16},{16,24},{1,9},{9,17},{17,25},{2,10},{10,18},{18,26},{... | collective-permute-start | bytes 294920 | tf_op jit(solution)/shard_map/while/body/eval_jaxpr/ppermute | solution.py:14
  58.1 2.2 collective-permute-done
  66.6 5.2 %collective-permute-start = (bf16[1,3,16,8,128]{4,3,2,1,0:T(8,128)(2,1)S(1)}, bf16[1,3,16,8,128]{4,3,2,1,0:T(8,128)(2,1)S(1)}, u32[]{:S(2)}, u32[]{:S(2)}) collective-permute-start(bf16[1,3,16,8,128]{4,3,2,1,0:T(8,128)(2,1)S(1)} %get-tuple-element.544), channel_id=1, source_target_pairs={{0,8},{8,16},{16,24},{1,9},{9,17},{17,25},{2,10},{10,18},{18,26},{... | collective-permute-start | bytes 294920 | tf_op jit(solution)/shard_map/while/body/eval_jaxpr/ppermute | solution.py:14
  71.8 2.2 collective-permute-done
  80.4 5.2 %collective-permute-start = (bf16[1,3,16,8,128]{4,3,2,1,0:T(8,128)(2,1)S(1)}, bf16[1,3,16,8,128]{4,3,2,1,0:T(8,128)(2,1)S(1)}, u32[]{:S(2)}, u32[]{:S(2)}) collective-permute-start(bf16[1,3,16,8,128]{4,3,2,1,0:T(8,128)(2,1)S(1)} %get-tuple-element.544), channel_id=1, source_target_pairs={{0,8},{8,16},{16,24},{1,9},{9,17},{17,25},{2,10},{10,18},{18,26},{... | collective-permute-start | bytes 294920 | tf_op jit(solution)/shard_map/while/body/eval_jaxpr/ppermute | solution.py:14
  85.6 2.2 collective-permute-done
  94.1 5.2 %collective-permute-start = (bf16[1,3,16,8,128]{4,3,2,1,0:T(8,128)(2,1)S(1)}, bf16[1,3,16,8,128]{4,3,2,1,0:T(8,128)(2,1)S(1)}, u32[]{:S(2)}, u32[]{:S(2)}) collective-permute-start(bf16[1,3,16,8,128]{4,3,2,1,0:T(8,128)(2,1)S(1)} %get-tuple-element.544), channel_id=1, source_target_pairs={{0,8},{8,16},{16,24},{1,9},{9,17},{17,25},{2,10},{10,18},{18,26},{... | collective-permute-start | bytes 294920 | tf_op jit(solution)/shard_map/while/body/eval_jaxpr/ppermute | solution.py:14
  99.3 2.2 collective-permute-done
  102.4 140.3 %while.34 = (s32[]{:T(128)}, bf16[1,3,16,8,128]{4,3,2,1,0:T(8,128)(2,1)S(1)}, bf16[4,1,3,16,8,128]{5,4,3,2,1,0:T(8,128)(2,1)}, f32[3456,128]{1,0:T(8,128)}, pred...) while((s32[]{:T(128)}, ...), condition=%wide.region_15.16_spmd.clone, body=%wide.region_6.15_spmd.clone.sunk | while | flops 686339328 | bytes 53340172 | solution.py:117
  104.6 2.0 convolution_bitcast_fusion.3
  106.7 1.7 fusion.197
  108.5 2.7 pad_add_fusion.2
  115.0 1.3 collective-permute-start.1
  118.0 1.8 fusion.226
  119.9 2.9 collective-permute-done.1
  124.9 2.0 convolution_bitcast_fusion.3
  127.0 1.7 fusion.197
  128.8 2.7 pad_add_fusion.2
  135.3 1.3 collective-permute-start.1
  138.3 1.8 fusion.226
  140.2 2.9 collective-permute-done.1
  145.2 2.0 convolution_bitcast_fusion.3
  147.3 1.7 fusion.197
  149.1 2.7 pad_add_fusion.2
  155.6 1.3 collective-permute-start.1
  158.7 1.8 fusion.226
  160.5 2.5 collective-permute-done.1
  165.2 2.0 convolution_bitcast_fusion.3
  167.2 1.7 fusion.197
  169.1 2.7 pad_add_fusion.2
  175.5 1.3 collective-permute-start.1
  178.6 1.8 fusion.226
  180.4 2.5 collective-permute-done.1
  185.1 2.0 convolution_bitcast_fusion.3
  187.1 1.7 fusion.197
  189.0 2.7 pad_add_fusion.2
  195.5 1.3 collective-permute-start.1
  198.5 1.8 fusion.226
  200.3 2.5 collective-permute-done.1
  205.0 2.0 convolution_bitcast_fusion.3
  207.1 1.7 fusion.197
  208.9 2.7 pad_add_fusion.2
  215.4 1.3 collective-permute-start.1
  218.4 1.8 fusion.226
  220.3 2.5 collective-permute-done.1
  224.9 2.0 convolution_bitcast_fusion.3
  227.0 1.7 fusion.197
  228.8 2.7 pad_add_fusion.2
  235.3 1.3 collective-permute-start.1
  238.4 1.8 fusion.226
  240.2 2.5 collective-permute-done.1
  242.7 2.5 convert_bitcast_fusion.1
  246.5 59.3 %all-reduce.33.cloned.1.call-done = bf16[442368]{0:T(1024)(128)(2,1)} async-done(((bf16[442368]{0:T(1024)(128)(2,1)}), bf16[442368]{0:T(1024)(128)(2,1)}) %all-reduce.33.cloned.1.call-update) | async-done | bytes 884752
  305.8 1.6 convert_multiply_fusion
  (817 shorter events, 86.3 us)
Async XLA Ops:
  7.2 298.6 %all-reduce.33.cloned.1.call-start = ((), (), s32[]{:S(2)}) async-start(), calls=%async_computation | async-start | bytes 1769472
  11.5 1.0 copy-start.4
  11.7 1.2 copy-start
  13.8 7.0 %collective-permute-start = (bf16[1,3,16,8,128]{4,3,2,1,0:T(8,128)(2,1)S(1)}, bf16[1,3,16,8,128]{4,3,2,1,0:T(8,128)(2,1)S(1)}, u32[]{:S(2)}, u32[]{:S(2)}) collective-permute-start(bf16[1,3,16,8,128]{4,3,2,1,0:T(8,128)(2,1)S(1)} %get-tuple-element.544), channel_id=1, source_target_pairs={{0,8},{8,16},{16,24},{1,9},{9,17},{17,25},{2,10},{10,18},{18,26},{... | collective-permute-start | bytes 294920 | tf_op jit(solution)/shard_map/while/body/eval_jaxpr/ppermute | solution.py:14
  24.9 1.0 copy-start.4
  25.1 1.2 copy-start
  27.2 6.5 %collective-permute-start = (bf16[1,3,16,8,128]{4,3,2,1,0:T(8,128)(2,1)S(1)}, bf16[1,3,16,8,128]{4,3,2,1,0:T(8,128)(2,1)S(1)}, u32[]{:S(2)}, u32[]{:S(2)}) collective-permute-start(bf16[1,3,16,8,128]{4,3,2,1,0:T(8,128)(2,1)S(1)} %get-tuple-element.544), channel_id=1, source_target_pairs={{0,8},{8,16},{16,24},{1,9},{9,17},{17,25},{2,10},{10,18},{18,26},{... | collective-permute-start | bytes 294920 | tf_op jit(solution)/shard_map/while/body/eval_jaxpr/ppermute | solution.py:14
  37.7 1.0 copy-start.4
  38.0 1.2 copy-start
  40.0 6.5 %collective-permute-start = (bf16[1,3,16,8,128]{4,3,2,1,0:T(8,128)(2,1)S(1)}, bf16[1,3,16,8,128]{4,3,2,1,0:T(8,128)(2,1)S(1)}, u32[]{:S(2)}, u32[]{:S(2)}) collective-permute-start(bf16[1,3,16,8,128]{4,3,2,1,0:T(8,128)(2,1)S(1)} %get-tuple-element.544), channel_id=1, source_target_pairs={{0,8},{8,16},{16,24},{1,9},{9,17},{17,25},{2,10},{10,18},{18,26},{... | collective-permute-start | bytes 294920 | tf_op jit(solution)/shard_map/while/body/eval_jaxpr/ppermute | solution.py:14
  50.6 1.0 copy-start.4
  50.8 1.2 copy-start
  52.9 7.4 %collective-permute-start = (bf16[1,3,16,8,128]{4,3,2,1,0:T(8,128)(2,1)S(1)}, bf16[1,3,16,8,128]{4,3,2,1,0:T(8,128)(2,1)S(1)}, u32[]{:S(2)}, u32[]{:S(2)}) collective-permute-start(bf16[1,3,16,8,128]{4,3,2,1,0:T(8,128)(2,1)S(1)} %get-tuple-element.544), channel_id=1, source_target_pairs={{0,8},{8,16},{16,24},{1,9},{9,17},{17,25},{2,10},{10,18},{18,26},{... | collective-permute-start | bytes 294920 | tf_op jit(solution)/shard_map/while/body/eval_jaxpr/ppermute | solution.py:14
  64.3 1.0 copy-start.4
  64.5 1.2 copy-start
  66.6 7.4 %collective-permute-start = (bf16[1,3,16,8,128]{4,3,2,1,0:T(8,128)(2,1)S(1)}, bf16[1,3,16,8,128]{4,3,2,1,0:T(8,128)(2,1)S(1)}, u32[]{:S(2)}, u32[]{:S(2)}) collective-permute-start(bf16[1,3,16,8,128]{4,3,2,1,0:T(8,128)(2,1)S(1)} %get-tuple-element.544), channel_id=1, source_target_pairs={{0,8},{8,16},{16,24},{1,9},{9,17},{17,25},{2,10},{10,18},{18,26},{... | collective-permute-start | bytes 294920 | tf_op jit(solution)/shard_map/while/body/eval_jaxpr/ppermute | solution.py:14
  78.1 1.0 copy-start.4
  78.3 1.2 copy-start
  80.4 7.4 %collective-permute-start = (bf16[1,3,16,8,128]{4,3,2,1,0:T(8,128)(2,1)S(1)}, bf16[1,3,16,8,128]{4,3,2,1,0:T(8,128)(2,1)S(1)}, u32[]{:S(2)}, u32[]{:S(2)}) collective-permute-start(bf16[1,3,16,8,128]{4,3,2,1,0:T(8,128)(2,1)S(1)} %get-tuple-element.544), channel_id=1, source_target_pairs={{0,8},{8,16},{16,24},{1,9},{9,17},{17,25},{2,10},{10,18},{18,26},{... | collective-permute-start | bytes 294920 | tf_op jit(solution)/shard_map/while/body/eval_jaxpr/ppermute | solution.py:14
  91.8 1.0 copy-start.4
  92.1 1.2 copy-start
  94.1 7.4 %collective-permute-start = (bf16[1,3,16,8,128]{4,3,2,1,0:T(8,128)(2,1)S(1)}, bf16[1,3,16,8,128]{4,3,2,1,0:T(8,128)(2,1)S(1)}, u32[]{:S(2)}, u32[]{:S(2)}) collective-permute-start(bf16[1,3,16,8,128]{4,3,2,1,0:T(8,128)(2,1)S(1)} %get-tuple-element.544), channel_id=1, source_target_pairs={{0,8},{8,16},{16,24},{1,9},{9,17},{17,25},{2,10},{10,18},{18,26},{... | collective-permute-start | bytes 294920 | tf_op jit(solution)/shard_map/while/body/eval_jaxpr/ppermute | solution.py:14
  101.5 0.9 copy-start.1
  108.5 3.7 %copy-start.5 = (f32[1,128]{1,0:T(1,128)S(1)}, f32[1,128]{1,0:T(1,128)}, u32[]{:S(2)}) copy-start(f32[1,128]{1,0:T(1,128)} %get-tuple-element.677) | copy-start | bytes 1540 | tf_op jit(solution)/shard_map/while
  115.0 7.8 %collective-permute-start.1 = (bf16[1,3,16,8,128]{4,3,2,1,0:T(8,128)(2,1)S(1)}, bf16[1,3,16,8,128]{4,3,2,1,0:T(8,128)(2,1)S(1)}, u32[]{:S(2)}, u32[]{:S(2)}) collective-permute-start(bf16[1,3,16,8,128]{4,3,2,1,0:T(8,128)(2,1)S(1)} %get-tuple-element.587), channel_id=1, source_target_pairs={{8,0},{16,8},{24,16},{9,1},{17,9},{25,17},{10,2},{18,10},{26,18},{... | collective-permute-start | bytes 294920 | tf_op jit(solution)/shard_map/while/body/eval_jaxpr/ppermute | solution.py:14
  116.6 1.5 copy-start.2
  119.8 2.9 copy-start.3
  128.8 3.7 %copy-start.5 = (f32[1,128]{1,0:T(1,128)S(1)}, f32[1,128]{1,0:T(1,128)}, u32[]{:S(2)}) copy-start(f32[1,128]{1,0:T(1,128)} %get-tuple-element.677) | copy-start | bytes 1540 | tf_op jit(solution)/shard_map/while
  135.3 7.8 %collective-permute-start.1 = (bf16[1,3,16,8,128]{4,3,2,1,0:T(8,128)(2,1)S(1)}, bf16[1,3,16,8,128]{4,3,2,1,0:T(8,128)(2,1)S(1)}, u32[]{:S(2)}, u32[]{:S(2)}) collective-permute-start(bf16[1,3,16,8,128]{4,3,2,1,0:T(8,128)(2,1)S(1)} %get-tuple-element.587), channel_id=1, source_target_pairs={{8,0},{16,8},{24,16},{9,1},{17,9},{25,17},{10,2},{18,10},{26,18},{... | collective-permute-start | bytes 294920 | tf_op jit(solution)/shard_map/while/body/eval_jaxpr/ppermute | solution.py:14
  136.9 1.5 copy-start.2
  140.2 2.9 copy-start.3
  149.1 3.7 %copy-start.5 = (f32[1,128]{1,0:T(1,128)S(1)}, f32[1,128]{1,0:T(1,128)}, u32[]{:S(2)}) copy-start(f32[1,128]{1,0:T(1,128)} %get-tuple-element.677) | copy-start | bytes 1540 | tf_op jit(solution)/shard_map/while
  155.6 7.4 %collective-permute-start.1 = (bf16[1,3,16,8,128]{4,3,2,1,0:T(8,128)(2,1)S(1)}, bf16[1,3,16,8,128]{4,3,2,1,0:T(8,128)(2,1)S(1)}, u32[]{:S(2)}, u32[]{:S(2)}) collective-permute-start(bf16[1,3,16,8,128]{4,3,2,1,0:T(8,128)(2,1)S(1)} %get-tuple-element.587), channel_id=1, source_target_pairs={{8,0},{16,8},{24,16},{9,1},{17,9},{25,17},{10,2},{18,10},{26,18},{... | collective-permute-start | bytes 294920 | tf_op jit(solution)/shard_map/while/body/eval_jaxpr/ppermute | solution.py:14
  157.2 1.5 copy-start.2
  160.5 2.5 copy-start.3
  169.1 3.7 %copy-start.5 = (f32[1,128]{1,0:T(1,128)S(1)}, f32[1,128]{1,0:T(1,128)}, u32[]{:S(2)}) copy-start(f32[1,128]{1,0:T(1,128)} %get-tuple-element.677) | copy-start | bytes 1540 | tf_op jit(solution)/shard_map/while
  175.5 7.4 %collective-permute-start.1 = (bf16[1,3,16,8,128]{4,3,2,1,0:T(8,128)(2,1)S(1)}, bf16[1,3,16,8,128]{4,3,2,1,0:T(8,128)(2,1)S(1)}, u32[]{:S(2)}, u32[]{:S(2)}) collective-permute-start(bf16[1,3,16,8,128]{4,3,2,1,0:T(8,128)(2,1)S(1)} %get-tuple-element.587), channel_id=1, source_target_pairs={{8,0},{16,8},{24,16},{9,1},{17,9},{25,17},{10,2},{18,10},{26,18},{... | collective-permute-start | bytes 294920 | tf_op jit(solution)/shard_map/while/body/eval_jaxpr/ppermute | solution.py:14
  177.1 1.5 copy-start.2
  180.4 2.5 copy-start.3
  189.0 3.7 %copy-start.5 = (f32[1,128]{1,0:T(1,128)S(1)}, f32[1,128]{1,0:T(1,128)}, u32[]{:S(2)}) copy-start(f32[1,128]{1,0:T(1,128)} %get-tuple-element.677) | copy-start | bytes 1540 | tf_op jit(solution)/shard_map/while
  195.5 7.4 %collective-permute-start.1 = (bf16[1,3,16,8,128]{4,3,2,1,0:T(8,128)(2,1)S(1)}, bf16[1,3,16,8,128]{4,3,2,1,0:T(8,128)(2,1)S(1)}, u32[]{:S(2)}, u32[]{:S(2)}) collective-permute-start(bf16[1,3,16,8,128]{4,3,2,1,0:T(8,128)(2,1)S(1)} %get-tuple-element.587), channel_id=1, source_target_pairs={{8,0},{16,8},{24,16},{9,1},{17,9},{25,17},{10,2},{18,10},{26,18},{... | collective-permute-start | bytes 294920 | tf_op jit(solution)/shard_map/while/body/eval_jaxpr/ppermute | solution.py:14
  197.0 1.5 copy-start.2
  200.3 2.5 copy-start.3
  208.9 3.7 %copy-start.5 = (f32[1,128]{1,0:T(1,128)S(1)}, f32[1,128]{1,0:T(1,128)}, u32[]{:S(2)}) copy-start(f32[1,128]{1,0:T(1,128)} %get-tuple-element.677) | copy-start | bytes 1540 | tf_op jit(solution)/shard_map/while
  215.4 7.4 %collective-permute-start.1 = (bf16[1,3,16,8,128]{4,3,2,1,0:T(8,128)(2,1)S(1)}, bf16[1,3,16,8,128]{4,3,2,1,0:T(8,128)(2,1)S(1)}, u32[]{:S(2)}, u32[]{:S(2)}) collective-permute-start(bf16[1,3,16,8,128]{4,3,2,1,0:T(8,128)(2,1)S(1)} %get-tuple-element.587), channel_id=1, source_target_pairs={{8,0},{16,8},{24,16},{9,1},{17,9},{25,17},{10,2},{18,10},{26,18},{... | collective-permute-start | bytes 294920 | tf_op jit(solution)/shard_map/while/body/eval_jaxpr/ppermute | solution.py:14
  217.0 1.5 copy-start.2
  220.2 2.5 copy-start.3
  228.8 3.7 %copy-start.5 = (f32[1,128]{1,0:T(1,128)S(1)}, f32[1,128]{1,0:T(1,128)}, u32[]{:S(2)}) copy-start(f32[1,128]{1,0:T(1,128)} %get-tuple-element.677) | copy-start | bytes 1540 | tf_op jit(solution)/shard_map/while
  235.3 7.4 %collective-permute-start.1 = (bf16[1,3,16,8,128]{4,3,2,1,0:T(8,128)(2,1)S(1)}, bf16[1,3,16,8,128]{4,3,2,1,0:T(8,128)(2,1)S(1)}, u32[]{:S(2)}, u32[]{:S(2)}) collective-permute-start(bf16[1,3,16,8,128]{4,3,2,1,0:T(8,128)(2,1)S(1)} %get-tuple-element.587), channel_id=1, source_target_pairs={{8,0},{16,8},{24,16},{9,1},{17,9},{25,17},{10,2},{18,10},{26,18},{... | collective-permute-start | bytes 294920 | tf_op jit(solution)/shard_map/while/body/eval_jaxpr/ppermute | solution.py:14
  236.9 1.5 copy-start.2
  240.2 2.5 copy-start.3
  242.7 2.5 copy-start.6
Sparse Core Ops, SparseCore 0:
  245.3 60.4 all-reduce.32
where the time goes:
time: 316 us; the launch traced here: 314 us
  waiting for transfers between devices  93.1 us (29%)
  local copies, waits for them, and re-layouts  60.9 us (19%)
  other arithmetic  56.5 us (18%)
  starting transfers between devices  43.3 us (14%)
  matrix products  33.1 us (10%)
  between operations  14.8 us (5%)
  loops' own time  12.6 us (4%)
    unnamed x2, waiting for transfers between devices  59.3 us
    ppermute x14, starting transfers between devices, shifted(): lax.ppermute(value, axis, [(source, source + steps) for source in range(i...  43.3 us
    ppermute x14, waiting for transfers between devices, shifted(): lax.ppermute(value, axis, [(source, source + steps) for source in range(i...  33.7 us
    while x413, local copies, waits for them, and re-layouts  19 us
    add_any x7, other arithmetic, patches(): padded[:, frame_off:frame_off + frames, row_off:row_off + rows, col_off:c...  18.8 us
    dot_general x7, matrix products, backward(): lax.dot_general(flat_grad, weight, (((1,), (1,)), ((), ())), preferred_el...  14.3 us
    split x14, local copies, waits for them, and re-layouts, patches(): return jnp.concatenate(pieces, axis=-1).reshape(-1, 27 * act.shape[-1])  12.9 us
    dot_general x7, matrix products, backward(): lax.dot_general(cols_mat, flat_grad, (((0,), (0,)), ((), ())), preferred_...  12.6 us
  transfers between devices with their start and end apart: 15, of which 15 were waited for; matrix products, arithmetic and copies ran while one was open for 7% of the time, Pallas kernels for 0%

commit v1 on v0

v1 whole, which is shorter than its diff:
```python
import functools
import math

import jax
import jax.numpy as jnp
from jax import lax
from jax.experimental import pallas as pl
from jax.experimental.pallas import tpu as pltpu
from jax.sharding import PartitionSpec as P

GROUPS = 32
EPS = 1e-06
BF, F32 = jnp.bfloat16, jnp.float32
VMEM_LIMIT = 28 * 1024 * 1024
VM = pl.BlockSpec(memory_space=pltpu.VMEM)
SM = pl.BlockSpec(memory_space=pltpu.SMEM)
ANY = pl.BlockSpec(memory_space=pl.ANY)


def call(kernel, out_shape, in_specs, out_specs, scratch=(), flops=0, moved=0):
    return pl.pallas_call(
        kernel,
        out_shape=out_shape,
        in_specs=in_specs,
        out_specs=out_specs,
        scratch_shapes=list(scratch),
        compiler_params=pltpu.CompilerParams(vmem_limit_bytes=VMEM_LIMIT),
        cost_estimate=pl.CostEstimate(flops=flops, bytes_accessed=moved, transcendentals=0),
    )


def swap(value, axis, bits):
    count = lax.axis_size(axis)
    return lax.ppermute(value, axis, [(i, i ^ bits) for i in range(count)])


def group_sum(row, width):
    chans = row.shape[-1]
    lane = lax.broadcasted_iota(jnp.int32, row.shape, 1)
    step = 1
    while step < width:
        up = pltpu.roll(row, chans - step, 1)
        down = pltpu.roll(row, step, 1)
        row = row + jnp.where((lane & step) == 0, up, down)
        step *= 2
    return row


def total_rows(values):
    part = jnp.sum(values.reshape(-1, 8, values.shape[-1]), axis=0)
    return jnp.broadcast_to(jnp.sum(part, axis=0, keepdims=True), part.shape)


def side(frame, cols, step):
    count = frame.shape[0]
    moved = pltpu.roll(frame, (-step) % count, 0)
    col = lax.broadcasted_iota(jnp.int32, frame.shape, 0) & (cols - 1)
    keep = col < cols - 1 if step > 0 else col > 0
    return jnp.where(keep, moved, 0.0)


def row_shift(frame, cols, step):
    gap = jnp.zeros((cols, frame.shape[1]), frame.dtype)
    if step > 0:
        return jnp.concatenate([frame[cols:], gap], axis=0)
    return jnp.concatenate([gap, frame[:-cols]], axis=0)


def three_rows(ref, index, frame, cols, steps):
    chans = frame.shape[1]
    for at, step in enumerate(steps):
        piece = frame if step == 0 else row_shift(frame, cols, step)
        ref[index, :, at * chans : (at + 1) * chans] = piece.astype(BF)


def join_cols(parts, cols, chans, steps):
    total = None
    for at, step in enumerate(steps):
        piece = parts[:, at * chans : (at + 1) * chans]
        piece = piece if step == 0 else side(piece, cols, step)
        total = piece if total is None else total + piece
    return total


def load_weights(sections, place, own, chunks, halves, quarter, buffer, sems, split, only=None):
    chans = own.shape[-1]

    def put(source, rows, slot, index):
        for tap in range(3):
            lanes = pl.ds(tap * chans, chans)
            if split == "c":
                src = source.at[:, tap]
                dst = buffer.at[slot, :, rows, lanes]
            else:
                src = source.at[:, tap]
                dst = buffer.at[slot, :, :, rows, lanes]
            pltpu.make_async_copy(src, dst, sems.at[index]).start()

    def view(ref):
        rows = ref.shape[-2]
        if split == "c":
            return ref.reshape(9, 3, rows, chans)
        return ref.reshape(3, 3, 3, rows, chans)

    def section(k):
        slot = 0 if only is not None else place ^ k
        index = 0 if only is not None else place ^ k
        if k == 0:
            put(view(own), pl.ds(0, chans), slot, index)
            return
        for ref, at in zip(chunks[k - 1], halves):
            rows = pl.multiple_of(at * quarter, quarter)
            put(view(ref), pl.ds(rows, quarter), slot, index)

    for k in range(sections):
        if only is None:
            section(k)
        else:
            pl.when((place ^ k) == only)(functools.partial(section, k))


def wait_weights(buffer, sems, slot):
    pltpu.make_async_copy(buffer.at[slot], buffer.at[slot], sems.at[slot]).wait()


def norm_parts(x32, mean, rstd, gain):
    normed = (x32 - mean) * rstd
    scaled = normed * gain
    return normed, scaled, 1.0 / (1.0 + jnp.exp(-scaled))


def full(row, count):
    return jnp.broadcast_to(row[:1], (count, row.shape[1]))


def forward_kernel(sections, dims, quarter, n_chunk, ids, x_ref, gains, own, *refs):
    frames, rows, cols, chans = dims
    plane, points = rows * cols, frames * rows * cols
    n_in = (sections - 1) * n_chunk
    chunks = [refs[i * n_chunk : (i + 1) * n_chunk] for i in range(sections - 1)]
    outs, stats = refs[n_in : n_in + 2]
    sends = refs[n_in + 2 : n_in + 2 + sections]
    weights, spread, taps, sems = refs[n_in + 2 + sections :]
    place = ids[0]
    load_weights(sections, place, own, chunks, piece_ids(ids, n_chunk), quarter, weights, sems, "c")
    width = chans // GROUPS
    count = float(points * width)
    x32 = x_ref[...].astype(F32)
    for unit in range(sections):
        mean = group_sum(total_rows(x32), width) / count
        cent = x32 - full(mean, points)
        var = group_sum(total_rows(cent * cent), width) / count
        rstd = lax.rsqrt(var + EPS)
        stats[unit, 0:8] = mean
        stats[unit, 8:16] = rstd
        _, scaled, gate = norm_parts(x32, full(mean, points), full(rstd, points), full(gains[unit : unit + 1], points))
        act = scaled * gate
        for k in range(sections):
            @pl.when((place ^ k) == unit)
            def _(k=k):
                sends[k][...] = act.astype(BF)
        for f in range(frames):
            three_rows(spread, f, act[f * plane : (f + 1) * plane], cols, (-1, 0, 1))
        wait_weights(weights, sems, unit)
        spots = [0]
        for a in range(3):
            used = max(1, frames - 2 + a)
            lhs = spread[0:used].reshape(used * plane, 3 * chans)
            rhs = weights[unit, 3 * a : 3 * a + 3].reshape(3 * chans, 3 * chans)
            product = jnp.dot(lhs, rhs, preferred_element_type=F32)
            taps[spots[a] : spots[a] + used] = product.reshape(used, plane, 3 * chans)
            spots.append(spots[a] + used)
        fresh = []
        for f in range(frames):
            total = functools.reduce(lambda u, v: u + v, [taps[spots[a] + max(f - 2 + a, 0)] for a in range(3)])
            fresh.append(x32[f * plane : (f + 1) * plane] + join_cols(total, cols, chans, (-1, 0, 1)))
        for f in range(frames):
            outs[unit, f * plane : (f + 1) * plane] = fresh[f].astype(BF)
        x32 = outs[unit].astype(F32)


def piece_ids(ids, n_chunk):
    per = n_chunk // 2
    return [ids[1] * per + j for j in range(per)] + [(1 - ids[1]) * per + j for j in range(per)]


def unit_backward(dims, x32, grad, stat, gain, weights, slot, spread, taps):
    frames, rows, cols, chans = dims
    plane, points = rows * cols, frames * rows * cols
    width = chans // GROUPS
    count = float(points * width)
    g32 = grad.astype(F32)
    per = [g32[f * plane : (f + 1) * plane] for f in range(frames)]
    contribs = []
    at = 0
    for a in range(3):
        folded = [f for f in range(frames) if f - 2 + a <= 0]
        rest = [f for f in range(frames) if f - 2 + a > 0]
        first = functools.reduce(lambda u, v: u + v, [per[f] for f in folded])
        group = [first] + [per[f] for f in rest]
        for i, piece in enumerate(group):
            three_rows(spread, at + i, piece, cols, (1, 0, -1))
        contribs.append((at, len(group)))
        at += len(group)
    for a in range(3):
        start, used = contribs[a]
        lhs = spread[start : start + used].reshape(used * plane, 3 * chans)
        rhs = weights[slot, a].reshape(3 * chans, 3 * chans)
        product = lax.dot_general(lhs, rhs, (((1,), (1,)), ((), ())), preferred_element_type=F32)
        taps[start : start + used] = product.reshape(used, plane, 3 * chans)
    gact = []
    for f in range(frames):
        total = functools.reduce(lambda u, v: u + v, [taps[start + f] for start, used in contribs if f < used])
        gact.append(join_cols(total, cols, chans, (1, 0, -1)))
    gact = jnp.concatenate(gact, axis=0)
    rstd = full(stat[8:16], points)
    wide_gain = full(gain, points)
    normed, scaled, gate = norm_parts(x32, full(stat[0:8], points), rstd, wide_gain)
    d_normed = gact * (gate * (1.0 + scaled * (1.0 - gate))) * wide_gain
    m1 = group_sum(total_rows(d_normed), width) / count
    m2 = group_sum(total_rows(d_normed * normed), width) / count
    dx = rstd * (d_normed - full(m1, points) - normed * full(m2, points))
    return (g32 + dx).astype(BF)


def backward_kernel(sections, dims, quarter, n_chunk, ids, outs, grad_ref, stats, gains, own, *refs):
    n_in = (sections - 1) * n_chunk
    chunks = [refs[i * n_chunk : (i + 1) * n_chunk] for i in range(sections - 1)]
    grads = refs[n_in]
    sends = refs[n_in + 1 : n_in + 1 + sections]
    weights, spread, taps, sems = refs[n_in + 1 + sections :]
    place = ids[0]
    load_weights(sections, place, own, chunks, piece_ids(ids, n_chunk), quarter, weights, sems, "b")
    grad = grad_ref[...]
    for unit in range(sections - 1, 0, -1):
        wait_weights(weights, sems, unit)
        grad = unit_backward(
            dims, outs[unit - 1].astype(F32), grad, stats[unit], gains[unit : unit + 1], weights, unit, spread, taps
        )
        grads[unit - 1] = grad
        for k in range(sections):
            home = place ^ k
            hit = (home == unit - 1) | (home == unit) if unit == sections - 1 else home == unit - 1
            @pl.when(hit)
            def _(k=k, grad=grad):
                sends[k][...] = grad
    wait_weights(weights, sems, 0)


def first_unit_kernel(sections, dims, quarter, n_chunk, ids, x_ref, outs, grads, stats, gains, own, *refs):
    n_in = (sections - 1) * n_chunk
    chunks = [refs[i * n_chunk : (i + 1) * n_chunk] for i in range(sections - 1)]
    sends = refs[n_in : n_in + sections]
    weights, spread, taps, sems = refs[n_in + sections :]
    place = ids[0]
    load_weights(sections, place, own, chunks, piece_ids(ids, n_chunk), quarter, weights, sems, "b", only=0)
    for k in range(sections):
        home = place ^ k
        sends[k][0] = outs[home]
        sends[k][1] = grads[jnp.maximum(home - 1, 0)]
    wait_weights(weights, sems, 0)
    grad = unit_backward(dims, x_ref[...].astype(F32), grads[0], stats[0], gains[0:1], weights, 0, spread, taps)
    for k in range(sections):
        @pl.when((place ^ k) == 0)
        def _(k=k):
            sends[k][1] = grad


def turn_kernel(dims, n, *refs):
    frames, rows, cols, chans = dims
    plane = rows * cols
    acts, turned = refs[:n], refs[n]
    for k in range(n):
        for f in range(frames):
            frame = acts[k][f * plane : (f + 1) * plane].astype(F32)
            for at, step in enumerate((-1, 0, 1)):
                piece = frame if step == 0 else row_shift(frame, cols, step)
                turned[at * chans : (at + 1) * chans, pl.ds((f * n + k) * plane, plane)] = piece.T.astype(BF)


def term_kernel(sections, dims, n, shares, ids, turned, cot, *refs):
    frames, rows, cols, chans = dims
    plane = rows * cols
    grads = refs[:n]
    rest = refs[n:]
    term = rest[-1] if shares else rest[0]
    right = rest[-2] if shares else rest[1]
    place = ids[0]
    is_last = place == sections - 1
    spots = [0]
    for a in range(3):
        spots.append(spots[-1] + max(1, min(frames, frames - 2 + a)))
    for k in range(n):
        mine = jnp.where(is_last, cot[(place ^ k) % n].astype(F32), grads[k][...].astype(F32))
        per = [mine[f * plane : (f + 1) * plane] for f in range(frames)]
        sides = [[side(p, cols, 1), p, side(p, cols, -1)] for p in per]
        for a in range(3):
            folded = [f for f in range(frames) if f - 2 + a <= 0]
            groups = [folded] + [[f] for f in range(frames) if f - 2 + a > 0]
            for i, group in enumerate(groups):
                for c in range(3):
                    piece = functools.reduce(lambda u, v: u + v, [sides[f][c] for f in group])
                    right[pl.ds(((spots[a] + i) * n + k) * plane, plane), c * chans : (c + 1) * chans] = piece.astype(BF)
    for a in range(3):
        used = (spots[a + 1] - spots[a]) * n * plane
        lhs = turned[:, 0:used]
        rhs = right[pl.ds(spots[a] * n * plane, used), :]
        out = jnp.dot(lhs, rhs, preferred_element_type=F32)
        for b in range(3):
            for c in range(3):
                block = out[b * chans : (b + 1) * chans, c * chans : (c + 1) * chans]
                term[pl.ds(((a * 3 + b) * 3 + c) * chans, chans), :] = block.astype(BF)
    if shares:
        keep, send = rest[0], rest[1]
        core = ids[1]
        size = keep.shape[1]
        for j in range(shares // 2):
            here = pl.multiple_of((2 * j + core) * size, size)
            there = pl.multiple_of((2 * j + 1 - core) * size, size)
            keep[j] = term[pl.ds(here, size), :]
            send[j] = term[pl.ds(there, size), :]


def pair_kernel(count, ids, keep, got, own, *sends):
    level = ids[2]
    for k in range(count):
        at = level ^ k
        total = keep[at].astype(F32) + got[at].astype(F32)
        if k == 0:
            own[...] = total
        else:
            sends[k - 1][...] = total.astype(BF)


def sum_kernel(scale, own, *refs):
    total = own[...]
    for ref in refs[:-1]:
        total = total + ref[...].astype(F32)
    refs[-1][...] = total * scale


def home_kernel(n, ids, *refs):
    pieces, seg, ing = refs[:n], refs[n], refs[n + 1]
    for k in range(n):
        at = (ids[0] ^ k) % n
        seg[at] = pieces[k][0]
        ing[at] = pieces[k][1]


def gather_chunks(weights, core, sections, parts):
    taps, chans = weights.shape[0], weights.shape[-1]
    quarter = weights.shape[1] // (2 * parts)
    cut = weights.reshape(taps, 2 * parts, quarter, chans)
    mine = [lax.dynamic_index_in_dim(cut, core * parts + j, 1, False) for j in range(parts)]
    got = {}
    if sections == 4 and parts == 2:
        first = swap(mine[0], "pipe", 1)
        second = swap(mine[1], "pipe", 2)
        got[1] = [first, swap(mine[1], "pipe", 1)]
        got[2] = [swap(mine[0], "pipe", 2), second]
        got[3] = [swap(first, "pipe", 2), swap(second, "pipe", 1)]
    else:
        for k in range(1, sections):
            got[k] = [swap(piece, "pipe", k) for piece in mine]
    return [got[k] + [swap(piece, "dp", 1) for piece in got[k]] for k in range(1, sections)]


def body(video, cotangent, weights, gains):
    sections = lax.axis_size("pipe")
    ranks = lax.axis_size("dp")
    place = lax.axis_index("pipe")
    rank = lax.axis_index("dp")
    core = rank % 2
    ids = jnp.stack([place, core, rank // 2]).astype(jnp.int32)
    micro, clips, frames, rows, cols, chans = video.shape
    points = frames * rows * cols
    dims = (frames, rows, cols, chans)
    parts = 2
    n_chunk = 2 * parts
    quarter = chans // n_chunk

    video = video.reshape(micro, points, chans)
    cot = cotangent.reshape(micro, points, chans)
    kernel_rows = weights.reshape(27, chans, chans)
    chunks = gather_chunks(kernel_rows, core, sections, parts)
    flat = [piece for group in chunks for piece in group]
    all_gains = lax.all_gather(gains[0], "pipe")
    mb = place % micro
    x = lax.dynamic_index_in_dim(video, mb, 0, False)
    grad = lax.dynamic_index_in_dim(cot, mb, 0, False)

    act_shape = jax.ShapeDtypeStruct((points, chans), BF)
    two = jax.ShapeDtypeStruct((2, points, chans), BF)
    unit_flops = 2 * points * 27 * chans * chans
    spread = pltpu.VMEM((2 * frames, rows * cols, 3 * chans), BF)
    taps = pltpu.VMEM((2 * frames, rows * cols, 3 * chans), F32)
    sems = pltpu.SemaphoreType.DMA((sections,))

    outs, stats, *acts = call(
        functools.partial(forward_kernel, sections, dims, quarter, n_chunk),
        [jax.ShapeDtypeStruct((sections, points, chans), BF), jax.ShapeDtypeStruct((sections, 16, chans), F32)]
        + [act_shape] * sections,
        [SM, VM, VM, ANY] + [ANY] * len(flat),
        [VM] * (2 + sections),
        [pltpu.VMEM((sections, 9, chans, 3 * chans), BF), spread, taps, sems],
        flops=4 * sections * unit_flops,
    )(ids, x, all_gains, kernel_rows, *flat)

    n = min(sections, micro)
    acts_home = [acts[0]] + [swap(acts[k], "pipe", k) for k in range(1, n)]

    grads, *gsends = call(
        functools.partial(backward_kernel, sections, dims, quarter, n_chunk),
        [jax.ShapeDtypeStruct((sections - 1, points, chans), BF)] + [act_shape] * sections,
        [SM, VM, VM, VM, VM, ANY] + [ANY] * len(flat),
        [VM] * (1 + sections),
        [pltpu.VMEM((sections, 3, 3, chans, 3 * chans), BF), spread, taps, sems],
        flops=4 * (sections - 1) * unit_flops,
    )(ids, outs, grad, stats, all_gains, kernel_rows, *flat)
    grads_home = [gsends[0]] + [swap(gsends[k], "pipe", k) for k in range(1, n)]

    osends = call(
        functools.partial(first_unit_kernel, sections, dims, quarter, n_chunk),
        [two] * sections,
        [SM, VM, VM, VM, VM, VM, ANY] + [ANY] * len(flat),
        [VM] * sections,
        [pltpu.VMEM((1, 3, 3, chans, 3 * chans), BF), spread, taps, pltpu.SemaphoreType.DMA((1,))],
        flops=4 * unit_flops,
    )(ids, x, outs, grads, stats, all_gains, kernel_rows, *flat)

    turned = call(
        functools.partial(turn_kernel, dims, n),
        jax.ShapeDtypeStruct((3 * chans, n * points), BF),
        [VM] * n,
        VM,
        flops=unit_flops,
    )(*acts_home)

    size = 27 * chans // ranks
    spots = sum(max(1, min(frames, frames - 2 + a)) for a in range(3))
    right = pltpu.VMEM((spots * n * rows * cols, 3 * chans), BF)
    half = jax.ShapeDtypeStruct((ranks // 2, size, chans), BF)
    levels = ranks // 2
    if size % 16 == 0:
        keep, send = call(
            functools.partial(term_kernel, sections, dims, n, ranks),
            [half, half],
            [SM, VM, VM] + [VM] * n,
            [VM, VM],
            [right, pltpu.VMEM((27 * chans, chans), BF)],
            flops=n * unit_flops,
        )(ids, turned, cot, *grads_home)
    else:
        term = call(
            functools.partial(term_kernel, sections, dims, n, 0),
            jax.ShapeDtypeStruct((27 * chans, chans), BF),
            [SM, VM, VM] + [VM] * n,
            VM,
            [right],
            flops=n * unit_flops,
        )(ids, turned, cot, *grads_home)
        shares = term.reshape(levels, 2, size, chans)
        keep = lax.dynamic_index_in_dim(shares, core, 1, False)
        send = lax.dynamic_index_in_dim(shares, 1 - core, 1, False)
    got = swap(send, "dp", 1)
    piece = jax.ShapeDtypeStruct((size, chans), BF)
    own, *zsends = call(
        functools.partial(pair_kernel, levels),
        [jax.ShapeDtypeStruct((size, chans), F32)] + [piece] * (levels - 1),
        [SM, VM, VM],
        [VM] * levels,
    )(ids, keep, got)
    arrived = [swap(zsends[k - 1], "dp", 2 * k) for k in range(1, levels)]

    scale = 1.0 / math.sqrt(micro * clips * ranks * points)
    share = call(
        functools.partial(sum_kernel, scale),
        jax.ShapeDtypeStruct((size, chans), F32),
        [VM] * levels,
        VM,
    )(own, *arrived)

    homes = [osends[0]] + [swap(osends[k], "pipe", k) for k in range(1, n)]
    seg, ing = call(
        functools.partial(home_kernel, n),
        [jax.ShapeDtypeStruct((micro, points, chans), BF)] * 2,
        [SM] + [VM] * n,
        [VM, VM],
    )(ids, *homes)
    shape = (1, micro, clips, frames, rows, cols, chans)
    return (seg.reshape(shape), ing.reshape(shape), share.reshape(1, size * chans))


def solution(mesh):
    in_specs = (
        P(None, "dp", None, None, None, None),
        P(None, "dp", None, None, None, None),
        P("pipe", None, None),
        P("pipe", None),
    )
    out_specs = (
        P("pipe", None, "dp", None, None, None, None),
        P("pipe", None, "dp", None, None, None, None),
        P("pipe", "dp"),
    )
    return jax.shard_map(body, mesh=mesh, in_specs=in_specs, out_specs=out_specs, check_vma=False)
```

time: 316 us -> 69.8 us (0.22)
  waiting for transfers between devices: 93.1 us -> 12.4 us
  local copies, waits for them, and re-layouts: 60.9 us -> 2.12 us
  other arithmetic: 56.5 us -> 0.08 us
  matrix products: 33.1 us -> 0 us
  Pallas kernels: 0 us -> 17.1 us
  starting transfers between devices: 43.3 us -> 27.6 us
  between operations: 14.8 us -> 0.79 us
  loops' own time: 12.6 us -> 0 us
  blocking collectives: 0 us -> 9.59 us
    unnamed x2 -> x0, waiting for transfers between devices: 59.3 us -> none
    dot_general x21 -> x0, matrix products: 33.1 us -> none  [the longest x7 14.3 us: backward(): lax.dot_general(flat_grad, weight, (((1,), (1,)), ((), ())), preferred_el...]
    ppermute x14 -> x25, waiting for transfers between devices: 33.7 us -> 12.4 us  [swap(): return lax.ppermute(value, axis, [(i, i ^ bits) for i in range(count)])]
    while x413 -> x0, local copies, waits for them, and re-layouts: 19 us -> none
    add_any x14 -> x0, other arithmetic: 18.9 us -> none  [the longest x7 18.8 us: patches(): padded[:, frame_off:frame_off + frames, row_off:row_off + rows, col_off:c...]
    pallas_call x0 -> x8, Pallas kernels: none -> 17.1 us  [the longest x1 5.67 us: body(): call(functools.partial(forward_kernel, sections, dims, quarter, n_chunk),...]
    ppermute x14 -> x25, starting transfers between devices: 43.3 us -> 27.6 us  [swap(): return lax.ppermute(value, axis, [(i, i ^ bits) for i in range(count)])]
    dynamic_slice x28 -> x0, local copies, waits for them, and re-layouts: 14.8 us -> none  [the longest x14 8.35 us: body(): lax.scan(forward_tick, start, jnp.arange(ticks, dtype=jnp.int32))]
  transfers between devices with their start and end apart: 15 -> 25, of which waited for: 15 -> 9; matrix products, arithmetic and copies ran while one was open for 7% -> 1% of each run, Pallas kernels for 0% -> 12%
where the time goes in v1:
time: 69.8 us; the launch traced here: 69.6 us
  starting transfers between devices  27.6 us (40%)
  Pallas kernels  17.1 us (24%)
  waiting for transfers between devices  12.4 us (18%)
  blocking collectives  9.59 us (14%)
  local copies, waits for them, and re-layouts  2.12 us (3%)
  between operations  0.79 us (1%)
    ppermute x25, starting transfers between devices, swap(): return lax.ppermute(value, axis, [(i, i ^ bits) for i in range(count)])  27.6 us
    ppermute x25, waiting for transfers between devices, swap(): return lax.ppermute(value, axis, [(i, i ^ bits) for i in range(count)])  12.4 us
    all_gather x1, blocking collectives, body(): all_gains = lax.all_gather(gains[0], 'pipe')  9.59 us
    pallas_call x1, Pallas kernels, body(): call(functools.partial(forward_kernel, sections, dims, quarter, n_chunk),...  5.67 us
    pallas_call x1, Pallas kernels, body(): call(functools.partial(backward_kernel, sections, dims, quarter, n_chunk)...  4 us
    pallas_call x1, Pallas kernels, body(): call(functools.partial(term_kernel, sections, dims, n, ranks), [half, hal...  2.45 us
    pallas_call x1, Pallas kernels, body(): call(functools.partial(first_unit_kernel, sections, dims, quarter, n_chun...  1.7 us
    pallas_call x1, Pallas kernels, body(): call(functools.partial(home_kernel, n), [jax.ShapeDtypeStruct((micro, poi...  1.48 us
  transfers between devices with their start and end apart: 25, of which 9 were waited for; matrix products, arithmetic and copies ran while one was open for 1% of the time, Pallas kernels for 12%

profile of v1, /device:TPU:0, one launch (start us, length us, event | category | flops | bytes accessed | tf_op | source)
XLA Modules:
  0.0 69.6 jit_solution(4236253599831528987)
XLA Ops:
  0.6 0.0 copy-start
  0.7 1.2 %dynamic-slice_bitcast_fusion = (bf16[27,32,128]{2,1,0:T(8,128)(2,1)S(1)}, bf16[27,32,128]{2,1,0:T(8,128)(2,1)S(1)}) fusion(bf16[27,4,32,128]{3,2,1,0:T(8,128)(2,1)} %bitcast.28, s32[]{:T(128)S(6)} %select_n.32, s32[]{:T(128)S(6)} %select_n.31), kind=kLoop, calls=%fused_computation | loop fusion | bytes 884744 | tf_op jit(solution)/shard_map/jit(dynamic_index_in_dim)/squeeze | solution.py:354
  1.8 3.0 %collective-permute-start.5 = (bf16[27,32,128]{2,1,0:T(8,128)(2,1)S(1)}, bf16[27,32,128]{2,1,0:T(8,128)(2,1)S(1)}, u32[]{:S(2)}, u32[]{:S(2)}) collective-permute-start(bf16[27,32,128]{2,1,0:T(8,128)(2,1)S(1)} %get-tuple-element.55), channel_id=1, source_target_pairs={{0,16},{8,24},{16,0},{24,8},{1,17},{9,25},{17,1},{25,9},{2,18},{10... | collective-permute-start | bytes 663560 | tf_op jit(solution)/shard_map/ppermute | solution.py:34
  4.9 1.5 %collective-permute-start = (bf16[27,32,128]{2,1,0:T(8,128)(2,1)S(1)}, bf16[27,32,128]{2,1,0:T(8,128)(2,1)S(1)}, u32[]{:S(2)}, u32[]{:S(2)}) collective-permute-start(bf16[27,32,128]{2,1,0:T(8,128)(2,1)S(1)} %get-tuple-element.56), channel_id=1, source_target_pairs={{0,8},{8,0},{16,24},{24,16},{1,9},{9,1},{17,25},{25,17},{2,10},{10... | collective-permute-start | bytes 663560 | tf_op jit(solution)/shard_map/ppermute | solution.py:34
  6.3 0.5 collective-permute-start.1
  6.9 0.1 collective-permute-start.4
  7.0 4.2 %collective-permute-done.5.refs_5_ = bf16[27,32,128]{2,1,0:T(8,128)(2,1)S(1)} collective-permute-done((bf16[27,32,128]{2,1,0:T(8,128)(2,1)S(1)}, bf16[27,32,128]{2,1,0:T(8,128)(2,1)S(1)}, u32[]{:S(2)}, u32[]{:S(2)}) %collective-permute-start.5) | collective-permute-done | bytes 221216 | tf_op jit(solution)/shard_map/ppermute | solution.py:34
  11.1 2.0 %collective-permute-start.9 = (bf16[27,32,128]{2,1,0:T(8,128)(2,1)S(1)}, bf16[27,32,128]{2,1,0:T(8,128)(2,1)S(1)}, u32[]{:S(2)}, u32[]{:S(2)}) collective-permute-start(bf16[27,32,128]{2,1,0:T(8,128)(2,1)S(1)} %collective-permute-done.5.refs_5_), channel_id=1, source_target_pairs={{0,8},{8,0},{16,24},{24,16},{1,9},{9,1},{17,25},{25,17},{2,10},{10... | collective-permute-start | bytes 663560 | tf_op jit(solution)/shard_map/ppermute | solution.py:34
  13.1 0.0 collective-permute-start.7
  13.1 0.1 collective-permute-done.refs_0_
  13.2 1.5 %collective-permute-start.8 = (bf16[27,32,128]{2,1,0:T(8,128)(2,1)S(1)}, bf16[27,32,128]{2,1,0:T(8,128)(2,1)S(1)}, u32[]{:S(2)}, u32[]{:S(2)}) collective-permute-start(bf16[27,32,128]{2,1,0:T(8,128)(2,1)S(1)} %collective-permute-done.refs_0_), channel_id=1, source_target_pairs={{0,16},{8,24},{16,0},{24,8},{1,17},{9,25},{17,1},{25,9},{2,18},{10... | collective-permute-start | bytes 663560 | tf_op jit(solution)/shard_map/ppermute | solution.py:34
  14.7 9.6 %all-gather = f32[4,1,128]{2,1,0:T(1,128)S(1)} all-gather(f32[1,1,128]{2,1,0:T(1,128)} %bitcast.39), channel_id=1, replica_groups=mesh['pipe'=4,'dp'=8] {'pipe'}, dimensions={0}, use_global_device_ids=true | all-gather | bytes 2560 | tf_op jit(solution)/shard_map/all_gather | solution.py:387
  24.3 0.0 collective-permute-done.1.refs_1_
  24.3 0.0 collective-permute-start.2
  24.3 0.0 collective-permute-done.4.refs_4_
  24.3 0.5 collective-permute-start.3
  24.8 0.0 collective-permute-done.9.refs_9_
  24.8 0.1 collective-permute-start.6
  24.9 0.0 collective-permute-done.7.refs_7_
  24.9 0.4 collective-permute-start.11
  25.3 0.0 collective-permute-done.8.refs_8_
  25.3 0.1 collective-permute-start.10
  25.4 0.1 pad_add_fusion.ids
  25.5 1.0 %dynamic-slice_bitcast_fusion.2 = (bf16[384,128]{1,0:T(8,128)(2,1)S(1)}, bf16[384,128]{1,0:T(8,128)(2,1)S(1)}) fusion(bf16[4,384,128]{2,1,0:T(8,128)(2,1)} %bitcast.32, s32[]{:T(128)S(6)} %select_n.30, bf16[4,384,128]{2,1,0:T(8,128)(2,1)} %bitcast.38), kind=kLoop, calls=%fused_computation.2 | loop fusion | bytes 393220 | tf_op jit(solution)/shard_map/jit(dynamic_index_in_dim)/squeeze | solution.py:390
  26.4 0.0 collective-permute-done.3.refs_3_
  26.4 0.0 collective-permute-done.6.refs_6_
  26.4 0.0 collective-permute-done.2.refs_2_
  26.4 0.2 collective-permute-done.11.refs_11_
  26.7 0.3 collective-permute-done.10.refs_10_
  27.0 5.7 %shard_map.67 = (bf16[4,384,128]{2,1,0:T(8,128)(2,1)S(1)}, f32[4,16,128]{2,1,0:T(8,128)S(1)}, bf16[384,128]{1,0:T(8,128)(2,1)S(1)}, bf16[384,128]{1,0:T(8,128)(2...) custom-call(s32[3]{0:T(128)S(1)} %pad_add_fusion.ids, bf16[384,128]{1,0:T(8,128)(2,1)S(1)} %get-tuple-element.58.x_ref, ...), custom_call_target="tpu_custom_call" | custom-call | flops 5435817984 | tf_op jit(solution)/shard_map/pallas_call | solution.py:399
  32.7 0.6 collective-permute-start.15
  33.3 1.4 %collective-permute-start.16 = (bf16[384,128]{1,0:T(8,128)(2,1)S(1)}, bf16[384,128]{1,0:T(8,128)(2,1)S(1)}, u32[]{:S(2)}, u32[]{:S(2)}) collective-permute-start(bf16[384,128]{1,0:T(8,128)(2,1)S(1)} %get-tuple-element.37), channel_id=1, source_target_pairs={{0,16},{8,24},{16,0},{24,8},{1,17},{9,25},{17,1},{25,9},{2,18},{10... | collective-permute-start | bytes 294920 | tf_op jit(solution)/shard_map/ppermute | solution.py:34
  34.6 1.6 %collective-permute-start.17 = (bf16[384,128]{1,0:T(8,128)(2,1)S(1)}, bf16[384,128]{1,0:T(8,128)(2,1)S(1)}, u32[]{:S(2)}, u32[]{:S(2)}) collective-permute-start(bf16[384,128]{1,0:T(8,128)(2,1)S(1)} %get-tuple-element.38), channel_id=1, source_target_pairs={{0,24},{8,16},{16,8},{24,0},{1,25},{9,17},{17,9},{25,1},{2,26},{10... | collective-permute-start | bytes 294920 | tf_op jit(solution)/shard_map/ppermute | solution.py:34
  36.2 4.0 %shard_map.68 = (bf16[3,384,128]{2,1,0:T(8,128)(2,1)S(1)}, bf16[384,128]{1,0:T(8,128)(2,1)S(1)}, bf16[384,128]{1,0:T(8,128)(2,1)S(1)}, bf16[384,128]{1,0:T(8,128)(2,1)S(1)}, bf16[384,128]{1,0:T(8,128)(2,1)S(1)}) custom-call(s32[3]{0:T(128)S(1)} %pad_add_fusion.ids, bf16[4,384,128]{2,1,0:T(8,128)(2,1)S(1)} %get-tuple-element.26.outs, ...), custom_call_target="tpu_custom_call" | custom-call | flops 4076863488 | tf_op jit(solution)/shard_map/pallas_call | solution.py:412
  40.3 0.0 copy-start.1
  40.3 0.6 collective-permute-start.18
  40.9 1.4 %collective-permute-start.19 = (bf16[384,128]{1,0:T(8,128)(2,1)S(1)}, bf16[384,128]{1,0:T(8,128)(2,1)S(1)}, u32[]{:S(2)}, u32[]{:S(2)}) collective-permute-start(bf16[384,128]{1,0:T(8,128)(2,1)S(1)} %get-tuple-element.41), channel_id=1, source_target_pairs={{0,16},{8,24},{16,0},{24,8},{1,17},{9,25},{17,1},{25,9},{2,18},{10... | collective-permute-start | bytes 294920 | tf_op jit(solution)/shard_map/ppermute | solution.py:34
  42.2 0.0 collective-permute-done.15.refs_1_
  42.2 1.6 %collective-permute-start.20 = (bf16[384,128]{1,0:T(8,128)(2,1)S(1)}, bf16[384,128]{1,0:T(8,128)(2,1)S(1)}, u32[]{:S(2)}, u32[]{:S(2)}) collective-permute-start(bf16[384,128]{1,0:T(8,128)(2,1)S(1)} %get-tuple-element.42), channel_id=1, source_target_pairs={{0,24},{8,16},{16,8},{24,0},{1,25},{9,17},{17,9},{25,1},{2,26},{10... | collective-permute-start | bytes 294920 | tf_op jit(solution)/shard_map/ppermute | solution.py:34
  43.8 0.0 collective-permute-done.16.refs_2_
  43.8 0.0 collective-permute-done.17.refs_3_
  43.8 0.4 shard_map.71.turned
  44.2 1.6 %collective-permute-done.18.refs_1_ = bf16[384,128]{1,0:T(8,128)(2,1)S(1)} collective-permute-done((bf16[384,128]{1,0:T(8,128)(2,1)S(1)}, bf16[384,128]{1,0:T(8,128)(2,1)S(1)}, u32[]{:S(2)}, u32[]{:S(2)}) %collective-permute-start.18) | collective-permute-done | bytes 98336 | tf_op jit(solution)/shard_map/ppermute | solution.py:34
  45.8 0.7 %collective-permute-done.19.refs_2_ = bf16[384,128]{1,0:T(8,128)(2,1)S(1)} collective-permute-done((bf16[384,128]{1,0:T(8,128)(2,1)S(1)}, bf16[384,128]{1,0:T(8,128)(2,1)S(1)}, u32[]{:S(2)}, u32[]{:S(2)}) %collective-permute-start.19) | collective-permute-done | bytes 98336 | tf_op jit(solution)/shard_map/ppermute | solution.py:34
  46.5 1.2 %collective-permute-done.20.refs_3_ = bf16[384,128]{1,0:T(8,128)(2,1)S(1)} collective-permute-done((bf16[384,128]{1,0:T(8,128)(2,1)S(1)}, bf16[384,128]{1,0:T(8,128)(2,1)S(1)}, u32[]{:S(2)}, u32[]{:S(2)}) %collective-permute-start.20) | collective-permute-done | bytes 98336 | tf_op jit(solution)/shard_map/ppermute | solution.py:34
  47.7 2.4 %shard_map.72 = (bf16[4,432,128]{2,1,0:T(8,128)(2,1)S(1)}, bf16[4,432,128]{2,1,0:T(8,128)(2,1)S(1)}) custom-call(s32[3]{0:T(128)S(1)} %pad_add_fusion.ids, bf16[384,1536]{1,0:T(8,128)(2,1)S(1)} %shard_map.71.turned, bf16[4,384,128]{2,1,0:T(8,128)(2,1)S(1)} %bitcast.33, bf16[384,128]{1,0:T(8,128)(2,1)S(1)} %get-tuple-element.39.refs_0_, ...), custom_call_target="tpu_custom_call" | custom-call | flops 1358954496 | tf_op jit(solution)/shard_map/pallas_call | solution.py:445
  50.2 0.1 collective-permute-start.21
  50.3 1.7 %shard_map.69 = (bf16[2,384,128]{2,1,0:T(8,128)(2,1)S(1)}, bf16[2,384,128]{2,1,0:T(8,128)(2,1)S(1)}, bf16[2,384,128]{2,1,0:T(8,128)(2,1)S(1)}, bf16[2,384,128]{2,1,0:T(8,128)(2,1)S(1)}) custom-call(s32[3]{0:T(128)S(1)} %pad_add_fusion.ids, bf16[384,128]{1,0:T(8,128)(2,1)S(1)} %get-tuple-element.58.x_ref, bf16[4,384,128]{2,1,0:T(8,128)(2,1)S(1)} %get-tuple-element.26.outs, ...), custom_call_target="tpu_custom_call" | custom-call | flops 1358954496 | tf_op jit(solution)/shard_map/pallas_call | solution.py:422
  52.0 1.0 %collective-permute-start.12 = (bf16[2,384,128]{2,1,0:T(8,128)(2,1)S(1)}, bf16[2,384,128]{2,1,0:T(8,128)(2,1)S(1)}, u32[]{:S(2)}, u32[]{:S(2)}) collective-permute-start(bf16[2,384,128]{2,1,0:T(8,128)(2,1)S(1)} %get-tuple-element.30), channel_id=1, source_target_pairs={{0,8},{8,0},{16,24},{24,16},{1,9},{9,1},{17,25},{25,17},{2,10},{10... | collective-permute-start | bytes 589832 | tf_op jit(solution)/shard_map/ppermute | solution.py:34
  53.0 1.2 %collective-permute-start.13 = (bf16[2,384,128]{2,1,0:T(8,128)(2,1)S(1)}, bf16[2,384,128]{2,1,0:T(8,128)(2,1)S(1)}, u32[]{:S(2)}, u32[]{:S(2)}) collective-permute-start(bf16[2,384,128]{2,1,0:T(8,128)(2,1)S(1)} %get-tuple-element.31), channel_id=1, source_target_pairs={{0,16},{8,24},{16,0},{24,8},{1,17},{9,25},{17,1},{25,9},{2,18},{10... | collective-permute-start | bytes 589832 | tf_op jit(solution)/shard_map/ppermute | solution.py:34
  54.2 1.3 %collective-permute-start.14 = (bf16[2,384,128]{2,1,0:T(8,128)(2,1)S(1)}, bf16[2,384,128]{2,1,0:T(8,128)(2,1)S(1)}, u32[]{:S(2)}, u32[]{:S(2)}) collective-permute-start(bf16[2,384,128]{2,1,0:T(8,128)(2,1)S(1)} %get-tuple-element.32), channel_id=1, source_target_pairs={{0,24},{8,16},{16,8},{24,0},{1,25},{9,17},{17,9},{25,1},{2,26},{10... | collective-permute-start | bytes 589832 | tf_op jit(solution)/shard_map/ppermute | solution.py:34
  55.5 0.0 collective-permute-done.21.got
  55.5 0.6 shard_map.73
  56.2 1.6 %collective-permute-start.22 = (bf16[432,128]{1,0:T(8,128)(2,1)S(1)}, bf16[432,128]{1,0:T(8,128)(2,1)S(1)}, u32[]{:S(2)}, u32[]{:S(2)}) collective-permute-start(bf16[432,128]{1,0:T(8,128)(2,1)S(1)} %get-tuple-element.46), channel_id=1, source_target_pairs={{0,2},{1,3},{2,0},{3,1},{4,6},{5,7},{6,4},{7,5},{8,10},{9,11},{10,... | collective-permute-start | bytes 331784 | tf_op jit(solution)/shard_map/ppermute | solution.py:34
  57.8 2.6 %collective-permute-start.23 = (bf16[432,128]{1,0:T(8,128)(2,1)S(1)}, bf16[432,128]{1,0:T(8,128)(2,1)S(1)}, u32[]{:S(2)}, u32[]{:S(2)}) collective-permute-start(bf16[432,128]{1,0:T(8,128)(2,1)S(1)} %get-tuple-element.47), channel_id=1, source_target_pairs={{0,4},{1,5},{2,6},{3,7},{4,0},{5,1},{6,2},{7,3},{8,12},{9,13},{10,... | collective-permute-start | bytes 331784 | tf_op jit(solution)/shard_map/ppermute | solution.py:34
  60.4 0.0 collective-permute-done.12.refs_1_
  60.4 2.9 %collective-permute-start.24 = (bf16[432,128]{1,0:T(8,128)(2,1)S(1)}, bf16[432,128]{1,0:T(8,128)(2,1)S(1)}, u32[]{:S(2)}, u32[]{:S(2)}) collective-permute-start(bf16[432,128]{1,0:T(8,128)(2,1)S(1)} %get-tuple-element.48), channel_id=1, source_target_pairs={{0,6},{1,7},{2,4},{3,5},{4,2},{5,3},{6,0},{7,1},{8,14},{9,15},{10,... | collective-permute-start | bytes 331784 | tf_op jit(solution)/shard_map/ppermute | solution.py:34
  63.4 0.9 %collective-permute-done.13.refs_2_ = bf16[2,384,128]{2,1,0:T(8,128)(2,1)S(1)} collective-permute-done((bf16[2,384,128]{2,1,0:T(8,128)(2,1)S(1)}, bf16[2,384,128]{2,1,0:T(8,128)(2,1)S(1)}, u32[]{:S(2)}, u32[]{:S(2)}) %collective-permute-start.13) | collective-permute-done | bytes 196640 | tf_op jit(solution)/shard_map/ppermute | solution.py:34
  64.2 0.0 collective-permute-done.14.refs_3_
  64.2 1.5 %shard_map.70 = (bf16[4,384,128]{2,1,0:T(8,128)(2,1)}, bf16[4,384,128]{2,1,0:T(8,128)(2,1)}) custom-call(s32[3]{0:T(128)S(1)} %pad_add_fusion.ids, bf16[2,384,128]{2,1,0:T(8,128)(2,1)S(1)} %get-tuple-element.29.refs_0_, bf16[2,384,128]{2,1,0:T(8,128)(2,1)S(1)} %collective-permute-done.12.refs_1_, bf16[2,384,128]{2,1,0:T(8,128)(2,1)S(1)} %collective-permute-done.13.refs_2_, ...), custom_call_target="tpu_custom_call" | custom-call | tf_op jit(solution)/shard_map/pallas_call | solution.py:484
  65.7 0.0 collective-permute-done.22.refs_0_
  65.7 3.2 %collective-permute-done.23.refs_1_ = bf16[432,128]{1,0:T(8,128)(2,1)S(1)} collective-permute-done((bf16[432,128]{1,0:T(8,128)(2,1)S(1)}, bf16[432,128]{1,0:T(8,128)(2,1)S(1)}, u32[]{:S(2)}, u32[]{:S(2)}) %collective-permute-start.23) | collective-permute-done | bytes 110624 | tf_op jit(solution)/shard_map/ppermute | solution.py:34
  68.9 0.0 collective-permute-done.24.refs_2_
  68.9 0.7 %shard_map.74 = f32[432,128]{1,0:T(8,128)} custom-call(f32[432,128]{1,0:T(8,128)S(1)} %get-tuple-element.45.own, bf16[432,128]{1,0:T(8,128)(2,1)S(1)} %collective-permute-done.22.refs_0_, bf16[432,128]{1,0:T(8,128)(2,1)S(1)} %collective-permute-done.23.refs_1_, bf16[432,128]{1,0:T(8,128)(2,1)S(1)} %collective-permute-done.24.refs_2_), custom_call_target="tpu_custom_call" | custom-call | tf_op jit(solution)/shard_map/pallas_call | solution.py:476
  (2 shorter events, 0.0 us)
Async XLA Ops:
  0.6 26.4 %copy-start = (bf16[1,3456,128]{2,1,0:T(8,128)(2,1)S(1)}, bf16[1,3456,128]{2,1,0:T(8,128)(2,1)}, u32[]{:S(2)}) copy-start(bf16[1,3456,128]{2,1,0:T(8,128)(2,1)} %param.6) | copy-start | bytes 2654212
  1.8 9.3 %collective-permute-start.5 = (bf16[27,32,128]{2,1,0:T(8,128)(2,1)S(1)}, bf16[27,32,128]{2,1,0:T(8,128)(2,1)S(1)}, u32[]{:S(2)}, u32[]{:S(2)}) collective-permute-start(bf16[27,32,128]{2,1,0:T(8,128)(2,1)S(1)} %get-tuple-element.55), channel_id=1, source_target_pairs={{0,16},{8,24},{16,0},{24,8},{1,17},{9,25},{17,1},{25,9},{2,18},{10... | collective-permute-start | bytes 663560 | tf_op jit(solution)/shard_map/ppermute | solution.py:34
  4.9 8.4 %collective-permute-start = (bf16[27,32,128]{2,1,0:T(8,128)(2,1)S(1)}, bf16[27,32,128]{2,1,0:T(8,128)(2,1)S(1)}, u32[]{:S(2)}, u32[]{:S(2)}) collective-permute-start(bf16[27,32,128]{2,1,0:T(8,128)(2,1)S(1)} %get-tuple-element.56), channel_id=1, source_target_pairs={{0,8},{8,0},{16,24},{24,16},{1,9},{9,1},{17,25},{25,17},{2,10},{10... | collective-permute-start | bytes 663560 | tf_op jit(solution)/shard_map/ppermute | solution.py:34
  6.3 17.9 %collective-permute-start.1 = (bf16[27,32,128]{2,1,0:T(8,128)(2,1)S(1)}, bf16[27,32,128]{2,1,0:T(8,128)(2,1)S(1)}, u32[]{:S(2)}, u32[]{:S(2)}) collective-permute-start(bf16[27,32,128]{2,1,0:T(8,128)(2,1)S(1)} %get-tuple-element.55), channel_id=1, source_target_pairs={{0,8},{8,0},{16,24},{24,16},{1,9},{9,1},{17,25},{25,17},{2,10},{10... | collective-permute-start | bytes 663560 | tf_op jit(solution)/shard_map/ppermute | solution.py:34
  6.9 17.4 %collective-permute-start.4 = (bf16[27,32,128]{2,1,0:T(8,128)(2,1)S(1)}, bf16[27,32,128]{2,1,0:T(8,128)(2,1)S(1)}, u32[]{:S(2)}, u32[]{:S(2)}) collective-permute-start(bf16[27,32,128]{2,1,0:T(8,128)(2,1)S(1)} %get-tuple-element.56), channel_id=1, source_target_pairs={{0,16},{8,24},{16,0},{24,8},{1,17},{9,25},{17,1},{25,9},{2,18},{10... | collective-permute-start | bytes 663560 | tf_op jit(solution)/shard_map/ppermute | solution.py:34
  11.1 13.7 %collective-permute-start.9 = (bf16[27,32,128]{2,1,0:T(8,128)(2,1)S(1)}, bf16[27,32,128]{2,1,0:T(8,128)(2,1)S(1)}, u32[]{:S(2)}, u32[]{:S(2)}) collective-permute-start(bf16[27,32,128]{2,1,0:T(8,128)(2,1)S(1)} %collective-permute-done.5.refs_5_), channel_id=1, source_target_pairs={{0,8},{8,0},{16,24},{24,16},{1,9},{9,1},{17,25},{25,17},{2,10},{10... | collective-permute-start | bytes 663560 | tf_op jit(solution)/shard_map/ppermute | solution.py:34
  13.1 11.7 %collective-permute-start.7 = (bf16[27,32,128]{2,1,0:T(8,128)(2,1)S(1)}, bf16[27,32,128]{2,1,0:T(8,128)(2,1)S(1)}, u32[]{:S(2)}, u32[]{:S(2)}) collective-permute-start(bf16[27,32,128]{2,1,0:T(8,128)(2,1)S(1)} %collective-permute-done.5.refs_5_), channel_id=1, source_target_pairs={{0,1},{1,0},{2,3},{3,2},{4,5},{5,4},{6,7},{7,6},{8,9},{9,8},{10,11... | collective-permute-start | bytes 663560 | tf_op jit(solution)/shard_map/ppermute | solution.py:34
  13.2 12.1 %collective-permute-start.8 = (bf16[27,32,128]{2,1,0:T(8,128)(2,1)S(1)}, bf16[27,32,128]{2,1,0:T(8,128)(2,1)S(1)}, u32[]{:S(2)}, u32[]{:S(2)}) collective-permute-start(bf16[27,32,128]{2,1,0:T(8,128)(2,1)S(1)} %collective-permute-done.refs_0_), channel_id=1, source_target_pairs={{0,16},{8,24},{16,0},{24,8},{1,17},{9,25},{17,1},{25,9},{2,18},{10... | collective-permute-start | bytes 663560 | tf_op jit(solution)/shard_map/ppermute | solution.py:34
  24.3 2.2 %collective-permute-start.2 = (bf16[27,32,128]{2,1,0:T(8,128)(2,1)S(1)}, bf16[27,32,128]{2,1,0:T(8,128)(2,1)S(1)}, u32[]{:S(2)}, u32[]{:S(2)}) collective-permute-start(bf16[27,32,128]{2,1,0:T(8,128)(2,1)S(1)} %collective-permute-done.refs_0_), channel_id=1, source_target_pairs={{0,1},{1,0},{2,3},{3,2},{4,5},{5,4},{6,7},{7,6},{8,9},{9,8},{10,11... | collective-permute-start | bytes 663560 | tf_op jit(solution)/shard_map/ppermute | solution.py:34
  24.3 2.1 %collective-permute-start.3 = (bf16[27,32,128]{2,1,0:T(8,128)(2,1)S(1)}, bf16[27,32,128]{2,1,0:T(8,128)(2,1)S(1)}, u32[]{:S(2)}, u32[]{:S(2)}) collective-permute-start(bf16[27,32,128]{2,1,0:T(8,128)(2,1)S(1)} %collective-permute-done.1.refs_1_), channel_id=1, source_target_pairs={{0,1},{1,0},{2,3},{3,2},{4,5},{5,4},{6,7},{7,6},{8,9},{9,8},{10,11... | collective-permute-start | bytes 663560 | tf_op jit(solution)/shard_map/ppermute | solution.py:34
  24.8 1.6 %collective-permute-start.6 = (bf16[27,32,128]{2,1,0:T(8,128)(2,1)S(1)}, bf16[27,32,128]{2,1,0:T(8,128)(2,1)S(1)}, u32[]{:S(2)}, u32[]{:S(2)}) collective-permute-start(bf16[27,32,128]{2,1,0:T(8,128)(2,1)S(1)} %collective-permute-done.4.refs_4_), channel_id=1, source_target_pairs={{0,1},{1,0},{2,3},{3,2},{4,5},{5,4},{6,7},{7,6},{8,9},{9,8},{10,11... | collective-permute-start | bytes 663560 | tf_op jit(solution)/shard_map/ppermute | solution.py:34
  24.9 1.8 %collective-permute-start.11 = (bf16[27,32,128]{2,1,0:T(8,128)(2,1)S(1)}, bf16[27,32,128]{2,1,0:T(8,128)(2,1)S(1)}, u32[]{:S(2)}, u32[]{:S(2)}) collective-permute-start(bf16[27,32,128]{2,1,0:T(8,128)(2,1)S(1)} %collective-permute-done.9.refs_9_), channel_id=1, source_target_pairs={{0,1},{1,0},{2,3},{3,2},{4,5},{5,4},{6,7},{7,6},{8,9},{9,8},{10,11... | collective-permute-start | bytes 663560 | tf_op jit(solution)/shard_map/ppermute | solution.py:34
  25.3 1.7 %collective-permute-start.10 = (bf16[27,32,128]{2,1,0:T(8,128)(2,1)S(1)}, bf16[27,32,128]{2,1,0:T(8,128)(2,1)S(1)}, u32[]{:S(2)}, u32[]{:S(2)}) collective-permute-start(bf16[27,32,128]{2,1,0:T(8,128)(2,1)S(1)} %collective-permute-done.8.refs_8_), channel_id=1, source_target_pairs={{0,1},{1,0},{2,3},{3,2},{4,5},{5,4},{6,7},{7,6},{8,9},{9,8},{10,11... | collective-permute-start | bytes 663560 | tf_op jit(solution)/shard_map/ppermute | solution.py:34
  32.7 9.5 %collective-permute-start.15 = (bf16[384,128]{1,0:T(8,128)(2,1)S(1)}, bf16[384,128]{1,0:T(8,128)(2,1)S(1)}, u32[]{:S(2)}, u32[]{:S(2)}) collective-permute-start(bf16[384,128]{1,0:T(8,128)(2,1)S(1)} %get-tuple-element.36), channel_id=1, source_target_pairs={{0,8},{8,0},{16,24},{24,16},{1,9},{9,1},{17,25},{25,17},{2,10},{10... | collective-permute-start | bytes 294920 | tf_op jit(solution)/shard_map/ppermute | solution.py:34
  33.3 10.5 %collective-permute-start.16 = (bf16[384,128]{1,0:T(8,128)(2,1)S(1)}, bf16[384,128]{1,0:T(8,128)(2,1)S(1)}, u32[]{:S(2)}, u32[]{:S(2)}) collective-permute-start(bf16[384,128]{1,0:T(8,128)(2,1)S(1)} %get-tuple-element.37), channel_id=1, source_target_pairs={{0,16},{8,24},{16,0},{24,8},{1,17},{9,25},{17,1},{25,9},{2,18},{10... | collective-permute-start | bytes 294920 | tf_op jit(solution)/shard_map/ppermute | solution.py:34
  34.6 9.2 %collective-permute-start.17 = (bf16[384,128]{1,0:T(8,128)(2,1)S(1)}, bf16[384,128]{1,0:T(8,128)(2,1)S(1)}, u32[]{:S(2)}, u32[]{:S(2)}) collective-permute-start(bf16[384,128]{1,0:T(8,128)(2,1)S(1)} %get-tuple-element.38), channel_id=1, source_target_pairs={{0,24},{8,16},{16,8},{24,0},{1,25},{9,17},{17,9},{25,1},{2,26},{10... | collective-permute-start | bytes 294920 | tf_op jit(solution)/shard_map/ppermute | solution.py:34
  40.3 7.5 %copy-start.1 = (bf16[4,1,3,16,8,128]{5,4,3,2,1,0:T(8,128)(2,1)S(1)}, bf16[4,1,3,16,8,128]{5,4,3,2,1,0:T(8,128)(2,1)}, u32[]{:S(2)}) copy-start(bf16[4,1,3,16,8,128]{5,4,3,2,1,0:T(8,128)(2,1)} %param.5) | copy-start | bytes 1179652
  40.3 5.6 %collective-permute-start.18 = (bf16[384,128]{1,0:T(8,128)(2,1)S(1)}, bf16[384,128]{1,0:T(8,128)(2,1)S(1)}, u32[]{:S(2)}, u32[]{:S(2)}) collective-permute-start(bf16[384,128]{1,0:T(8,128)(2,1)S(1)} %get-tuple-element.40), channel_id=1, source_target_pairs={{0,8},{8,0},{16,24},{24,16},{1,9},{9,1},{17,25},{25,17},{2,10},{10... | collective-permute-start | bytes 294920 | tf_op jit(solution)/shard_map/ppermute | solution.py:34
  40.9 5.7 %collective-permute-start.19 = (bf16[384,128]{1,0:T(8,128)(2,1)S(1)}, bf16[384,128]{1,0:T(8,128)(2,1)S(1)}, u32[]{:S(2)}, u32[]{:S(2)}) collective-permute-start(bf16[384,128]{1,0:T(8,128)(2,1)S(1)} %get-tuple-element.41), channel_id=1, source_target_pairs={{0,16},{8,24},{16,0},{24,8},{1,17},{9,25},{17,1},{25,9},{2,18},{10... | collective-permute-start | bytes 294920 | tf_op jit(solution)/shard_map/ppermute | solution.py:34
  42.2 5.5 %collective-permute-start.20 = (bf16[384,128]{1,0:T(8,128)(2,1)S(1)}, bf16[384,128]{1,0:T(8,128)(2,1)S(1)}, u32[]{:S(2)}, u32[]{:S(2)}) collective-permute-start(bf16[384,128]{1,0:T(8,128)(2,1)S(1)} %get-tuple-element.42), channel_id=1, source_target_pairs={{0,24},{8,16},{16,8},{24,0},{1,25},{9,17},{17,9},{25,1},{2,26},{10... | collective-permute-start | bytes 294920 | tf_op jit(solution)/shard_map/ppermute | solution.py:34
  50.2 5.3 %collective-permute-start.21 = (bf16[4,432,128]{2,1,0:T(8,128)(2,1)S(1)}, bf16[4,432,128]{2,1,0:T(8,128)(2,1)S(1)}, u32[]{:S(2)}, u32[]{:S(2)}) collective-permute-start(bf16[4,432,128]{2,1,0:T(8,128)(2,1)S(1)} %get-tuple-element.44), channel_id=1, source_target_pairs={{0,1},{1,0},{2,3},{3,2},{4,5},{5,4},{6,7},{7,6},{8,9},{9,8},{10,11... | collective-permute-start | bytes 1327112 | tf_op jit(solution)/shard_map/ppermute | solution.py:34
  52.0 8.4 %collective-permute-start.12 = (bf16[2,384,128]{2,1,0:T(8,128)(2,1)S(1)}, bf16[2,384,128]{2,1,0:T(8,128)(2,1)S(1)}, u32[]{:S(2)}, u32[]{:S(2)}) collective-permute-start(bf16[2,384,128]{2,1,0:T(8,128)(2,1)S(1)} %get-tuple-element.30), channel_id=1, source_target_pairs={{0,8},{8,0},{16,24},{24,16},{1,9},{9,1},{17,25},{25,17},{2,10},{10... | collective-permute-start | bytes 589832 | tf_op jit(solution)/shard_map/ppermute | solution.py:34
  53.0 11.2 %collective-permute-start.13 = (bf16[2,384,128]{2,1,0:T(8,128)(2,1)S(1)}, bf16[2,384,128]{2,1,0:T(8,128)(2,1)S(1)}, u32[]{:S(2)}, u32[]{:S(2)}) collective-permute-start(bf16[2,384,128]{2,1,0:T(8,128)(2,1)S(1)} %get-tuple-element.31), channel_id=1, source_target_pairs={{0,16},{8,24},{16,0},{24,8},{1,17},{9,25},{17,1},{25,9},{2,18},{10... | collective-permute-start | bytes 589832 | tf_op jit(solution)/shard_map/ppermute | solution.py:34
  54.2 10.0 %collective-permute-start.14 = (bf16[2,384,128]{2,1,0:T(8,128)(2,1)S(1)}, bf16[2,384,128]{2,1,0:T(8,128)(2,1)S(1)}, u32[]{:S(2)}, u32[]{:S(2)}) collective-permute-start(bf16[2,384,128]{2,1,0:T(8,128)(2,1)S(1)} %get-tuple-element.32), channel_id=1, source_target_pairs={{0,24},{8,16},{16,8},{24,0},{1,25},{9,17},{17,9},{25,1},{2,26},{10... | collective-permute-start | bytes 589832 | tf_op jit(solution)/shard_map/ppermute | solution.py:34
  56.2 9.5 %collective-permute-start.22 = (bf16[432,128]{1,0:T(8,128)(2,1)S(1)}, bf16[432,128]{1,0:T(8,128)(2,1)S(1)}, u32[]{:S(2)}, u32[]{:S(2)}) collective-permute-start(bf16[432,128]{1,0:T(8,128)(2,1)S(1)} %get-tuple-element.46), channel_id=1, source_target_pairs={{0,2},{1,3},{2,0},{3,1},{4,6},{5,7},{6,4},{7,5},{8,10},{9,11},{10,... | collective-permute-start | bytes 331784 | tf_op jit(solution)/shard_map/ppermute | solution.py:34
  57.8 11.0 %collective-permute-start.23 = (bf16[432,128]{1,0:T(8,128)(2,1)S(1)}, bf16[432,128]{1,0:T(8,128)(2,1)S(1)}, u32[]{:S(2)}, u32[]{:S(2)}) collective-permute-start(bf16[432,128]{1,0:T(8,128)(2,1)S(1)} %get-tuple-element.47), channel_id=1, source_target_pairs={{0,4},{1,5},{2,6},{3,7},{4,0},{5,1},{6,2},{7,3},{8,12},{9,13},{10,... | collective-permute-start | bytes 331784 | tf_op jit(solution)/shard_map/ppermute | solution.py:34
  60.4 8.4 %collective-permute-start.24 = (bf16[432,128]{1,0:T(8,128)(2,1)S(1)}, bf16[432,128]{1,0:T(8,128)(2,1)S(1)}, u32[]{:S(2)}, u32[]{:S(2)}) collective-permute-start(bf16[432,128]{1,0:T(8,128)(2,1)S(1)} %get-tuple-element.48), channel_id=1, source_target_pairs={{0,6},{1,7},{2,4},{3,5},{4,2},{5,3},{6,0},{7,1},{8,14},{9,15},{10,... | collective-permute-start | bytes 331784 | tf_op jit(solution)/shard_map/ppermute | solution.py:34

commit v2 on v1

v2 whole, which is shorter than its diff:
```python
import functools
import math

import jax
import jax.numpy as jnp
from jax import lax
from jax.experimental import pallas as pl
from jax.experimental.pallas import tpu as pltpu
from jax.sharding import PartitionSpec as P

GROUPS = 32
EPS = 1e-06
BF, F32 = jnp.bfloat16, jnp.float32
VMEM_LIMIT = 28 * 1024 * 1024
VM = pl.BlockSpec(memory_space=pltpu.VMEM)
SM = pl.BlockSpec(memory_space=pltpu.SMEM)
ANY = pl.BlockSpec(memory_space=pl.ANY)
HBM = pl.BlockSpec(memory_space=pltpu.HBM)


def call(kernel, out_shape, in_specs, out_specs, scratch=(), flops=0, moved=0, limit=VMEM_LIMIT):
    return pl.pallas_call(
        kernel,
        out_shape=out_shape,
        in_specs=in_specs,
        out_specs=out_specs,
        scratch_shapes=list(scratch),
        compiler_params=pltpu.CompilerParams(vmem_limit_bytes=limit),
        cost_estimate=pl.CostEstimate(flops=flops, bytes_accessed=moved, transcendentals=0),
    )


def swap(value, axis, bits):
    count = lax.axis_size(axis)
    return lax.ppermute(value, axis, [(i, i ^ bits) for i in range(count)])


def lane_partner(row, step):
    lane = lax.broadcasted_iota(jnp.int32, row.shape, 1)
    ahead = pltpu.roll(row, row.shape[1] - step, 1)
    return jnp.where((lane & step) == 0, ahead, pltpu.roll(row, step, 1))


def tree(parts):
    parts = list(parts)
    while len(parts) > 1:
        pairs = [u + v for u, v in zip(parts[::2], parts[1::2])]
        parts = pairs + parts[len(pairs) * 2 :]
    return parts[0]


def tiles(values):
    return [values[i : i + 8] for i in range(0, values.shape[0], 8)]


def group_sum(values, width):
    row = tree(tiles(values))
    for step in (4, 2, 1):
        row = row + pltpu.roll(row, step, 0)
    step = 1
    while step < width:
        row = row + lane_partner(row, step)
        step *= 2
    return row


def statistics(x32, width):
    parts = tiles(x32)
    pivot = parts[0]
    gaps = [part - pivot for part in parts[1:]]
    first = tree(gaps)
    second = tree([gap * gap for gap in gaps])
    count = float(len(parts))
    mean = pivot + first * (1.0 / count)
    spread = jnp.maximum(second - first * first * (1.0 / count), 0.0)

    def join(mean, spread, other, other_spread):
        gap = mean - other
        return (mean + other) * 0.5, spread + other_spread + gap * gap * (0.5 * count)

    for step in (4, 2, 1):
        mean, spread = join(mean, spread, pltpu.roll(mean, step, 0), pltpu.roll(spread, step, 0))
        count *= 2.0
    step = 1
    while step < width:
        mean, spread = join(mean, spread, lane_partner(mean, step), lane_partner(spread, step))
        count *= 2.0
        step *= 2
    return mean, lax.rsqrt(spread * (1.0 / count) + EPS)


def side(frame, cols, step):
    lines = frame.reshape(-1, cols, frame.shape[1])
    moved = pltpu.roll(lines, (-step) % cols, 1)
    col = lax.broadcasted_iota(jnp.int32, lines.shape, 1)
    keep = col < cols - 1 if step > 0 else col > 0
    return jnp.where(keep, moved, 0.0).reshape(frame.shape)


def row_shift(frame, cols, step):
    gap = jnp.zeros((cols, frame.shape[1]), frame.dtype)
    if step > 0:
        return jnp.concatenate([frame[cols:], gap], axis=0)
    return jnp.concatenate([gap, frame[:-cols]], axis=0)


def three_rows(frame, cols, steps):
    return [(frame if step == 0 else row_shift(frame, cols, step)).astype(BF) for step in steps]


def put_rows(spread, index, a, pieces):
    for b, piece in enumerate(pieces):
        chans = piece.shape[1]
        at = (3 * a + b) * chans
        spread[index, :, at : at + chans] = piece


def join_cols(parts, cols, chans, steps):
    total = None
    for at, step in enumerate(steps):
        piece = parts[:, at * chans : (at + 1) * chans]
        piece = piece if step == 0 else side(piece, cols, step)
        total = piece if total is None else total + piece
    return total


def copies_of(chunks, halves, target, sem):
    quarter = chunks[0].shape[1]
    return [
        pltpu.make_async_copy(
            ref.at[0 : target.shape[0]], target.at[:, pl.ds(pl.multiple_of(at * quarter, quarter), quarter), :], sem
        )
        for ref, at in zip(chunks, halves)
    ]


def piece_ids(ids, n_chunk):
    per = n_chunk // 2
    return [ids[1] * per + j for j in range(per)] + [(1 - ids[1]) * per + j for j in range(per)]


def forward_matrix(taps):
    chans = taps.shape[-1]
    parts = taps.reshape(9, 3, chans, chans)
    return jnp.concatenate([parts[:, c].reshape(9 * chans, chans) for c in range(3)], axis=1)


def backward_matrix(taps):
    chans = taps.shape[-1]
    parts = taps.reshape(9, 3 * chans, chans)
    return jnp.concatenate([parts[ab] for ab in range(9)], axis=1)


def norm_parts(x32, mean, rstd, gain):
    normed = (x32 - mean) * rstd
    scaled = normed * gain
    return normed, scaled, 0.5 * jnp.tanh(0.5 * scaled) + 0.5


def full(row, count):
    return jnp.broadcast_to(row[:1], (count, row.shape[1]))


def spread_forward(dims, values, found, gain, spread):
    frames, rows, cols, chans = dims
    plane, points = rows * cols, frames * rows * cols
    for k, x32 in enumerate(values):
        mean, rstd = found[k]
        _, scaled, gate = norm_parts(x32, full(mean, points), full(rstd, points), full(gain, points))
        act = scaled * gate
        for source in range(frames):
            pieces = three_rows(act[source * plane : (source + 1) * plane], cols, (-1, 0, 1))
            for f in range(frames):
                for a in range(3):
                    if max(f - 2 + a, 0) == source:
                        put_rows(spread, k * frames + f, a, pieces)


def cut_kernel(parts, ids, gain, own, *refs):
    pieces, sems = refs[:parts], refs[parts]
    taps, quarter = own.shape[0], pieces[0].shape[1]
    copies = []
    for j in range(parts):
        rows = pl.ds(pl.multiple_of((ids[1] * parts + j) * quarter, quarter), quarter)
        copies.append(pltpu.make_async_copy(own.at[:, rows, :], pieces[j].at[0:taps], sems.at[j]))
    for copy in copies:
        copy.start()
    wide = full(gain[...], quarter)
    high = wide.astype(BF).astype(F32)
    middle = (wide - high).astype(BF).astype(F32)
    low = wide - high - middle
    row = lax.broadcasted_iota(jnp.int32, wide.shape, 0)
    pieces[0][taps] = jnp.where(row == 0, high, jnp.where(row == 1, middle, low)).astype(BF)
    for copy in copies:
        copy.wait()


def forward_kernel(sections, dims, ids, x_ref, gain, *refs):
    frames, rows, cols, chans = dims
    plane = rows * cols
    n_chunk = (len(refs) - 8 - sections) // sections
    chunks = [refs[k * n_chunk : (k + 1) * n_chunk] for k in range(sections)]
    refs = refs[sections * n_chunk :]
    outs, stats, every = refs[:3]
    sends = refs[3 : 3 + sections]
    spread, product, gain_rows, gain_sem, sems = refs[3 + sections :]
    place = ids[0]
    taps = every.shape[1]
    copies = [
        pltpu.make_async_copy(chunks[k][0].at[taps], gain_rows.at[k - 1], gain_sem.at[k - 1])
        for k in range(1, sections)
    ]
    for copy in copies:
        copy.start()

    def start(slot, k):
        for copy in copies_of(chunks[k], piece_ids(ids, n_chunk), every.at[slot], sems.at[slot]):
            copy.start()

    for slot in range(sections):
        for k in range(sections):
            pl.when((place ^ k) == slot)(functools.partial(start, slot, k))
    stats[place, 16:24] = full(gain[...], 8)
    for k in range(1, sections):
        copies[k - 1].wait()
        parts = gain_rows[k - 1].astype(F32)
        stats[place ^ k, 16:24] = full(parts[0:1] + parts[1:2] + parts[2:3], 8)
    x = x_ref[...]
    for unit in range(sections):
        for k in range(sections):
            @pl.when((place ^ k) == unit)
            def _(k=k, x=x):
                sends[k][...] = x

        x32 = x.astype(F32)
        mean, rstd = statistics(x32, chans // GROUPS)
        stats[unit, 0:8], stats[unit, 8:16] = mean, rstd
        spread_forward(dims, [x32], [(mean, rstd)], stats[unit, 16:17], spread)
        pltpu.make_async_copy(every.at[unit], every.at[unit], sems.at[unit]).wait()
        lhs = spread[...].reshape(frames * plane, 9 * chans)
        product[...] = jnp.dot(lhs, forward_matrix(every[unit]), preferred_element_type=F32)
        for f in range(frames):
            spot = slice(f * plane, (f + 1) * plane)
            joined = join_cols(product[spot], cols, chans, (-1, 0, 1))
            outs[unit, spot] = (x32[spot] + joined).astype(BF)
        x = outs[unit]


def turn_kernel(dims, n, gain, *refs):
    frames, rows, cols, chans = dims
    plane, points = rows * cols, frames * rows * cols
    xs, (turned, stats) = refs[:n], refs[n:]
    for k in range(n):
        x32 = xs[k][...].astype(F32)
        mean, rstd = statistics(x32, chans // GROUPS)
        stats[k, 0:8], stats[k, 8:16] = mean, rstd
        _, scaled, gate = norm_parts(x32, full(mean, points), full(rstd, points), full(gain[...], points))
        act = (scaled * gate).astype(BF).astype(F32)
        for f in range(frames):
            frame = act[f * plane : (f + 1) * plane]
            for at, step in enumerate((-1, 0, 1)):
                piece = frame if step == 0 else row_shift(frame, cols, step)
                turned[at * chans : (at + 1) * chans, pl.ds((f * n + k) * plane, plane)] = piece.T.astype(BF)


def home_forward_kernel(dims, n, ids, stats, gain, own, *refs):
    frames, rows, cols, chans = dims
    plane = rows * cols
    xs, (seg, spread) = refs[:n], refs[n:]
    values = [ref[...].astype(F32) for ref in xs]
    known = [(stats[k, 0:8], stats[k, 8:16]) for k in range(n)]
    spread_forward(dims, values, known, gain[...], spread)
    lhs = spread[...].reshape(n * frames * plane, 9 * chans)
    product = jnp.dot(lhs, forward_matrix(own[...]), preferred_element_type=F32)
    for k in range(n):
        at = (ids[0] ^ k) % n
        for f in range(frames):
            spot = slice(f * plane, (f + 1) * plane)
            joined = join_cols(product[(k * frames + f) * plane : (k * frames + f + 1) * plane], cols, chans, (-1, 0, 1))
            seg[at, spot] = (values[k][spot] + joined).astype(BF)


def unit_backward(dims, x32, grad, stat, gain, multiply, spread):
    frames, rows, cols, chans = dims
    plane, points = rows * cols, frames * rows * cols
    width = chans // GROUPS
    count = float(points * width)
    g32 = grad.astype(F32)
    per = [g32[f * plane : (f + 1) * plane] for f in range(frames)]
    for f in range(frames):
        for a in range(3):
            sources = [q for q in range(frames) if max(q - 2 + a, 0) == f]
            if sources:
                total = functools.reduce(lambda u, v: u + v, [per[q] for q in sources])
                put_rows(spread, f, a, three_rows(total, cols, (1, 0, -1)))
            else:
                put_rows(spread, f, a, [jnp.zeros((plane, chans), BF)] * 3)
    product = multiply(spread[...].reshape(points, 9 * chans))
    gact = jnp.concatenate(
        [join_cols(product[f * plane : (f + 1) * plane], cols, chans, (1, 0, -1)) for f in range(frames)], axis=0
    )
    rstd = full(stat[8:16], points)
    wide_gain = full(gain, points)
    normed, scaled, gate = norm_parts(x32, full(stat[0:8], points), rstd, wide_gain)
    d_normed = gact * (gate * (1.0 + scaled * (1.0 - gate))) * wide_gain
    m1 = group_sum(d_normed, width) * (1.0 / count)
    m2 = group_sum(d_normed * normed, width) * (1.0 / count)
    dx = rstd * (d_normed - full(m1, points) - normed * full(m2, points))
    return (g32 + dx).astype(BF)


def times_transposed(lhs, taps):
    return lax.dot_general(lhs, backward_matrix(taps), (((1,), (1,)), ((), ())), preferred_element_type=F32)


def backward_kernel(sections, dims, ids, outs, grad_ref, stats, every, *refs):
    sends, spread = refs[:sections], refs[sections]
    place = ids[0]
    grad = grad_ref[...]
    for k in range(sections):
        @pl.when((place ^ k) == sections - 1)
        def _(k=k, grad=grad):
            sends[k][...] = grad
    for unit in range(sections - 1, 0, -1):

        def multiply(lhs, unit=unit):
            return times_transposed(lhs, every[unit])

        grad = unit_backward(dims, outs[unit - 1].astype(F32), grad, stats[unit], stats[unit, 16:17], multiply, spread)
        for k in range(sections):
            @pl.when((place ^ k) == unit - 1)
            def _(k=k, grad=grad):
                sends[k][...] = grad


def home_backward_kernel(dims, n, first, last, ids, stats, gain, own, *refs):
    count = last - first
    xs, grads = refs[:count], refs[count : 2 * count]
    refs = refs[2 * count :]
    done = refs[:first] if last == n else ()
    outs, spread = refs[len(done) : -1], refs[-1]
    place = ids[0]
    for k in range(len(done)):
        outs[0][(place ^ k) % n] = done[k][...]
    for i in range(count):
        result = unit_backward(
            dims,
            xs[i][...].astype(F32),
            grads[i][...],
            stats[first + i],
            gain[...],
            lambda lhs: times_transposed(lhs, own[...]),
            spread,
        )
        if last == n:
            outs[0][(place ^ (first + i)) % n] = result
        else:
            outs[i][...] = result


def term_kernel(dims, n, shares, ids, turned, *refs):
    frames, rows, cols, chans = dims
    plane = rows * cols
    grads = refs[:n]
    rest = refs[n:]
    term = rest[-1] if shares else rest[0]
    right = rest[-2] if shares else rest[1]
    spots = [0]
    for a in range(3):
        spots.append(spots[-1] + max(1, min(frames, frames - 2 + a)))
    for k in range(n):
        mine = grads[k][...].astype(F32)
        per = [mine[f * plane : (f + 1) * plane] for f in range(frames)]
        sides = [[side(p, cols, 1), p, side(p, cols, -1)] for p in per]
        for a in range(3):
            folded = [f for f in range(frames) if f - 2 + a <= 0]
            groups = [folded] + [[f] for f in range(frames) if f - 2 + a > 0]
            for i, group in enumerate(groups):
                for c in range(3):
                    piece = functools.reduce(lambda u, v: u + v, [sides[f][c] for f in group])
                    right[pl.ds(((spots[a] + i) * n + k) * plane, plane), c * chans : (c + 1) * chans] = piece.astype(BF)
    for a in range(3):
        used = (spots[a + 1] - spots[a]) * n * plane
        lhs = turned[:, 0:used]
        rhs = right[pl.ds(spots[a] * n * plane, used), :]
        out = jnp.dot(lhs, rhs, preferred_element_type=F32)
        for b in range(3):
            for c in range(3):
                block = out[b * chans : (b + 1) * chans, c * chans : (c + 1) * chans]
                term[pl.ds(((a * 3 + b) * 3 + c) * chans, chans), :] = block.astype(BF)
    if shares:
        keep, send = rest[0], rest[1]
        core = ids[1]
        size = keep.shape[1]
        for j in range(shares // 2):
            here = pl.multiple_of((2 * j + core) * size, size)
            there = pl.multiple_of((2 * j + 1 - core) * size, size)
            keep[j] = term[pl.ds(here, size), :]
            send[j] = term[pl.ds(there, size), :]


def pair_kernel(count, ids, keep, got, own, *sends):
    level = ids[2]
    for k in range(count):
        at = level ^ k
        total = keep[at].astype(F32) + got[at].astype(F32)
        if k == 0:
            own[...] = total
        else:
            sends[k - 1][...] = total.astype(BF)


def sum_kernel(scale, own, *refs):
    total = own[...]
    for ref in refs[:-1]:
        total = total + ref[...].astype(F32)
    refs[-1][...] = total * scale


def gather_chunks(mine, sections, ride):
    parts = len(mine)
    got = {}
    if sections == 4 and parts == 2:
        first = swap(mine[0], "pipe", 1)
        second = swap(mine[1], "pipe", 2)
        first, *ride = lax.optimization_barrier((first, *ride))
        got[1] = [first, swap(mine[1], "pipe", 1)]
        got[2] = [swap(mine[0], "pipe", 2), second]
        got[3] = [swap(first, "pipe", 2), swap(second, "pipe", 1)]
    else:
        for k in range(1, sections):
            got[k] = [swap(piece, "pipe", k) for piece in mine]
    return got, ride


def body(video, cotangent, weights, gains):
    sections = lax.axis_size("pipe")
    ranks = lax.axis_size("dp")
    place = lax.axis_index("pipe")
    rank = lax.axis_index("dp")
    core = lax.rem(rank, 2)
    micro, clips, frames, rows, cols, chans = video.shape
    ids = jnp.stack([place, core, lax.div(rank, 2)]).astype(jnp.int32)
    points = frames * rows * cols
    dims = (frames, rows, cols, chans)
    parts = 2
    n_chunk = 2 * parts
    quarter = chans // n_chunk

    video = video.reshape(micro, points, chans)
    cot = cotangent.reshape(micro, points, chans)
    kernel_rows = weights.reshape(27, chans, chans)
    gain_rows = jnp.broadcast_to(gains, (8, chans))
    mine = call(
        functools.partial(cut_kernel, parts),
        [jax.ShapeDtypeStruct((27 + (j == 0), quarter, chans), BF) for j in range(parts)],
        [SM, VM, ANY],
        [VM] * parts,
        [pltpu.SemaphoreType.DMA((parts,))],
    )(ids, gain_rows, kernel_rows)
    x = lax.dynamic_index_in_dim(video, lax.rem(place, micro), 0, False)
    grad = lax.dynamic_index_in_dim(cot, lax.rem(place, micro), 0, False)
    got, (x, grad) = gather_chunks(mine, sections, (x, grad))
    got[0] = list(mine)
    flat = [piece for k in range(sections) for piece in got[k] + [swap(piece, "dp", 1) for piece in got[k]]]

    act_shape = jax.ShapeDtypeStruct((points, chans), BF)
    unit_flops = 2 * points * 27 * chans * chans
    n = min(sections, micro)
    spots = sum(max(1, frames - 2 + a) for a in range(3))

    def spread(count):
        return pltpu.VMEM((count * frames, rows * cols, 9 * chans), BF)

    product = pltpu.VMEM((points, 3 * chans), F32)

    outs, stats, every, *xsends = call(
        functools.partial(forward_kernel, sections, dims),
        [
            jax.ShapeDtypeStruct((sections, points, chans), BF),
            jax.ShapeDtypeStruct((sections, 24, chans), F32),
            jax.ShapeDtypeStruct((sections, 27, chans, chans), BF),
        ]
        + [act_shape] * sections,
        [SM, VM, VM] + [ANY] * len(flat),
        [VM] * (3 + sections),
        [
            spread(1),
            product,
            pltpu.VMEM((sections - 1, quarter, chans), BF),
            pltpu.SemaphoreType.DMA((sections - 1,)),
            pltpu.SemaphoreType.DMA((sections,)),
        ],
        flops=4 * sections * unit_flops,
    )(ids, x, gain_rows, *flat)
    xs_home = [xsends[0]] + [swap(xsends[k], "pipe", k) for k in range(1, n)]

    gsends = call(
        functools.partial(backward_kernel, sections, dims),
        [act_shape] * sections,
        [SM] + [VM] * 4,
        [VM] * sections,
        [spread(1)],
        flops=4 * (sections - 1) * unit_flops,
    )(ids, outs, grad, stats, every)
    grads_home = [gsends[0]] + [swap(gsends[k], "pipe", k) for k in range(1, n)]

    turned, home_stats = call(
        functools.partial(turn_kernel, dims, n),
        [jax.ShapeDtypeStruct((3 * chans, n * points), BF), jax.ShapeDtypeStruct((n, 16, chans), F32)],
        [VM] * (1 + n),
        [VM] * 2,
        flops=n * unit_flops,
    )(gain_rows, *xs_home)

    def home_forward(ids):
        return call(
            functools.partial(home_forward_kernel, dims, n),
            jax.ShapeDtypeStruct((micro, points, chans), BF),
            [SM, VM, VM, VM] + [VM] * n,
            VM,
            [spread(n)],
            flops=4 * n * unit_flops,
        )(ids, home_stats, gain_rows, kernel_rows, *xs_home)

    def home_backward(first, last, done, ids):
        count = last - first
        return call(
            functools.partial(home_backward_kernel, dims, n, first, last),
            [jax.ShapeDtypeStruct((micro, points, chans), BF)] if last == n else [act_shape] * count,
            [SM, VM, VM, VM] + [VM] * (2 * count + len(done)),
            [VM] * (1 if last == n else count),
            [spread(1)],
            flops=4 * count * unit_flops,
        )(ids, home_stats, gain_rows, kernel_rows, *xs_home[first:last], *grads_home[first:last], *done)

    size = 27 * chans // ranks
    right = pltpu.VMEM((spots * n * rows * cols, 3 * chans), BF)
    half = jax.ShapeDtypeStruct((ranks // 2, size, chans), BF)
    levels = ranks // 2
    if size % 16 == 0:
        keep, send = call(
            functools.partial(term_kernel, dims, n, ranks),
            [half, half],
            [SM, VM] + [VM] * n,
            [VM, VM],
            [right, pltpu.VMEM((27 * chans, chans), BF)],
            flops=n * unit_flops,
        )(ids, turned, *grads_home)
    else:
        term = call(
            functools.partial(term_kernel, dims, n, 0),
            jax.ShapeDtypeStruct((27 * chans, chans), BF),
            [SM, VM] + [VM] * n,
            VM,
            [right],
            flops=n * unit_flops,
        )(ids, turned, *grads_home)
        shares = term.reshape(levels, 2, size, chans)
        keep = lax.dynamic_index_in_dim(shares, core, 1, False)
        send = lax.dynamic_index_in_dim(shares, 1 - core, 1, False)
    got = swap(send, "dp", 1)
    early = home_backward(0, n // 2, (), ids)
    piece = jax.ShapeDtypeStruct((size, chans), BF)
    own, *zsends = call(
        functools.partial(pair_kernel, levels),
        [jax.ShapeDtypeStruct((size, chans), F32)] + [piece] * (levels - 1),
        [SM, VM, VM],
        [VM] * levels,
    )(ids, keep, got)
    arrived = [swap(zsends[k - 1], "dp", 2 * k) for k in range(levels - 1, 0, -1)]

    scale = 1.0 / math.sqrt(micro * clips * ranks * points)
    share = call(
        functools.partial(sum_kernel, scale),
        jax.ShapeDtypeStruct((size, chans), F32),
        [VM] * levels,
        VM,
    )(own, *arrived)

    late, _ = lax.optimization_barrier((ids, own))
    (ing,) = home_backward(n // 2, n, early, late)
    seg = home_forward(late)
    shape = (1, micro, clips, frames, rows, cols, chans)
    return (seg.reshape(shape), ing.reshape(shape), share.reshape(1, size * chans))


def solution(mesh):
    in_specs = (
        P(None, "dp", None, None, None, None),
        P(None, "dp", None, None, None, None),
        P("pipe", None, None),
        P("pipe", None),
    )
    out_specs = (
        P("pipe", None, "dp", None, None, None, None),
        P("pipe", None, "dp", None, None, None, None),
        P("pipe", "dp"),
    )
    return jax.shard_map(body, mesh=mesh, in_specs=in_specs, out_specs=out_specs, check_vma=False)
```

time: 69.8 us -> 66 us (0.946)
  blocking collectives: 9.59 us -> 0 us
  starting transfers between devices: 27.6 us -> 21 us
  Pallas kernels: 17.1 us -> 23 us
  waiting for transfers between devices: 12.4 us -> 18.2 us
    all_gather x1 -> x0, blocking collectives: 9.59 us -> none  [body(): all_gains = lax.all_gather(gains[0], 'pipe')]
    ppermute x25 -> x24, starting transfers between devices: 27.6 us -> 21 us  [swap(): return lax.ppermute(value, axis, [(i, i ^ bits) for i in range(count)])]
    pallas_call x6 -> x8, Pallas kernels: 15.7 us -> 21.6 us  [the longest x1 5.58 us: body(): call(functools.partial(forward_kernel, sections, dims), [jax.ShapeDtypeSt...]
    ppermute x25 -> x24, waiting for transfers between devices: 12.4 us -> 18.2 us  [swap(): return lax.ppermute(value, axis, [(i, i ^ bits) for i in range(count)])]
    unnamed x4, local copies, waits for them, and re-layouts: 0.01 us -> 1.17 us
    squeeze x2 -> x1, local copies, waits for them, and re-layouts: 2.11 us -> 0.95 us  [body(): grad = lax.dynamic_index_in_dim(cot, lax.rem(place, micro), 0, False)]
  transfers between devices with their start and end apart: 25 -> 24, of which waited for: 9 -> 12; matrix products, arithmetic and copies ran while one was open for 1% -> 1% of each run, Pallas kernels for 12% -> 20%
where the time goes in v2:
time: 66 us; the launch traced here: 65.8 us
  Pallas kernels  23 us (35%)
  starting transfers between devices  21 us (32%)
  waiting for transfers between devices  18.2 us (28%)
  local copies, waits for them, and re-layouts  2.78 us (4%)
  between operations  0.75 us (1%)
    ppermute x24, starting transfers between devices, swap(): return lax.ppermute(value, axis, [(i, i ^ bits) for i in range(count)])  21 us
    ppermute x24, waiting for transfers between devices, swap(): return lax.ppermute(value, axis, [(i, i ^ bits) for i in range(count)])  18.2 us
    pallas_call x1, Pallas kernels, body(): call(functools.partial(forward_kernel, sections, dims), [jax.ShapeDtypeSt...  5.58 us
    pallas_call x2, Pallas kernels, home_backward(): call(functools.partial(home_backward_kernel, dims, n, first, last), [jax....  4.92 us
    pallas_call x1, Pallas kernels, home_forward(): call(functools.partial(home_forward_kernel, dims, n), jax.ShapeDtypeStruc...  3.69 us
    pallas_call x1, Pallas kernels, body(): call(functools.partial(backward_kernel, sections, dims), [act_shape] * se...  3.66 us
    pallas_call x1, Pallas kernels, body(): call(functools.partial(term_kernel, dims, n, ranks), [half, half], [SM, V...  2.28 us
  transfers between devices with their start and end apart: 24, of which 12 were waited for; matrix products, arithmetic and copies ran while one was open for 1% of the time, Pallas kernels for 20%

profile of v2, /device:TPU:0, one launch (start us, length us, event | category | flops | bytes accessed | tf_op | source)
XLA Modules:
  0.0 65.8 jit_solution(6325540430322154317)
XLA Ops:
  0.6 0.1 pad_add_fusion.ids
  0.7 0.7 %broadcast_in_dim.8.gain = f32[8,128]{1,0:T(8,128)S(1)} broadcast(f32[128]{0:T(128)} %bitcast.25), dimensions={1} | broadcast | bytes 4608 | tf_op jit(solution)/shard_map/broadcast_in_dim | solution.py:453
  1.4 1.2 %copy-done = bf16[1,3456,128]{2,1,0:T(8,128)(2,1)S(1)} copy-done((bf16[1,3456,128]{2,1,0:T(8,128)(2,1)S(1)}, bf16[1,3456,128]{2,1,0:T(8,128)(2,1)}, u32[]{:S(2)}) %copy-start) | copy-done | bytes 884760
  2.5 0.6 shard_map.67
  3.2 3.0 %collective-permute-start = (bf16[28,32,128]{2,1,0:T(8,128)(2,1)S(1)}, bf16[28,32,128]{2,1,0:T(8,128)(2,1)S(1)}, u32[]{:S(2)}, u32[]{:S(2)}) collective-permute-start(bf16[28,32,128]{2,1,0:T(8,128)(2,1)S(1)} %get-tuple-element.30.refs_0_), channel_id=1, source_target_pairs={{0,8},{8,0},{16,24},{24,16},{1,9},{9,1},{17,25},{25,17},{2,10},{10... | collective-permute-start | bytes 688136 | tf_op jit(solution)/shard_map/ppermute | solution.py:35
  6.2 1.5 %collective-permute-start.7 = (bf16[27,32,128]{2,1,0:T(8,128)(2,1)S(1)}, bf16[27,32,128]{2,1,0:T(8,128)(2,1)S(1)}, u32[]{:S(2)}, u32[]{:S(2)}) collective-permute-start(bf16[27,32,128]{2,1,0:T(8,128)(2,1)S(1)} %get-tuple-element.32.refs_1_), channel_id=1, source_target_pairs={{0,16},{8,24},{16,0},{24,8},{1,17},{9,25},{17,1},{25,9},{2,18},{10... | collective-permute-start | bytes 663560 | tf_op jit(solution)/shard_map/ppermute | solution.py:35
  7.7 0.5 collective-permute-start.3
  8.2 0.0 collective-permute-start.2
  8.2 0.1 collective-permute-start.6
  8.3 1.0 %dynamic-slice_bitcast_fusion = (bf16[384,128]{1,0:T(8,128)(2,1)S(1)}, bf16[384,128]{1,0:T(8,128)(2,1)S(1)}) fusion(bf16[4,384,128]{2,1,0:T(8,128)(2,1)} %bitcast.23, s32[]{:T(128)S(6)} %select_n.5, bf16[4,384,128]{2,1,0:T(8,128)(2,1)} %bitcast.24), kind=kLoop, calls=%fused_computation | loop fusion | bytes 393220 | tf_op jit(solution)/shard_map/jit(dynamic_index_in_dim)/squeeze | solution.py:462
  9.3 3.4 %collective-permute-done.refs_4_ = bf16[28,32,128]{2,1,0:T(8,128)(2,1)S(1)} collective-permute-done((bf16[28,32,128]{2,1,0:T(8,128)(2,1)S(1)}, bf16[28,32,128]{2,1,0:T(8,128)(2,1)S(1)}, u32[]{:S(2)}, u32[]{:S(2)}) %collective-permute-start) | collective-permute-done | bytes 229408 | tf_op jit(solution)/shard_map/ppermute | solution.py:35
  12.6 0.0 collective-permute-start.1
  12.6 1.9 %collective-permute-done.7.refs_9_ = bf16[27,32,128]{2,1,0:T(8,128)(2,1)S(1)} collective-permute-done((bf16[27,32,128]{2,1,0:T(8,128)(2,1)S(1)}, bf16[27,32,128]{2,1,0:T(8,128)(2,1)S(1)}, u32[]{:S(2)}, u32[]{:S(2)}) %collective-permute-start.7) | collective-permute-done | bytes 221216 | tf_op jit(solution)/shard_map/ppermute | solution.py:35
  14.5 1.5 %collective-permute-start.10 = (bf16[28,32,128]{2,1,0:T(8,128)(2,1)S(1)}, bf16[28,32,128]{2,1,0:T(8,128)(2,1)S(1)}, u32[]{:S(2)}, u32[]{:S(2)}) collective-permute-start(bf16[28,32,128]{2,1,0:T(8,128)(2,1)S(1)} %collective-permute-done.refs_4_), channel_id=1, source_target_pairs={{0,16},{8,24},{16,0},{24,8},{1,17},{9,25},{17,1},{25,9},{2,18},{10... | collective-permute-start | bytes 688136 | tf_op jit(solution)/shard_map/ppermute | solution.py:35
  16.1 0.5 collective-permute-done.3.refs_5_
  16.5 1.7 %collective-permute-start.11 = (bf16[27,32,128]{2,1,0:T(8,128)(2,1)S(1)}, bf16[27,32,128]{2,1,0:T(8,128)(2,1)S(1)}, u32[]{:S(2)}, u32[]{:S(2)}) collective-permute-start(bf16[27,32,128]{2,1,0:T(8,128)(2,1)S(1)} %collective-permute-done.7.refs_9_), channel_id=1, source_target_pairs={{0,8},{8,0},{16,24},{24,16},{1,9},{9,1},{17,25},{25,17},{2,10},{10... | collective-permute-start | bytes 663560 | tf_op jit(solution)/shard_map/ppermute | solution.py:35
  18.3 0.0 collective-permute-done.2.refs_3_
  18.3 0.0 collective-permute-start.9
  18.3 1.2 %collective-permute-done.6.refs_8_ = bf16[28,32,128]{2,1,0:T(8,128)(2,1)S(1)} collective-permute-done((bf16[28,32,128]{2,1,0:T(8,128)(2,1)S(1)}, bf16[28,32,128]{2,1,0:T(8,128)(2,1)S(1)}, u32[]{:S(2)}, u32[]{:S(2)}) %collective-permute-start.6) | collective-permute-done | bytes 229408 | tf_op jit(solution)/shard_map/ppermute | solution.py:35
  19.5 0.0 collective-permute-start.8
  19.5 0.0 collective-permute-done.1.refs_2_
  19.5 0.5 collective-permute-start.4
  20.0 2.9 %collective-permute-done.10.refs_12_ = bf16[28,32,128]{2,1,0:T(8,128)(2,1)S(1)} collective-permute-done((bf16[28,32,128]{2,1,0:T(8,128)(2,1)S(1)}, bf16[28,32,128]{2,1,0:T(8,128)(2,1)S(1)}, u32[]{:S(2)}, u32[]{:S(2)}) %collective-permute-start.10) | collective-permute-done | bytes 229408 | tf_op jit(solution)/shard_map/ppermute | solution.py:35
  22.9 0.0 collective-permute-start.12
  22.9 0.2 collective-permute-done.11.refs_13_
  23.1 0.3 collective-permute-start.5
  23.4 0.0 collective-permute-done.9.refs_11_
  23.4 0.2 collective-permute-start.13
  23.7 1.1 %collective-permute-done.5.refs_7_ = bf16[27,32,128]{2,1,0:T(8,128)(2,1)S(1)} collective-permute-done((bf16[27,32,128]{2,1,0:T(8,128)(2,1)S(1)}, bf16[27,32,128]{2,1,0:T(8,128)(2,1)S(1)}, u32[]{:S(2)}, u32[]{:S(2)}) %collective-permute-start.5) | collective-permute-done | bytes 221216 | tf_op jit(solution)/shard_map/ppermute | solution.py:35
  24.7 0.0 collective-permute-done.8.refs_10_
  24.7 0.0 collective-permute-done.4.refs_6_
  24.7 0.3 collective-permute-done.13.refs_15_
  25.0 0.0 collective-permute-done.12.refs_14_
  25.0 5.6 %shard_map.68 = (bf16[4,384,128]{2,1,0:T(8,128)(2,1)S(1)}, f32[4,24,128]{2,1,0:T(8,128)S(1)}, bf16[4,27,128,128]{3,2,1,0:T(8,128)(2,1)S(1)}, bf16[384,128]{1,0:T...) custom-call(s32[3]{0:T(128)S(1)} %pad_add_fusion.ids, ...), custom_call_target="tpu_custom_call" | custom-call | flops 5435817984 | tf_op jit(solution)/shard_map/pallas_call | solution.py:477
  30.6 1.4 %collective-permute-start.14 = (bf16[384,128]{1,0:T(8,128)(2,1)S(1)}, bf16[384,128]{1,0:T(8,128)(2,1)S(1)}, u32[]{:S(2)}, u32[]{:S(2)}) collective-permute-start(bf16[384,128]{1,0:T(8,128)(2,1)S(1)} %get-tuple-element.35), channel_id=1, source_target_pairs={{0,8},{8,0},{16,24},{24,16},{1,9},{9,1},{17,25},{25,17},{2,10},{10... | collective-permute-start | bytes 294920 | tf_op jit(solution)/shard_map/ppermute | solution.py:35
  32.0 1.5 %collective-permute-start.15 = (bf16[384,128]{1,0:T(8,128)(2,1)S(1)}, bf16[384,128]{1,0:T(8,128)(2,1)S(1)}, u32[]{:S(2)}, u32[]{:S(2)}) collective-permute-start(bf16[384,128]{1,0:T(8,128)(2,1)S(1)} %get-tuple-element.36), channel_id=1, source_target_pairs={{0,16},{8,24},{16,0},{24,8},{1,17},{9,25},{17,1},{25,9},{2,18},{10... | collective-permute-start | bytes 294920 | tf_op jit(solution)/shard_map/ppermute | solution.py:35
  33.5 0.7 collective-permute-start.16
  34.2 3.7 %shard_map.70 = (bf16[384,128]{1,0:T(8,128)(2,1)S(1)}, bf16[384,128]{1,0:T(8,128)(2,1)S(1)}, bf16[384,128]{1,0:T(8,128)(2,1)S(1)}, bf16[384,128]{1,0:T(8,128)(2,1)S(1)}) custom-call(s32[3]{0:T(128)S(1)} %pad_add_fusion.ids, bf16[4,384,128]{2,1,0:T(8,128)(2,1)S(1)} %get-tuple-element.39.outs, bf16[384,128]{1,0:T(8,128)(2,1)S(1)} %get-tuple-element.40.grad_ref, ...), custom_call_target="tpu_custom_call" | custom-call | flops 4076863488 | tf_op jit(solution)/shard_map/pallas_call | solution.py:498
  37.8 1.4 %collective-permute-start.17 = (bf16[384,128]{1,0:T(8,128)(2,1)S(1)}, bf16[384,128]{1,0:T(8,128)(2,1)S(1)}, u32[]{:S(2)}, u32[]{:S(2)}) collective-permute-start(bf16[384,128]{1,0:T(8,128)(2,1)S(1)} %get-tuple-element.44), channel_id=1, source_target_pairs={{0,8},{8,0},{16,24},{24,16},{1,9},{9,1},{17,25},{25,17},{2,10},{10... | collective-permute-start | bytes 294920 | tf_op jit(solution)/shard_map/ppermute | solution.py:35
  39.2 1.5 %collective-permute-start.18 = (bf16[384,128]{1,0:T(8,128)(2,1)S(1)}, bf16[384,128]{1,0:T(8,128)(2,1)S(1)}, u32[]{:S(2)}, u32[]{:S(2)}) collective-permute-start(bf16[384,128]{1,0:T(8,128)(2,1)S(1)} %get-tuple-element.45), channel_id=1, source_target_pairs={{0,16},{8,24},{16,0},{24,8},{1,17},{9,25},{17,1},{25,9},{2,18},{10... | collective-permute-start | bytes 294920 | tf_op jit(solution)/shard_map/ppermute | solution.py:35
  40.8 0.0 collective-permute-done.14.refs_1_
  40.8 0.7 collective-permute-start.19
  41.4 0.0 collective-permute-done.15.refs_2_.refs_0_
  41.4 0.0 collective-permute-done.16.refs_3_.refs_1_
  41.4 0.8 %shard_map.69 = (bf16[384,1536]{1,0:T(8,128)(2,1)S(1)}, f32[4,16,128]{2,1,0:T(8,128)S(1)}) custom-call(f32[8,128]{1,0:T(8,128)S(1)} %broadcast_in_dim.8.gain, bf16[384,128]{1,0:T(8,128)(2,1)S(1)} %get-tuple-element.34.refs_0_, bf16[384,128]{1,0:T(8,128)(2,1)S(1)} %collective-permute-done.14.refs_1_, ...), custom_call_target="tpu_custom_call" | custom-call | flops 1358954496 | tf_op jit(solution)/shard_map/pallas_call | solution.py:508
  42.2 0.0 copy-start.1
  42.2 0.8 %collective-permute-done.17.refs_1_.refs_3_ = bf16[384,128]{1,0:T(8,128)(2,1)S(1)} collective-permute-done((bf16[384,128]{1,0:T(8,128)(2,1)S(1)}, bf16[384,128]{1,0:T(8,128)(2,1)S(1)}, u32[]{:S(2)}, u32[]{:S(2)}) %collective-permute-start.17) | collective-permute-done | bytes 98336 | tf_op jit(solution)/shard_map/ppermute | solution.py:35
  43.0 1.9 %collective-permute-done.18.refs_2_ = bf16[384,128]{1,0:T(8,128)(2,1)S(1)} collective-permute-done((bf16[384,128]{1,0:T(8,128)(2,1)S(1)}, bf16[384,128]{1,0:T(8,128)(2,1)S(1)}, u32[]{:S(2)}, u32[]{:S(2)}) %collective-permute-start.18) | collective-permute-done | bytes 98336 | tf_op jit(solution)/shard_map/ppermute | solution.py:35
  44.9 1.4 %collective-permute-done.19.refs_3_ = bf16[384,128]{1,0:T(8,128)(2,1)S(1)} collective-permute-done((bf16[384,128]{1,0:T(8,128)(2,1)S(1)}, bf16[384,128]{1,0:T(8,128)(2,1)S(1)}, u32[]{:S(2)}, u32[]{:S(2)}) %collective-permute-start.19) | collective-permute-done | bytes 98336 | tf_op jit(solution)/shard_map/ppermute | solution.py:35
  46.3 2.3 %shard_map.71 = (bf16[4,432,128]{2,1,0:T(8,128)(2,1)S(1)}, bf16[4,432,128]{2,1,0:T(8,128)(2,1)S(1)}) custom-call(s32[3]{0:T(128)S(1)} %pad_add_fusion.ids, bf16[384,1536]{1,0:T(8,128)(2,1)S(1)} %get-tuple-element.38.turned, bf16[384,128]{1,0:T(8,128)(2,1)S(1)} %get-tuple-element.43.refs_0_.refs_2_, ...), custom_call_target="tpu_custom_call" | custom-call | flops 1358954496 | tf_op jit(solution)/shard_map/pallas_call | solution.py:542
  48.6 0.1 collective-permute-start.20
  48.6 0.0 copy-done.1
  48.6 2.1 %shard_map.74 = (bf16[384,128]{1,0:T(8,128)(2,1)S(1)}, bf16[384,128]{1,0:T(8,128)(2,1)S(1)}) custom-call(s32[3]{0:T(128)S(1)} %pad_add_fusion.ids, f32[4,16,128]{2,1,0:T(8,128)S(1)} %get-tuple-element.51.stats, f32[8,128]{1,0:T(8,128)S(1)} %broadcast_in_dim.8.gain, bf16[27,128,128]{2,1,0:T(8,128)(2,1)S(1)} %bitcast.19, ...), custom_call_target="tpu_custom_call" | custom-call | flops 2717908992 | tf_op jit(solution)/shard_map/pallas_call | solution.py:528
  50.7 0.0 collective-permute-done.20.got
  50.7 0.6 shard_map.72
  51.4 3.7 %collective-permute-start.21 = (bf16[432,128]{1,0:T(8,128)(2,1)S(1)}, bf16[432,128]{1,0:T(8,128)(2,1)S(1)}, u32[]{:S(2)}, u32[]{:S(2)}) collective-permute-start(bf16[432,128]{1,0:T(8,128)(2,1)S(1)} %get-tuple-element.54), channel_id=1, source_target_pairs={{0,6},{1,7},{2,4},{3,5},{4,2},{5,3},{6,0},{7,1},{8,14},{9,15},{10,... | collective-permute-start | bytes 331784 | tf_op jit(solution)/shard_map/ppermute | solution.py:35
  55.1 0.0 collective-permute-start.22
  55.1 0.8 %collective-permute-start.23 = (bf16[432,128]{1,0:T(8,128)(2,1)S(1)}, bf16[432,128]{1,0:T(8,128)(2,1)S(1)}, u32[]{:S(2)}, u32[]{:S(2)}) collective-permute-start(bf16[432,128]{1,0:T(8,128)(2,1)S(1)} %get-tuple-element.56), channel_id=1, source_target_pairs={{0,2},{1,3},{2,0},{3,1},{4,6},{5,7},{6,4},{7,5},{8,10},{9,11},{10,... | collective-permute-start | bytes 331784 | tf_op jit(solution)/shard_map/ppermute | solution.py:35
  55.9 3.7 %shard_map.73 = bf16[4,384,128]{2,1,0:T(8,128)(2,1)} custom-call(s32[3]{0:T(128)S(1)} %pad_add_fusion.ids, f32[4,16,128]{2,1,0:T(8,128)S(1)} %get-tuple-element.51.stats, f32[8,128]{1,0:T(8,128)S(1)} %broadcast_in_dim.8.gain, bf16[27,128,128]{2,1,0:T(8,128)(2,1)S(1)} %bitcast.20, bf16[384,128]{1,0:T(8,128)(2,1)S(1)} %get-tuple-element.34.refs_0_, ...), custom_call_target="tpu_custom_call" | custom-call | flops 5435817984 | tf_op jit(solution)/shard_map/pallas_call | solution.py:517
  59.5 2.8 %shard_map.75 = bf16[4,384,128]{2,1,0:T(8,128)(2,1)} custom-call(s32[3]{0:T(128)S(1)} %pad_add_fusion.ids, f32[4,16,128]{2,1,0:T(8,128)S(1)} %get-tuple-element.51.stats, f32[8,128]{1,0:T(8,128)S(1)} %broadcast_in_dim.8.gain, bf16[27,128,128]{2,1,0:T(8,128)(2,1)S(1)} %bitcast.21, bf16[384,128]{1,0:T(8,128)(2,1)S(1)} %collective-permute-done.15.refs_2_.refs_0_, ...), custom_call_target="tpu_custom_call" | custom-call | flops 2717908992 | tf_op jit(solution)/shard_map/pallas_call | solution.py:528
  62.4 0.0 collective-permute-done.21.refs_0_
  62.4 2.6 %collective-permute-done.22.refs_1_ = bf16[432,128]{1,0:T(8,128)(2,1)S(1)} collective-permute-done((bf16[432,128]{1,0:T(8,128)(2,1)S(1)}, bf16[432,128]{1,0:T(8,128)(2,1)S(1)}, u32[]{:S(2)}, u32[]{:S(2)}) %collective-permute-start.22) | collective-permute-done | bytes 110624 | tf_op jit(solution)/shard_map/ppermute | solution.py:35
  65.0 0.0 collective-permute-done.23.refs_2_
  65.0 0.8 %shard_map.76 = f32[432,128]{1,0:T(8,128)} custom-call(f32[432,128]{1,0:T(8,128)S(1)} %get-tuple-element.49.own, bf16[432,128]{1,0:T(8,128)(2,1)S(1)} %collective-permute-done.21.refs_0_, bf16[432,128]{1,0:T(8,128)(2,1)S(1)} %collective-permute-done.22.refs_1_, bf16[432,128]{1,0:T(8,128)(2,1)S(1)} %collective-permute-done.23.refs_2_), custom_call_target="tpu_custom_call" | custom-call | tf_op jit(solution)/shard_map/pallas_call | solution.py:574
  (1 shorter events, 0.0 us)
Async XLA Ops:
  1.4 1.2 %copy-start = (bf16[1,3456,128]{2,1,0:T(8,128)(2,1)S(1)}, bf16[1,3456,128]{2,1,0:T(8,128)(2,1)}, u32[]{:S(2)}) copy-start(bf16[1,3456,128]{2,1,0:T(8,128)(2,1)} %param.6) | copy-start | bytes 2654212
  3.2 9.4 %collective-permute-start = (bf16[28,32,128]{2,1,0:T(8,128)(2,1)S(1)}, bf16[28,32,128]{2,1,0:T(8,128)(2,1)S(1)}, u32[]{:S(2)}, u32[]{:S(2)}) collective-permute-start(bf16[28,32,128]{2,1,0:T(8,128)(2,1)S(1)} %get-tuple-element.30.refs_0_), channel_id=1, source_target_pairs={{0,8},{8,0},{16,24},{24,16},{1,9},{9,1},{17,25},{25,17},{2,10},{10... | collective-permute-start | bytes 688136 | tf_op jit(solution)/shard_map/ppermute | solution.py:35
  6.2 8.4 %collective-permute-start.7 = (bf16[27,32,128]{2,1,0:T(8,128)(2,1)S(1)}, bf16[27,32,128]{2,1,0:T(8,128)(2,1)S(1)}, u32[]{:S(2)}, u32[]{:S(2)}) collective-permute-start(bf16[27,32,128]{2,1,0:T(8,128)(2,1)S(1)} %get-tuple-element.32.refs_1_), channel_id=1, source_target_pairs={{0,16},{8,24},{16,0},{24,8},{1,17},{9,25},{17,1},{25,9},{2,18},{10... | collective-permute-start | bytes 663560 | tf_op jit(solution)/shard_map/ppermute | solution.py:35
  7.7 8.8 %collective-permute-start.3 = (bf16[27,32,128]{2,1,0:T(8,128)(2,1)S(1)}, bf16[27,32,128]{2,1,0:T(8,128)(2,1)S(1)}, u32[]{:S(2)}, u32[]{:S(2)}) collective-permute-start(bf16[27,32,128]{2,1,0:T(8,128)(2,1)S(1)} %get-tuple-element.32.refs_1_), channel_id=1, source_target_pairs={{0,8},{8,0},{16,24},{24,16},{1,9},{9,1},{17,25},{25,17},{2,10},{10... | collective-permute-start | bytes 663560 | tf_op jit(solution)/shard_map/ppermute | solution.py:35
  8.2 10.0 %collective-permute-start.2 = (bf16[27,32,128]{2,1,0:T(8,128)(2,1)S(1)}, bf16[27,32,128]{2,1,0:T(8,128)(2,1)S(1)}, u32[]{:S(2)}, u32[]{:S(2)}) collective-permute-start(bf16[27,32,128]{2,1,0:T(8,128)(2,1)S(1)} %get-tuple-element.32.refs_1_), channel_id=1, source_target_pairs={{0,1},{1,0},{2,3},{3,2},{4,5},{5,4},{6,7},{7,6},{8,9},{9,8},{10,11... | collective-permute-start | bytes 663560 | tf_op jit(solution)/shard_map/ppermute | solution.py:35
  8.2 11.2 %collective-permute-start.6 = (bf16[28,32,128]{2,1,0:T(8,128)(2,1)S(1)}, bf16[28,32,128]{2,1,0:T(8,128)(2,1)S(1)}, u32[]{:S(2)}, u32[]{:S(2)}) collective-permute-start(bf16[28,32,128]{2,1,0:T(8,128)(2,1)S(1)} %get-tuple-element.30.refs_0_), channel_id=1, source_target_pairs={{0,16},{8,24},{16,0},{24,8},{1,17},{9,25},{17,1},{25,9},{2,18},{10... | collective-permute-start | bytes 688136 | tf_op jit(solution)/shard_map/ppermute | solution.py:35
  12.6 6.8 %collective-permute-start.1 = (bf16[28,32,128]{2,1,0:T(8,128)(2,1)S(1)}, bf16[28,32,128]{2,1,0:T(8,128)(2,1)S(1)}, u32[]{:S(2)}, u32[]{:S(2)}) collective-permute-start(bf16[28,32,128]{2,1,0:T(8,128)(2,1)S(1)} %get-tuple-element.30.refs_0_), channel_id=1, source_target_pairs={{0,1},{1,0},{2,3},{3,2},{4,5},{5,4},{6,7},{7,6},{8,9},{9,8},{10,11... | collective-permute-start | bytes 688136 | tf_op jit(solution)/shard_map/ppermute | solution.py:35
  14.5 8.4 %collective-permute-start.10 = (bf16[28,32,128]{2,1,0:T(8,128)(2,1)S(1)}, bf16[28,32,128]{2,1,0:T(8,128)(2,1)S(1)}, u32[]{:S(2)}, u32[]{:S(2)}) collective-permute-start(bf16[28,32,128]{2,1,0:T(8,128)(2,1)S(1)} %collective-permute-done.refs_4_), channel_id=1, source_target_pairs={{0,16},{8,24},{16,0},{24,8},{1,17},{9,25},{17,1},{25,9},{2,18},{10... | collective-permute-start | bytes 688136 | tf_op jit(solution)/shard_map/ppermute | solution.py:35
  16.5 6.6 %collective-permute-start.11 = (bf16[27,32,128]{2,1,0:T(8,128)(2,1)S(1)}, bf16[27,32,128]{2,1,0:T(8,128)(2,1)S(1)}, u32[]{:S(2)}, u32[]{:S(2)}) collective-permute-start(bf16[27,32,128]{2,1,0:T(8,128)(2,1)S(1)} %collective-permute-done.7.refs_9_), channel_id=1, source_target_pairs={{0,8},{8,0},{16,24},{24,16},{1,9},{9,1},{17,25},{25,17},{2,10},{10... | collective-permute-start | bytes 663560 | tf_op jit(solution)/shard_map/ppermute | solution.py:35
  18.3 5.1 %collective-permute-start.9 = (bf16[27,32,128]{2,1,0:T(8,128)(2,1)S(1)}, bf16[27,32,128]{2,1,0:T(8,128)(2,1)S(1)}, u32[]{:S(2)}, u32[]{:S(2)}) collective-permute-start(bf16[27,32,128]{2,1,0:T(8,128)(2,1)S(1)} %collective-permute-done.7.refs_9_), channel_id=1, source_target_pairs={{0,1},{1,0},{2,3},{3,2},{4,5},{5,4},{6,7},{7,6},{8,9},{9,8},{10,11... | collective-permute-start | bytes 663560 | tf_op jit(solution)/shard_map/ppermute | solution.py:35
  19.5 5.3 %collective-permute-start.8 = (bf16[28,32,128]{2,1,0:T(8,128)(2,1)S(1)}, bf16[28,32,128]{2,1,0:T(8,128)(2,1)S(1)}, u32[]{:S(2)}, u32[]{:S(2)}) collective-permute-start(bf16[28,32,128]{2,1,0:T(8,128)(2,1)S(1)} %collective-permute-done.6.refs_8_), channel_id=1, source_target_pairs={{0,1},{1,0},{2,3},{3,2},{4,5},{5,4},{6,7},{7,6},{8,9},{9,8},{10,11... | collective-permute-start | bytes 688136 | tf_op jit(solution)/shard_map/ppermute | solution.py:35
  19.5 5.3 %collective-permute-start.4 = (bf16[28,32,128]{2,1,0:T(8,128)(2,1)S(1)}, bf16[28,32,128]{2,1,0:T(8,128)(2,1)S(1)}, u32[]{:S(2)}, u32[]{:S(2)}) collective-permute-start(bf16[28,32,128]{2,1,0:T(8,128)(2,1)S(1)} %collective-permute-done.refs_4_), channel_id=1, source_target_pairs={{0,1},{1,0},{2,3},{3,2},{4,5},{5,4},{6,7},{7,6},{8,9},{9,8},{10,11... | collective-permute-start | bytes 688136 | tf_op jit(solution)/shard_map/ppermute | solution.py:35
  22.9 2.1 %collective-permute-start.12 = (bf16[28,32,128]{2,1,0:T(8,128)(2,1)S(1)}, bf16[28,32,128]{2,1,0:T(8,128)(2,1)S(1)}, u32[]{:S(2)}, u32[]{:S(2)}) collective-permute-start(bf16[28,32,128]{2,1,0:T(8,128)(2,1)S(1)} %collective-permute-done.10.refs_12_), channel_id=1, source_target_pairs={{0,1},{1,0},{2,3},{3,2},{4,5},{5,4},{6,7},{7,6},{8,9},{9,8},{10,11... | collective-permute-start | bytes 688136 | tf_op jit(solution)/shard_map/ppermute | solution.py:35
  23.1 1.6 %collective-permute-start.5 = (bf16[27,32,128]{2,1,0:T(8,128)(2,1)S(1)}, bf16[27,32,128]{2,1,0:T(8,128)(2,1)S(1)}, u32[]{:S(2)}, u32[]{:S(2)}) collective-permute-start(bf16[27,32,128]{2,1,0:T(8,128)(2,1)S(1)} %collective-permute-done.3.refs_5_), channel_id=1, source_target_pairs={{0,1},{1,0},{2,3},{3,2},{4,5},{5,4},{6,7},{7,6},{8,9},{9,8},{10,11... | collective-permute-start | bytes 663560 | tf_op jit(solution)/shard_map/ppermute | solution.py:35
  23.4 1.6 %collective-permute-start.13 = (bf16[27,32,128]{2,1,0:T(8,128)(2,1)S(1)}, bf16[27,32,128]{2,1,0:T(8,128)(2,1)S(1)}, u32[]{:S(2)}, u32[]{:S(2)}) collective-permute-start(bf16[27,32,128]{2,1,0:T(8,128)(2,1)S(1)} %collective-permute-done.11.refs_13_), channel_id=1, source_target_pairs={{0,1},{1,0},{2,3},{3,2},{4,5},{5,4},{6,7},{7,6},{8,9},{9,8},{10,11... | collective-permute-start | bytes 663560 | tf_op jit(solution)/shard_map/ppermute | solution.py:35
  30.6 10.1 %collective-permute-start.14 = (bf16[384,128]{1,0:T(8,128)(2,1)S(1)}, bf16[384,128]{1,0:T(8,128)(2,1)S(1)}, u32[]{:S(2)}, u32[]{:S(2)}) collective-permute-start(bf16[384,128]{1,0:T(8,128)(2,1)S(1)} %get-tuple-element.35), channel_id=1, source_target_pairs={{0,8},{8,0},{16,24},{24,16},{1,9},{9,1},{17,25},{25,17},{2,10},{10... | collective-permute-start | bytes 294920 | tf_op jit(solution)/shard_map/ppermute | solution.py:35
  32.0 9.4 %collective-permute-start.15 = (bf16[384,128]{1,0:T(8,128)(2,1)S(1)}, bf16[384,128]{1,0:T(8,128)(2,1)S(1)}, u32[]{:S(2)}, u32[]{:S(2)}) collective-permute-start(bf16[384,128]{1,0:T(8,128)(2,1)S(1)} %get-tuple-element.36), channel_id=1, source_target_pairs={{0,16},{8,24},{16,0},{24,8},{1,17},{9,25},{17,1},{25,9},{2,18},{10... | collective-permute-start | bytes 294920 | tf_op jit(solution)/shard_map/ppermute | solution.py:35
  33.5 7.9 %collective-permute-start.16 = (bf16[384,128]{1,0:T(8,128)(2,1)S(1)}, bf16[384,128]{1,0:T(8,128)(2,1)S(1)}, u32[]{:S(2)}, u32[]{:S(2)}) collective-permute-start(bf16[384,128]{1,0:T(8,128)(2,1)S(1)} %get-tuple-element.37), channel_id=1, source_target_pairs={{0,24},{8,16},{16,8},{24,0},{1,25},{9,17},{17,9},{25,1},{2,26},{10... | collective-permute-start | bytes 294920 | tf_op jit(solution)/shard_map/ppermute | solution.py:35
  37.8 5.2 %collective-permute-start.17 = (bf16[384,128]{1,0:T(8,128)(2,1)S(1)}, bf16[384,128]{1,0:T(8,128)(2,1)S(1)}, u32[]{:S(2)}, u32[]{:S(2)}) collective-permute-start(bf16[384,128]{1,0:T(8,128)(2,1)S(1)} %get-tuple-element.44), channel_id=1, source_target_pairs={{0,8},{8,0},{16,24},{24,16},{1,9},{9,1},{17,25},{25,17},{2,10},{10... | collective-permute-start | bytes 294920 | tf_op jit(solution)/shard_map/ppermute | solution.py:35
  39.2 5.7 %collective-permute-start.18 = (bf16[384,128]{1,0:T(8,128)(2,1)S(1)}, bf16[384,128]{1,0:T(8,128)(2,1)S(1)}, u32[]{:S(2)}, u32[]{:S(2)}) collective-permute-start(bf16[384,128]{1,0:T(8,128)(2,1)S(1)} %get-tuple-element.45), channel_id=1, source_target_pairs={{0,16},{8,24},{16,0},{24,8},{1,17},{9,25},{17,1},{25,9},{2,18},{10... | collective-permute-start | bytes 294920 | tf_op jit(solution)/shard_map/ppermute | solution.py:35
  40.8 5.5 %collective-permute-start.19 = (bf16[384,128]{1,0:T(8,128)(2,1)S(1)}, bf16[384,128]{1,0:T(8,128)(2,1)S(1)}, u32[]{:S(2)}, u32[]{:S(2)}) collective-permute-start(bf16[384,128]{1,0:T(8,128)(2,1)S(1)} %get-tuple-element.46), channel_id=1, source_target_pairs={{0,24},{8,16},{16,8},{24,0},{1,25},{9,17},{17,9},{25,1},{2,26},{10... | collective-permute-start | bytes 294920 | tf_op jit(solution)/shard_map/ppermute | solution.py:35
  42.2 6.4 %copy-start.1 = (bf16[1,3456,128]{2,1,0:T(8,128)(2,1)S(1)}, bf16[1,3456,128]{2,1,0:T(8,128)(2,1)}, u32[]{:S(2)}) copy-start(bf16[1,3456,128]{2,1,0:T(8,128)(2,1)} %param.6) | copy-start | bytes 2654212
  48.6 2.2 %collective-permute-start.20 = (bf16[4,432,128]{2,1,0:T(8,128)(2,1)S(1)}, bf16[4,432,128]{2,1,0:T(8,128)(2,1)S(1)}, u32[]{:S(2)}, u32[]{:S(2)}) collective-permute-start(bf16[4,432,128]{2,1,0:T(8,128)(2,1)S(1)} %get-tuple-element.48), channel_id=1, source_target_pairs={{0,1},{1,0},{2,3},{3,2},{4,5},{5,4},{6,7},{7,6},{8,9},{9,8},{10,11... | collective-permute-start | bytes 1327112 | tf_op jit(solution)/shard_map/ppermute | solution.py:35
  51.4 11.0 %collective-permute-start.21 = (bf16[432,128]{1,0:T(8,128)(2,1)S(1)}, bf16[432,128]{1,0:T(8,128)(2,1)S(1)}, u32[]{:S(2)}, u32[]{:S(2)}) collective-permute-start(bf16[432,128]{1,0:T(8,128)(2,1)S(1)} %get-tuple-element.54), channel_id=1, source_target_pairs={{0,6},{1,7},{2,4},{3,5},{4,2},{5,3},{6,0},{7,1},{8,14},{9,15},{10,... | collective-permute-start | bytes 331784 | tf_op jit(solution)/shard_map/ppermute | solution.py:35
  55.1 10.0 %collective-permute-start.22 = (bf16[432,128]{1,0:T(8,128)(2,1)S(1)}, bf16[432,128]{1,0:T(8,128)(2,1)S(1)}, u32[]{:S(2)}, u32[]{:S(2)}) collective-permute-start(bf16[432,128]{1,0:T(8,128)(2,1)S(1)} %get-tuple-element.55), channel_id=1, source_target_pairs={{0,4},{1,5},{2,6},{3,7},{4,0},{5,1},{6,2},{7,3},{8,12},{9,13},{10,... | collective-permute-start | bytes 331784 | tf_op jit(solution)/shard_map/ppermute | solution.py:35
  55.1 10.0 %collective-permute-start.23 = (bf16[432,128]{1,0:T(8,128)(2,1)S(1)}, bf16[432,128]{1,0:T(8,128)(2,1)S(1)}, u32[]{:S(2)}, u32[]{:S(2)}) collective-permute-start(bf16[432,128]{1,0:T(8,128)(2,1)S(1)} %get-tuple-element.56), channel_id=1, source_target_pairs={{0,2},{1,3},{2,0},{3,1},{4,6},{5,7},{6,4},{7,5},{8,10},{9,11},{10,... | collective-permute-start | bytes 331784 | tf_op jit(solution)/shard_map/ppermute | solution.py:35

commit v3 on v2

--- a/solution.py
+++ b/solution.py
@@ -198,12 +198,12 @@
 def forward_kernel(sections, dims, ids, x_ref, gain, *refs):
     frames, rows, cols, chans = dims
     plane = rows * cols
-    n_chunk = (len(refs) - 8 - sections) // sections
+    n_chunk = (len(refs) - 9 - sections) // sections
     chunks = [refs[k * n_chunk : (k + 1) * n_chunk] for k in range(sections)]
     refs = refs[sections * n_chunk :]
     outs, stats, every = refs[:3]
     sends = refs[3 : 3 + sections]
-    spread, product, gain_rows, gain_sem, sems = refs[3 + sections :]
+    spread, product, inputs, gain_rows, gain_sem, sems = refs[3 + sections :]
     place = ids[0]
     taps = every.shape[1]
     copies = [
@@ -213,13 +213,9 @@
     for copy in copies:
         copy.start()
 
-    def start(slot, k):
-        for copy in copies_of(chunks[k], piece_ids(ids, n_chunk), every.at[slot], sems.at[slot]):
+    for k in range(sections):
+        for copy in copies_of(chunks[k], piece_ids(ids, n_chunk), every.at[k], sems.at[k]):
             copy.start()
-
-    for slot in range(sections):
-        for k in range(sections):
-            pl.when((place ^ k) == slot)(functools.partial(start, slot, k))
     stats[place, 16:24] = full(gain[...], 8)
     for k in range(1, sections):
         copies[k - 1].wait()
@@ -227,23 +223,22 @@
         stats[place ^ k, 16:24] = full(parts[0:1] + parts[1:2] + parts[2:3], 8)
     x = x_ref[...]
     for unit in range(sections):
-        for k in range(sections):
-            @pl.when((place ^ k) == unit)
-            def _(k=k, x=x):
-                sends[k][...] = x
-
+        inputs[unit] = x
         x32 = x.astype(F32)
         mean, rstd = statistics(x32, chans // GROUPS)
         stats[unit, 0:8], stats[unit, 8:16] = mean, rstd
         spread_forward(dims, [x32], [(mean, rstd)], stats[unit, 16:17], spread)
-        pltpu.make_async_copy(every.at[unit], every.at[unit], sems.at[unit]).wait()
+        source = place ^ unit
+        pltpu.make_async_copy(every.at[source], every.at[source], sems.at[source]).wait()
         lhs = spread[...].reshape(frames * plane, 9 * chans)
-        product[...] = jnp.dot(lhs, forward_matrix(every[unit]), preferred_element_type=F32)
+        product[...] = jnp.dot(lhs, forward_matrix(every[source]), preferred_element_type=F32)
         for f in range(frames):
             spot = slice(f * plane, (f + 1) * plane)
             joined = join_cols(product[spot], cols, chans, (-1, 0, 1))
             outs[unit, spot] = (x32[spot] + joined).astype(BF)
         x = outs[unit]
+    for k in range(sections):
+        sends[k][...] = inputs[place ^ k]
 
 
 def turn_kernel(dims, n, gain, *refs):
@@ -259,7 +254,7 @@
         for f in range(frames):
             frame = act[f * plane : (f + 1) * plane]
             for at, step in enumerate((-1, 0, 1)):
-                piece = frame if step == 0 else row_shift(frame, cols, step)
+                piece = frame if step == 0 else side(frame, cols, step)
                 turned[at * chans : (at + 1) * chans, pl.ds((f * n + k) * plane, plane)] = piece.T.astype(BF)
 
 
@@ -314,23 +309,19 @@
 
 
 def backward_kernel(sections, dims, ids, outs, grad_ref, stats, every, *refs):
-    sends, spread = refs[:sections], refs[sections]
+    sends, (spread, grads) = refs[:sections], refs[sections:]
     place = ids[0]
     grad = grad_ref[...]
+    grads[sections - 1] = grad
+    for unit in range(sections - 1, 0, -1):
+
+        def multiply(lhs, unit=unit):
+            return times_transposed(lhs, every[place ^ unit])
+
+        grad = unit_backward(dims, outs[unit - 1].astype(F32), grad, stats[unit], stats[unit, 16:17], multiply, spread)
+        grads[unit - 1] = grad
     for k in range(sections):
-        @pl.when((place ^ k) == sections - 1)
-        def _(k=k, grad=grad):
-            sends[k][...] = grad
-    for unit in range(sections - 1, 0, -1):
-
-        def multiply(lhs, unit=unit):
-            return times_transposed(lhs, every[unit])
-
-        grad = unit_backward(dims, outs[unit - 1].astype(F32), grad, stats[unit], stats[unit, 16:17], multiply, spread)
-        for k in range(sections):
-            @pl.when((place ^ k) == unit - 1)
-            def _(k=k, grad=grad):
-                sends[k][...] = grad
+        sends[k][...] = grads[place ^ k]
 
 
 def home_backward_kernel(dims, n, first, last, ids, stats, gain, own, *refs):
@@ -358,56 +349,82 @@
             outs[i][...] = result
 
 
-def term_kernel(dims, n, shares, ids, turned, *refs):
+def tap_spots(frames, n, plane):
+    spots = [0]
+    for a in range(3):
+        spots.append(spots[-1] + max(1, frames - 2 + a) * n * plane)
+    return spots
+
+
+def put_right(dims, n, grads, right):
     frames, rows, cols, chans = dims
     plane = rows * cols
-    grads = refs[:n]
-    rest = refs[n:]
-    term = rest[-1] if shares else rest[0]
-    right = rest[-2] if shares else rest[1]
-    spots = [0]
-    for a in range(3):
-        spots.append(spots[-1] + max(1, min(frames, frames - 2 + a)))
+    spots = tap_spots(frames, n, plane)
     for k in range(n):
         mine = grads[k][...].astype(F32)
         per = [mine[f * plane : (f + 1) * plane] for f in range(frames)]
-        sides = [[side(p, cols, 1), p, side(p, cols, -1)] for p in per]
         for a in range(3):
             folded = [f for f in range(frames) if f - 2 + a <= 0]
             groups = [folded] + [[f] for f in range(frames) if f - 2 + a > 0]
             for i, group in enumerate(groups):
-                for c in range(3):
-                    piece = functools.reduce(lambda u, v: u + v, [sides[f][c] for f in group])
-                    right[pl.ds(((spots[a] + i) * n + k) * plane, plane), c * chans : (c + 1) * chans] = piece.astype(BF)
+                total = functools.reduce(lambda u, v: u + v, [per[f] for f in group])
+                at = spots[a] + (i * n + k) * plane
+                for b, piece in enumerate(three_rows(total, cols, (1, 0, -1))):
+                    right[at : at + plane, b * chans : (b + 1) * chans] = piece
+
+
+def put_term(dims, n, a, taps, turned, right, term, base):
+    frames, rows, cols, chans = dims
+    spots = tap_spots(frames, n, rows * cols)
+    used = spots[a + 1] - spots[a]
+    rhs = right[spots[a] : spots[a + 1], taps[0] * chans : (taps[-1] + 1) * chans]
+    out = jnp.dot(turned[:, 0:used], rhs, preferred_element_type=F32)
+    for b in range(len(taps)):
+        for c in range(3):
+            block = out[c * chans : (c + 1) * chans, b * chans : (b + 1) * chans]
+            term[pl.ds(base + (b * 3 + c) * chans, chans), :] = block.astype(BF)
+
+
+def term_kernel(dims, n, turned, *refs):
+    grads, (term, right) = refs[:n], refs[n:]
+    put_right(dims, n, grads, right)
     for a in range(3):
-        used = (spots[a + 1] - spots[a]) * n * plane
-        lhs = turned[:, 0:used]
-        rhs = right[pl.ds(spots[a] * n * plane, used), :]
-        out = jnp.dot(lhs, rhs, preferred_element_type=F32)
-        for b in range(3):
-            for c in range(3):
-                block = out[b * chans : (b + 1) * chans, c * chans : (c + 1) * chans]
-                term[pl.ds(((a * 3 + b) * 3 + c) * chans, chans), :] = block.astype(BF)
-    if shares:
-        keep, send = rest[0], rest[1]
-        core = ids[1]
-        size = keep.shape[1]
-        for j in range(shares // 2):
-            here = pl.multiple_of((2 * j + core) * size, size)
-            there = pl.multiple_of((2 * j + 1 - core) * size, size)
-            keep[j] = term[pl.ds(here, size), :]
-            send[j] = term[pl.ds(there, size), :]
-
-
-def pair_kernel(count, ids, keep, got, own, *sends):
-    level = ids[2]
-    for k in range(count):
-        at = level ^ k
-        total = keep[at].astype(F32) + got[at].astype(F32)
-        if k == 0:
-            own[...] = total
-        else:
-            sends[k - 1][...] = total.astype(BF)
+        put_term(dims, n, a, (0, 1, 2), turned, right, term, a * 9 * dims[3])
+
+
+def half_kernel(dims, n, far, levels, ids, turned, *refs):
+    chans = dims[3]
+    if far:
+        put_right(dims, n, refs[:n], refs[n])
+        refs = refs[n:]
+    right, keep, send, term = refs
+    upper = ids[2] >= levels // 2
+
+    def low():
+        put_term(dims, n, 0, (0, 1, 2), turned, right, term, 0)
+        put_term(dims, n, 1, (0, 1), turned, right, term, 9 * chans)
+
+    def high():
+        put_term(dims, n, 1, (1, 2), turned, right, term, 0)
+        put_term(dims, n, 2, (0, 1, 2), turned, right, term, 6 * chans)
+
+    wants_high = jnp.logical_not(upper) if far else upper
+    pl.when(wants_high)(high)
+    pl.when(jnp.logical_not(wants_high))(low)
+    skip = jnp.where(wants_high, 27 * chans // 2 - 12 * chans, 0)
+    core = ids[1]
+    size = keep.shape[1]
+    for j in range(levels // 2):
+        here = pl.multiple_of(skip + (2 * j + core) * size, 16)
+        there = pl.multiple_of(skip + (2 * j + 1 - core) * size, 16)
+        keep[j] = term[pl.ds(here, size), :]
+        send[j] = term[pl.ds(there, size), :]
+
+
+def pair_kernel(distances, ids, keep, got, *sends):
+    for k, out in zip(distances, sends):
+        at = lax.rem(ids[2] ^ k, keep.shape[0])
+        out[...] = (keep[at].astype(F32) + got[at].astype(F32)).astype(out.dtype)
 
 
 def sum_kernel(scale, own, *refs):
@@ -487,6 +504,7 @@
         [
             spread(1),
             product,
+            pltpu.VMEM((sections, points, chans), BF),
             pltpu.VMEM((sections - 1, quarter, chans), BF),
             pltpu.SemaphoreType.DMA((sections - 1,)),
             pltpu.SemaphoreType.DMA((sections,)),
@@ -500,7 +518,7 @@
         [act_shape] * sections,
         [SM] + [VM] * 4,
         [VM] * sections,
-        [spread(1)],
+        [spread(1), pltpu.VMEM((sections, points, chans), BF)],
         flops=4 * (sections - 1) * unit_flops,
     )(ids, outs, grad, stats, every)
     grads_home = [gsends[0]] + [swap(gsends[k], "pipe", k) for k in range(1, n)]
@@ -534,41 +552,65 @@
             flops=4 * count * unit_flops,
         )(ids, home_stats, gain_rows, kernel_rows, *xs_home[first:last], *grads_home[first:last], *done)
 
+    seg = home_forward(ids)
+    turned, seg = lax.optimization_barrier((turned, seg))
+
     size = 27 * chans // ranks
-    right = pltpu.VMEM((spots * n * rows * cols, 3 * chans), BF)
-    half = jax.ShapeDtypeStruct((ranks // 2, size, chans), BF)
     levels = ranks // 2
-    if size % 16 == 0:
-        keep, send = call(
-            functools.partial(term_kernel, dims, n, ranks),
-            [half, half],
+    right_shape = jax.ShapeDtypeStruct((tap_spots(frames, n, rows * cols)[-1], 3 * chans), BF)
+
+    def pair(keep, got, distances):
+        return call(
+            functools.partial(pair_kernel, distances),
+            [jax.ShapeDtypeStruct((size, chans), BF if k else F32) for k in distances],
+            [SM, VM, VM],
+            [VM] * len(distances),
+        )(ids, keep, got)
+
+    if size % 16 == 0 and levels % 2 == 0:
+        half = [jax.ShapeDtypeStruct((levels // 2, size, chans), BF)] * 2
+        term = pltpu.VMEM((15 * chans, chans), BF)
+        right, keep, send = call(
+            functools.partial(half_kernel, dims, n, True, levels),
+            [right_shape] + half,
             [SM, VM] + [VM] * n,
-            [VM, VM],
-            [right, pltpu.VMEM((27 * chans, chans), BF)],
-            flops=n * unit_flops,
+            [VM] * 3,
+            [term],
+            flops=n * unit_flops // 2,
         )(ids, turned, *grads_home)
+        got = swap(send, "dp", 1)
+        near_keep, near_send = call(
+            functools.partial(half_kernel, dims, n, False, levels),
+            half,
+            [SM, VM, VM],
+            [VM] * 2,
+            [term],
+            flops=n * unit_flops // 2,
+        )(ids, turned, right)
+        near_send, got = lax.optimization_barrier((near_send, got))
+        near_got = swap(near_send, "dp", 1)
+        far = range(levels // 2, levels)
+        zsends = dict(zip(far, pair(keep, got, far)))
+        near = range(levels // 2)
+        zsends.update(zip(near, pair(near_keep, near_got, near)))
     else:
         term = call(
-            functools.partial(term_kernel, dims, n, 0),
+            functools.partial(term_kernel, dims, n),
             jax.ShapeDtypeStruct((27 * chans, chans), BF),
-            [SM, VM] + [VM] * n,
+            [VM] * (1 + n),
             VM,
-            [right],
+            [pltpu.VMEM(right_shape.shape, BF)],
             flops=n * unit_flops,
-        )(ids, turned, *grads_home)
+        )(turned, *grads_home)
         shares = term.reshape(levels, 2, size, chans)
         keep = lax.dynamic_index_in_dim(shares, core, 1, False)
-        send = lax.dynamic_index_in_dim(shares, 1 - core, 1, False)
-    got = swap(send, "dp", 1)
-    early = home_backward(0, n // 2, (), ids)
-    piece = jax.ShapeDtypeStruct((size, chans), BF)
-    own, *zsends = call(
-        functools.partial(pair_kernel, levels),
-        [jax.ShapeDtypeStruct((size, chans), F32)] + [piece] * (levels - 1),
-        [SM, VM, VM],
-        [VM] * levels,
-    )(ids, keep, got)
-    arrived = [swap(zsends[k - 1], "dp", 2 * k) for k in range(levels - 1, 0, -1)]
+        got = swap(lax.dynamic_index_in_dim(shares, 1 - core, 1, False), "dp", 1)
+        zsends = dict(enumerate(pair(keep, got, range(levels))))
+    own = zsends[0]
+    arrived = [swap(zsends[k], "dp", 2 * k) for k in (*range(levels // 2, levels), *range(1, levels // 2))]
+
+    late, own = lax.optimization_barrier((ids, own))
+    (ing,) = home_backward(0, n, (), late)
 
     scale = 1.0 / math.sqrt(micro * clips * ranks * points)
     share = call(
@@ -578,9 +620,6 @@
         VM,
     )(own, *arrived)
 
-    late, _ = lax.optimization_barrier((ids, own))
-    (ing,) = home_backward(n // 2, n, early, late)
-    seg = home_forward(late)
     shape = (1, micro, clips, frames, rows, cols, chans)
     return (seg.reshape(shape), ing.reshape(shape), share.reshape(1, size * chans))
 

time: 66 us -> 64.1 us (0.971)
  waiting for transfers between devices: 18.2 us -> 15.5 us
    ppermute x24 -> x25, waiting for transfers between devices: 18.2 us -> 15.5 us  [swap(): return lax.ppermute(value, axis, [(i, i ^ bits) for i in range(count)])]
    pallas_call x2 -> x4, Pallas kernels: 2.92 us -> 4.37 us  [the longest x1 1.83 us: body(): call(functools.partial(half_kernel, dims, n, True, levels), [right_shape]...]
    pallas_call x2 -> x1, Pallas kernels: 4.92 us -> 3.96 us  [home_backward(): call(functools.partial(home_backward_kernel, dims, n, first, last), [jax....]
    ppermute x24 -> x25, starting transfers between devices: 21 us -> 21.4 us  [swap(): return lax.ppermute(value, axis, [(i, i ^ bits) for i in range(count)])]
  transfers between devices with their start and end apart: 24 -> 25, of which waited for: 12 -> 11; matrix products, arithmetic and copies ran while one was open for 1% -> 1% of each run, Pallas kernels for 20% -> 23%
where the time goes in v3:
time: 64.1 us; the launch traced here: 63.8 us
  Pallas kernels  23.1 us (36%)
  starting transfers between devices  21.4 us (33%)
  waiting for transfers between devices  15.5 us (24%)
  local copies, waits for them, and re-layouts  3.06 us (5%)
  between operations  0.74 us (1%)
    ppermute x25, starting transfers between devices, swap(): return lax.ppermute(value, axis, [(i, i ^ bits) for i in range(count)])  21.4 us
    ppermute x25, waiting for transfers between devices, swap(): return lax.ppermute(value, axis, [(i, i ^ bits) for i in range(count)])  15.5 us
    pallas_call x1, Pallas kernels, body(): call(functools.partial(forward_kernel, sections, dims), [jax.ShapeDtypeSt...  5.41 us
    pallas_call x1, Pallas kernels, home_backward(): call(functools.partial(home_backward_kernel, dims, n, first, last), [jax....  3.96 us
    pallas_call x1, Pallas kernels, home_forward(): call(functools.partial(home_forward_kernel, dims, n), jax.ShapeDtypeStruc...  3.69 us
    pallas_call x1, Pallas kernels, body(): call(functools.partial(backward_kernel, sections, dims), [act_shape] * se...  3.43 us
    pallas_call x1, Pallas kernels, body(): call(functools.partial(half_kernel, dims, n, True, levels), [right_shape]...  1.83 us
    unnamed x4, local copies, waits for them, and re-layouts  1.45 us
  transfers between devices with their start and end apart: 25, of which 11 were waited for; matrix products, arithmetic and copies ran while one was open for 1% of the time, Pallas kernels for 23%

profile of v3, /device:TPU:0, one launch (start us, length us, event | category | flops | bytes accessed | tf_op | source)
XLA Modules:
  0.0 63.8 jit_solution(2617149794939499304)
XLA Ops:
  0.6 0.1 pad_add_fusion.ids
  0.7 0.7 %broadcast_in_dim.8.gain = f32[8,128]{1,0:T(8,128)S(1)} broadcast(f32[128]{0:T(128)} %bitcast.24), dimensions={1} | broadcast | bytes 4608 | tf_op jit(solution)/shard_map/broadcast_in_dim | solution.py:470
  1.4 1.2 %copy-done = bf16[1,3456,128]{2,1,0:T(8,128)(2,1)S(1)} copy-done((bf16[1,3456,128]{2,1,0:T(8,128)(2,1)S(1)}, bf16[1,3456,128]{2,1,0:T(8,128)(2,1)}, u32[]{:S(2)}) %copy-start) | copy-done | bytes 884760
  2.5 0.6 %shard_map.67 = (bf16[28,32,128]{2,1,0:T(8,128)(2,1)S(1)}, bf16[27,32,128]{2,1,0:T(8,128)(2,1)S(1)}) custom-call(s32[3]{0:T(128)S(1)} %pad_add_fusion.ids, f32[8,128]{1,0:T(8,128)S(1)} %broadcast_in_dim.8.gain, bf16[27,128,128]{2,1,0:T(8,128)(2,1)S(1)} %bitcast.18), custom_call_target="tpu_custom_call" | custom-call | tf_op jit(solution)/shard_map/pallas_call | solution.py:471
  3.2 3.0 %collective-permute-start = (bf16[28,32,128]{2,1,0:T(8,128)(2,1)S(1)}, bf16[28,32,128]{2,1,0:T(8,128)(2,1)S(1)}, u32[]{:S(2)}, u32[]{:S(2)}) collective-permute-start(bf16[28,32,128]{2,1,0:T(8,128)(2,1)S(1)} %get-tuple-element.36.refs_0_), channel_id=1, source_target_pairs={{0,8},{8,0},{16,24},{24,16},{1,9},{9,1},{17,25},{25,17},{2,10},{10... | collective-permute-start | bytes 688136 | tf_op jit(solution)/shard_map/ppermute | solution.py:35
  6.2 1.5 %collective-permute-start.7 = (bf16[27,32,128]{2,1,0:T(8,128)(2,1)S(1)}, bf16[27,32,128]{2,1,0:T(8,128)(2,1)S(1)}, u32[]{:S(2)}, u32[]{:S(2)}) collective-permute-start(bf16[27,32,128]{2,1,0:T(8,128)(2,1)S(1)} %get-tuple-element.38.refs_1_), channel_id=1, source_target_pairs={{0,16},{8,24},{16,0},{24,8},{1,17},{9,25},{17,1},{25,9},{2,18},{10... | collective-permute-start | bytes 663560 | tf_op jit(solution)/shard_map/ppermute | solution.py:35
  7.7 0.5 collective-permute-start.3
  8.2 0.0 collective-permute-start.2
  8.2 0.1 collective-permute-start.6
  8.3 1.0 %dynamic-slice_bitcast_fusion = (bf16[384,128]{1,0:T(8,128)(2,1)S(1)}, bf16[384,128]{1,0:T(8,128)(2,1)S(1)}) fusion(bf16[4,384,128]{2,1,0:T(8,128)(2,1)} %bitcast.22, s32[]{:T(128)S(6)} %select_n.5, bf16[4,384,128]{2,1,0:T(8,128)(2,1)} %bitcast.23), kind=kLoop, calls=%fused_computation | loop fusion | bytes 393220 | tf_op jit(solution)/shard_map/jit(dynamic_index_in_dim)/squeeze | solution.py:479
  9.3 3.4 %collective-permute-done.refs_4_ = bf16[28,32,128]{2,1,0:T(8,128)(2,1)S(1)} collective-permute-done((bf16[28,32,128]{2,1,0:T(8,128)(2,1)S(1)}, bf16[28,32,128]{2,1,0:T(8,128)(2,1)S(1)}, u32[]{:S(2)}, u32[]{:S(2)}) %collective-permute-start) | collective-permute-done | bytes 229408 | tf_op jit(solution)/shard_map/ppermute | solution.py:35
  12.6 0.0 collective-permute-start.1
  12.6 1.9 %collective-permute-done.7.refs_9_ = bf16[27,32,128]{2,1,0:T(8,128)(2,1)S(1)} collective-permute-done((bf16[27,32,128]{2,1,0:T(8,128)(2,1)S(1)}, bf16[27,32,128]{2,1,0:T(8,128)(2,1)S(1)}, u32[]{:S(2)}, u32[]{:S(2)}) %collective-permute-start.7) | collective-permute-done | bytes 221216 | tf_op jit(solution)/shard_map/ppermute | solution.py:35
  14.5 1.5 %collective-permute-start.10 = (bf16[28,32,128]{2,1,0:T(8,128)(2,1)S(1)}, bf16[28,32,128]{2,1,0:T(8,128)(2,1)S(1)}, u32[]{:S(2)}, u32[]{:S(2)}) collective-permute-start(bf16[28,32,128]{2,1,0:T(8,128)(2,1)S(1)} %collective-permute-done.refs_4_), channel_id=1, source_target_pairs={{0,16},{8,24},{16,0},{24,8},{1,17},{9,25},{17,1},{25,9},{2,18},{10... | collective-permute-start | bytes 688136 | tf_op jit(solution)/shard_map/ppermute | solution.py:35
  16.1 0.5 collective-permute-done.3.refs_5_
  16.5 1.7 %collective-permute-start.11 = (bf16[27,32,128]{2,1,0:T(8,128)(2,1)S(1)}, bf16[27,32,128]{2,1,0:T(8,128)(2,1)S(1)}, u32[]{:S(2)}, u32[]{:S(2)}) collective-permute-start(bf16[27,32,128]{2,1,0:T(8,128)(2,1)S(1)} %collective-permute-done.7.refs_9_), channel_id=1, source_target_pairs={{0,8},{8,0},{16,24},{24,16},{1,9},{9,1},{17,25},{25,17},{2,10},{10... | collective-permute-start | bytes 663560 | tf_op jit(solution)/shard_map/ppermute | solution.py:35
  18.3 0.0 collective-permute-done.2.refs_3_
  18.3 0.0 collective-permute-start.9
  18.3 1.2 %collective-permute-done.6.refs_8_ = bf16[28,32,128]{2,1,0:T(8,128)(2,1)S(1)} collective-permute-done((bf16[28,32,128]{2,1,0:T(8,128)(2,1)S(1)}, bf16[28,32,128]{2,1,0:T(8,128)(2,1)S(1)}, u32[]{:S(2)}, u32[]{:S(2)}) %collective-permute-start.6) | collective-permute-done | bytes 229408 | tf_op jit(solution)/shard_map/ppermute | solution.py:35
  19.5 0.0 collective-permute-start.8
  19.5 0.0 collective-permute-done.1.refs_2_
  19.5 0.5 collective-permute-start.4
  20.0 2.9 %collective-permute-done.10.refs_12_ = bf16[28,32,128]{2,1,0:T(8,128)(2,1)S(1)} collective-permute-done((bf16[28,32,128]{2,1,0:T(8,128)(2,1)S(1)}, bf16[28,32,128]{2,1,0:T(8,128)(2,1)S(1)}, u32[]{:S(2)}, u32[]{:S(2)}) %collective-permute-start.10) | collective-permute-done | bytes 229408 | tf_op jit(solution)/shard_map/ppermute | solution.py:35
  22.9 0.0 collective-permute-start.12
  22.9 0.2 collective-permute-done.11.refs_13_
  23.1 0.3 collective-permute-start.5
  23.4 0.0 collective-permute-done.9.refs_11_
  23.4 0.2 collective-permute-start.13
  23.7 1.1 %collective-permute-done.5.refs_7_ = bf16[27,32,128]{2,1,0:T(8,128)(2,1)S(1)} collective-permute-done((bf16[27,32,128]{2,1,0:T(8,128)(2,1)S(1)}, bf16[27,32,128]{2,1,0:T(8,128)(2,1)S(1)}, u32[]{:S(2)}, u32[]{:S(2)}) %collective-permute-start.5) | collective-permute-done | bytes 221216 | tf_op jit(solution)/shard_map/ppermute | solution.py:35
  24.7 0.0 collective-permute-done.8.refs_10_
  24.7 0.3 collective-permute-done.13.refs_15_
  25.0 5.4 %shard_map.68 = (bf16[4,384,128]{2,1,0:T(8,128)(2,1)S(1)}, f32[4,24,128]{2,1,0:T(8,128)S(1)}, bf16[4,27,128,128]{3,2,1,0:T(8,128)(2,1)S(1)}, bf16[384,128]{1,0:T...) custom-call(s32[3]{0:T(128)S(1)} %pad_add_fusion.ids, ...), custom_call_target="tpu_custom_call" | custom-call | flops 5435817984 | tf_op jit(solution)/shard_map/pallas_call | solution.py:494
  30.4 1.4 %collective-permute-start.14 = (bf16[384,128]{1,0:T(8,128)(2,1)S(1)}, bf16[384,128]{1,0:T(8,128)(2,1)S(1)}, u32[]{:S(2)}, u32[]{:S(2)}) collective-permute-start(bf16[384,128]{1,0:T(8,128)(2,1)S(1)} %get-tuple-element.41), channel_id=1, source_target_pairs={{0,8},{8,0},{16,24},{24,16},{1,9},{9,1},{17,25},{25,17},{2,10},{10... | collective-permute-start | bytes 294920 | tf_op jit(solution)/shard_map/ppermute | solution.py:35
  31.8 1.5 %collective-permute-start.15 = (bf16[384,128]{1,0:T(8,128)(2,1)S(1)}, bf16[384,128]{1,0:T(8,128)(2,1)S(1)}, u32[]{:S(2)}, u32[]{:S(2)}) collective-permute-start(bf16[384,128]{1,0:T(8,128)(2,1)S(1)} %get-tuple-element.42), channel_id=1, source_target_pairs={{0,16},{8,24},{16,0},{24,8},{1,17},{9,25},{17,1},{25,9},{2,18},{10... | collective-permute-start | bytes 294920 | tf_op jit(solution)/shard_map/ppermute | solution.py:35
  33.4 0.6 collective-permute-start.16
  34.0 3.4 %shard_map.71 = (bf16[384,128]{1,0:T(8,128)(2,1)S(1)}, bf16[384,128]{1,0:T(8,128)(2,1)S(1)}, bf16[384,128]{1,0:T(8,128)(2,1)S(1)}, bf16[384,128]{1,0:T(8,128)(2,1)S(1)}) custom-call(s32[3]{0:T(128)S(1)} %pad_add_fusion.ids, bf16[4,384,128]{2,1,0:T(8,128)(2,1)S(1)} %get-tuple-element.48.outs, bf16[384,128]{1,0:T(8,128)(2,1)S(1)} %get-tuple-element.49.grad_ref, ...), custom_call_target="tpu_custom_call" | custom-call | flops 4076863488 | tf_op jit(solution)/shard_map/pallas_call | solution.py:516
  37.4 1.4 %collective-permute-start.17 = (bf16[384,128]{1,0:T(8,128)(2,1)S(1)}, bf16[384,128]{1,0:T(8,128)(2,1)S(1)}, u32[]{:S(2)}, u32[]{:S(2)}) collective-permute-start(bf16[384,128]{1,0:T(8,128)(2,1)S(1)} %get-tuple-element.53), channel_id=1, source_target_pairs={{0,8},{8,0},{16,24},{24,16},{1,9},{9,1},{17,25},{25,17},{2,10},{10... | collective-permute-start | bytes 294920 | tf_op jit(solution)/shard_map/ppermute | solution.py:35
  38.8 1.5 %collective-permute-start.18 = (bf16[384,128]{1,0:T(8,128)(2,1)S(1)}, bf16[384,128]{1,0:T(8,128)(2,1)S(1)}, u32[]{:S(2)}, u32[]{:S(2)}) collective-permute-start(bf16[384,128]{1,0:T(8,128)(2,1)S(1)} %get-tuple-element.54), channel_id=1, source_target_pairs={{0,16},{8,24},{16,0},{24,8},{1,17},{9,25},{17,1},{25,9},{2,18},{10... | collective-permute-start | bytes 294920 | tf_op jit(solution)/shard_map/ppermute | solution.py:35
  40.4 0.0 collective-permute-done.14.refs_1_
  40.4 0.6 collective-permute-start.19
  41.0 0.0 collective-permute-done.15.refs_2_
  41.0 0.0 collective-permute-done.16.refs_3_
  41.0 0.9 %shard_map.69 = (bf16[384,1536]{1,0:T(8,128)(2,1)S(1)}, f32[4,16,128]{2,1,0:T(8,128)S(1)}) custom-call(f32[8,128]{1,0:T(8,128)S(1)} %broadcast_in_dim.8.gain, bf16[384,128]{1,0:T(8,128)(2,1)S(1)} %get-tuple-element.40.refs_0_, bf16[384,128]{1,0:T(8,128)(2,1)S(1)} %collective-permute-done.14.refs_1_, bf16[384,128]{1,0:T(8,128)(2,1)S(1)} %collective-permute-done.15.refs_2_, ...), custom_call_target="tpu_custom_call" | custom-call | flops 1358954496 | tf_op jit(solution)/shard_map/pallas_call | solution.py:526
  41.9 0.3 copy-done.1
  42.2 3.7 %shard_map.70 = bf16[4,384,128]{2,1,0:T(8,128)(2,1)} custom-call(s32[3]{0:T(128)S(1)} %pad_add_fusion.ids, f32[4,16,128]{2,1,0:T(8,128)S(1)} %get-tuple-element.45.stats, f32[8,128]{1,0:T(8,128)S(1)} %broadcast_in_dim.8.gain, bf16[27,128,128]{2,1,0:T(8,128)(2,1)S(1)} %bitcast.19, bf16[384,128]{1,0:T(8,128)(2,1)S(1)} %get-tuple-element.40.refs_0_, ...), custom_call_target="tpu_custom_call" | custom-call | flops 5435817984 | tf_op jit(solution)/shard_map/pallas_call | solution.py:535
  45.9 0.0 collective-permute-done.17.refs_1_.refs_5_
  45.9 0.0 collective-permute-done.18.refs_2_.refs_6_
  45.9 0.0 collective-permute-done.19.refs_3_.refs_7_
  45.9 1.8 %shard_map.72 = (bf16[3072,384]{1,0:T(8,128)(2,1)S(1)}, bf16[2,432,128]{2,1,0:T(8,128)(2,1)S(1)}, bf16[2,432,128]{2,1,0:T(8,128)(2,1)S(1)}) custom-call(s32[3]{0:T(128)S(1)} %pad_add_fusion.ids, bf16[384,1536]{1,0:T(8,128)(2,1)S(1)} %get-tuple-element.47.turned, bf16[384,128]{1,0:T(8,128)(2,1)S(1)} %get-tuple-element.52.refs_0_.refs_4_, ...), custom_call_target="tpu_custom_call" | custom-call | flops 679477248 | tf_op jit(solution)/shard_map/pallas_call | solution.py:573
  47.7 0.1 collective-permute-start.20
  47.8 1.3 %shard_map.73 = (bf16[2,432,128]{2,1,0:T(8,128)(2,1)S(1)}, bf16[2,432,128]{2,1,0:T(8,128)(2,1)S(1)}) custom-call(s32[3]{0:T(128)S(1)} %pad_add_fusion.ids, bf16[384,1536]{1,0:T(8,128)(2,1)S(1)} %get-tuple-element.47.turned, bf16[3072,384]{1,0:T(8,128)(2,1)S(1)} %get-tuple-element.56.refs_0_), custom_call_target="tpu_custom_call" | custom-call | flops 679477248 | tf_op jit(solution)/shard_map/pallas_call | solution.py:582
  49.1 0.1 collective-permute-done.20.got
  49.3 0.5 collective-permute-start.21
  49.7 0.6 shard_map.76
  50.3 2.7 %collective-permute-start.22 = (bf16[432,128]{1,0:T(8,128)(2,1)S(1)}, bf16[432,128]{1,0:T(8,128)(2,1)S(1)}, u32[]{:S(2)}, u32[]{:S(2)}) collective-permute-start(bf16[432,128]{1,0:T(8,128)(2,1)S(1)} %get-tuple-element.66), channel_id=1, source_target_pairs={{0,4},{1,5},{2,6},{3,7},{4,0},{5,1},{6,2},{7,3},{8,12},{9,13},{10,... | collective-permute-start | bytes 331784 | tf_op jit(solution)/shard_map/ppermute | solution.py:35
  53.0 1.3 %collective-permute-start.23 = (bf16[432,128]{1,0:T(8,128)(2,1)S(1)}, bf16[432,128]{1,0:T(8,128)(2,1)S(1)}, u32[]{:S(2)}, u32[]{:S(2)}) collective-permute-start(bf16[432,128]{1,0:T(8,128)(2,1)S(1)} %get-tuple-element.67), channel_id=1, source_target_pairs={{0,6},{1,7},{2,4},{3,5},{4,2},{5,3},{6,0},{7,1},{8,14},{9,15},{10,... | collective-permute-start | bytes 331784 | tf_op jit(solution)/shard_map/ppermute | solution.py:35
  54.3 0.0 collective-permute-done.21.got
  54.3 0.6 shard_map.74
  54.9 0.3 collective-permute-start.24
  55.3 4.0 %shard_map.75 = bf16[4,384,128]{2,1,0:T(8,128)(2,1)} custom-call(s32[3]{0:T(128)S(1)} %pad_add_fusion.ids, f32[4,16,128]{2,1,0:T(8,128)S(1)} %get-tuple-element.45.stats, f32[8,128]{1,0:T(8,128)S(1)} %broadcast_in_dim.8.gain, bf16[27,128,128]{2,1,0:T(8,128)(2,1)S(1)} %bitcast.20, bf16[384,128]{1,0:T(8,128)(2,1)S(1)} %get-tuple-element.40.refs_0_, ...), custom_call_target="tpu_custom_call" | custom-call | flops 5435817984 | tf_op jit(solution)/shard_map/pallas_call | solution.py:546
  59.2 2.8 %collective-permute-done.22.refs_0_ = bf16[432,128]{1,0:T(8,128)(2,1)S(1)} collective-permute-done((bf16[432,128]{1,0:T(8,128)(2,1)S(1)}, bf16[432,128]{1,0:T(8,128)(2,1)S(1)}, u32[]{:S(2)}, u32[]{:S(2)}) %collective-permute-start.22) | collective-permute-done | bytes 110624 | tf_op jit(solution)/shard_map/ppermute | solution.py:35
  62.0 0.0 collective-permute-done.23.refs_1_
  62.0 1.1 %collective-permute-done.24.refs_2_ = bf16[432,128]{1,0:T(8,128)(2,1)S(1)} collective-permute-done((bf16[432,128]{1,0:T(8,128)(2,1)S(1)}, bf16[432,128]{1,0:T(8,128)(2,1)S(1)}, u32[]{:S(2)}, u32[]{:S(2)}) %collective-permute-start.24) | collective-permute-done | bytes 110624 | tf_op jit(solution)/shard_map/ppermute | solution.py:35
  63.1 0.7 %shard_map.77 = f32[432,128]{1,0:T(8,128)} custom-call(f32[432,128]{1,0:T(8,128)S(1)} %get-tuple-element.63.own, bf16[432,128]{1,0:T(8,128)(2,1)S(1)} %collective-permute-done.22.refs_0_, bf16[432,128]{1,0:T(8,128)(2,1)S(1)} %collective-permute-done.23.refs_1_, bf16[432,128]{1,0:T(8,128)(2,1)S(1)} %collective-permute-done.24.refs_2_), custom_call_target="tpu_custom_call" | custom-call | tf_op jit(solution)/shard_map/pallas_call | solution.py:616
  (4 shorter events, 0.0 us)
Async XLA Ops:
  1.4 1.2 %copy-start = (bf16[1,3456,128]{2,1,0:T(8,128)(2,1)S(1)}, bf16[1,3456,128]{2,1,0:T(8,128)(2,1)}, u32[]{:S(2)}) copy-start(bf16[1,3456,128]{2,1,0:T(8,128)(2,1)} %param.6) | copy-start | bytes 2654212
  3.2 9.4 %collective-permute-start = (bf16[28,32,128]{2,1,0:T(8,128)(2,1)S(1)}, bf16[28,32,128]{2,1,0:T(8,128)(2,1)S(1)}, u32[]{:S(2)}, u32[]{:S(2)}) collective-permute-start(bf16[28,32,128]{2,1,0:T(8,128)(2,1)S(1)} %get-tuple-element.36.refs_0_), channel_id=1, source_target_pairs={{0,8},{8,0},{16,24},{24,16},{1,9},{9,1},{17,25},{25,17},{2,10},{10... | collective-permute-start | bytes 688136 | tf_op jit(solution)/shard_map/ppermute | solution.py:35
  6.2 8.4 %collective-permute-start.7 = (bf16[27,32,128]{2,1,0:T(8,128)(2,1)S(1)}, bf16[27,32,128]{2,1,0:T(8,128)(2,1)S(1)}, u32[]{:S(2)}, u32[]{:S(2)}) collective-permute-start(bf16[27,32,128]{2,1,0:T(8,128)(2,1)S(1)} %get-tuple-element.38.refs_1_), channel_id=1, source_target_pairs={{0,16},{8,24},{16,0},{24,8},{1,17},{9,25},{17,1},{25,9},{2,18},{10... | collective-permute-start | bytes 663560 | tf_op jit(solution)/shard_map/ppermute | solution.py:35
  7.7 8.8 %collective-permute-start.3 = (bf16[27,32,128]{2,1,0:T(8,128)(2,1)S(1)}, bf16[27,32,128]{2,1,0:T(8,128)(2,1)S(1)}, u32[]{:S(2)}, u32[]{:S(2)}) collective-permute-start(bf16[27,32,128]{2,1,0:T(8,128)(2,1)S(1)} %get-tuple-element.38.refs_1_), channel_id=1, source_target_pairs={{0,8},{8,0},{16,24},{24,16},{1,9},{9,1},{17,25},{25,17},{2,10},{10... | collective-permute-start | bytes 663560 | tf_op jit(solution)/shard_map/ppermute | solution.py:35
  8.2 10.0 %collective-permute-start.2 = (bf16[27,32,128]{2,1,0:T(8,128)(2,1)S(1)}, bf16[27,32,128]{2,1,0:T(8,128)(2,1)S(1)}, u32[]{:S(2)}, u32[]{:S(2)}) collective-permute-start(bf16[27,32,128]{2,1,0:T(8,128)(2,1)S(1)} %get-tuple-element.38.refs_1_), channel_id=1, source_target_pairs={{0,1},{1,0},{2,3},{3,2},{4,5},{5,4},{6,7},{7,6},{8,9},{9,8},{10,11... | collective-permute-start | bytes 663560 | tf_op jit(solution)/shard_map/ppermute | solution.py:35
  8.2 11.2 %collective-permute-start.6 = (bf16[28,32,128]{2,1,0:T(8,128)(2,1)S(1)}, bf16[28,32,128]{2,1,0:T(8,128)(2,1)S(1)}, u32[]{:S(2)}, u32[]{:S(2)}) collective-permute-start(bf16[28,32,128]{2,1,0:T(8,128)(2,1)S(1)} %get-tuple-element.36.refs_0_), channel_id=1, source_target_pairs={{0,16},{8,24},{16,0},{24,8},{1,17},{9,25},{17,1},{25,9},{2,18},{10... | collective-permute-start | bytes 688136 | tf_op jit(solution)/shard_map/ppermute | solution.py:35
  12.6 6.8 %collective-permute-start.1 = (bf16[28,32,128]{2,1,0:T(8,128)(2,1)S(1)}, bf16[28,32,128]{2,1,0:T(8,128)(2,1)S(1)}, u32[]{:S(2)}, u32[]{:S(2)}) collective-permute-start(bf16[28,32,128]{2,1,0:T(8,128)(2,1)S(1)} %get-tuple-element.36.refs_0_), channel_id=1, source_target_pairs={{0,1},{1,0},{2,3},{3,2},{4,5},{5,4},{6,7},{7,6},{8,9},{9,8},{10,11... | collective-permute-start | bytes 688136 | tf_op jit(solution)/shard_map/ppermute | solution.py:35
  14.5 8.4 %collective-permute-start.10 = (bf16[28,32,128]{2,1,0:T(8,128)(2,1)S(1)}, bf16[28,32,128]{2,1,0:T(8,128)(2,1)S(1)}, u32[]{:S(2)}, u32[]{:S(2)}) collective-permute-start(bf16[28,32,128]{2,1,0:T(8,128)(2,1)S(1)} %collective-permute-done.refs_4_), channel_id=1, source_target_pairs={{0,16},{8,24},{16,0},{24,8},{1,17},{9,25},{17,1},{25,9},{2,18},{10... | collective-permute-start | bytes 688136 | tf_op jit(solution)/shard_map/ppermute | solution.py:35
  16.5 6.6 %collective-permute-start.11 = (bf16[27,32,128]{2,1,0:T(8,128)(2,1)S(1)}, bf16[27,32,128]{2,1,0:T(8,128)(2,1)S(1)}, u32[]{:S(2)}, u32[]{:S(2)}) collective-permute-start(bf16[27,32,128]{2,1,0:T(8,128)(2,1)S(1)} %collective-permute-done.7.refs_9_), channel_id=1, source_target_pairs={{0,8},{8,0},{16,24},{24,16},{1,9},{9,1},{17,25},{25,17},{2,10},{10... | collective-permute-start | bytes 663560 | tf_op jit(solution)/shard_map/ppermute | solution.py:35
  18.3 5.1 %collective-permute-start.9 = (bf16[27,32,128]{2,1,0:T(8,128)(2,1)S(1)}, bf16[27,32,128]{2,1,0:T(8,128)(2,1)S(1)}, u32[]{:S(2)}, u32[]{:S(2)}) collective-permute-start(bf16[27,32,128]{2,1,0:T(8,128)(2,1)S(1)} %collective-permute-done.7.refs_9_), channel_id=1, source_target_pairs={{0,1},{1,0},{2,3},{3,2},{4,5},{5,4},{6,7},{7,6},{8,9},{9,8},{10,11... | collective-permute-start | bytes 663560 | tf_op jit(solution)/shard_map/ppermute | solution.py:35
  19.5 5.3 %collective-permute-start.8 = (bf16[28,32,128]{2,1,0:T(8,128)(2,1)S(1)}, bf16[28,32,128]{2,1,0:T(8,128)(2,1)S(1)}, u32[]{:S(2)}, u32[]{:S(2)}) collective-permute-start(bf16[28,32,128]{2,1,0:T(8,128)(2,1)S(1)} %collective-permute-done.6.refs_8_), channel_id=1, source_target_pairs={{0,1},{1,0},{2,3},{3,2},{4,5},{5,4},{6,7},{7,6},{8,9},{9,8},{10,11... | collective-permute-start | bytes 688136 | tf_op jit(solution)/shard_map/ppermute | solution.py:35
  19.5 5.3 %collective-permute-start.4 = (bf16[28,32,128]{2,1,0:T(8,128)(2,1)S(1)}, bf16[28,32,128]{2,1,0:T(8,128)(2,1)S(1)}, u32[]{:S(2)}, u32[]{:S(2)}) collective-permute-start(bf16[28,32,128]{2,1,0:T(8,128)(2,1)S(1)} %collective-permute-done.refs_4_), channel_id=1, source_target_pairs={{0,1},{1,0},{2,3},{3,2},{4,5},{5,4},{6,7},{7,6},{8,9},{9,8},{10,11... | collective-permute-start | bytes 688136 | tf_op jit(solution)/shard_map/ppermute | solution.py:35
  22.9 2.1 %collective-permute-start.12 = (bf16[28,32,128]{2,1,0:T(8,128)(2,1)S(1)}, bf16[28,32,128]{2,1,0:T(8,128)(2,1)S(1)}, u32[]{:S(2)}, u32[]{:S(2)}) collective-permute-start(bf16[28,32,128]{2,1,0:T(8,128)(2,1)S(1)} %collective-permute-done.10.refs_12_), channel_id=1, source_target_pairs={{0,1},{1,0},{2,3},{3,2},{4,5},{5,4},{6,7},{7,6},{8,9},{9,8},{10,11... | collective-permute-start | bytes 688136 | tf_op jit(solution)/shard_map/ppermute | solution.py:35
  23.1 1.6 %collective-permute-start.5 = (bf16[27,32,128]{2,1,0:T(8,128)(2,1)S(1)}, bf16[27,32,128]{2,1,0:T(8,128)(2,1)S(1)}, u32[]{:S(2)}, u32[]{:S(2)}) collective-permute-start(bf16[27,32,128]{2,1,0:T(8,128)(2,1)S(1)} %collective-permute-done.3.refs_5_), channel_id=1, source_target_pairs={{0,1},{1,0},{2,3},{3,2},{4,5},{5,4},{6,7},{7,6},{8,9},{9,8},{10,11... | collective-permute-start | bytes 663560 | tf_op jit(solution)/shard_map/ppermute | solution.py:35
  23.4 1.6 %collective-permute-start.13 = (bf16[27,32,128]{2,1,0:T(8,128)(2,1)S(1)}, bf16[27,32,128]{2,1,0:T(8,128)(2,1)S(1)}, u32[]{:S(2)}, u32[]{:S(2)}) collective-permute-start(bf16[27,32,128]{2,1,0:T(8,128)(2,1)S(1)} %collective-permute-done.11.refs_13_), channel_id=1, source_target_pairs={{0,1},{1,0},{2,3},{3,2},{4,5},{5,4},{6,7},{7,6},{8,9},{9,8},{10,11... | collective-permute-start | bytes 663560 | tf_op jit(solution)/shard_map/ppermute | solution.py:35
  30.4 9.9 %collective-permute-start.14 = (bf16[384,128]{1,0:T(8,128)(2,1)S(1)}, bf16[384,128]{1,0:T(8,128)(2,1)S(1)}, u32[]{:S(2)}, u32[]{:S(2)}) collective-permute-start(bf16[384,128]{1,0:T(8,128)(2,1)S(1)} %get-tuple-element.41), channel_id=1, source_target_pairs={{0,8},{8,0},{16,24},{24,16},{1,9},{9,1},{17,25},{25,17},{2,10},{10... | collective-permute-start | bytes 294920 | tf_op jit(solution)/shard_map/ppermute | solution.py:35
  31.8 9.2 %collective-permute-start.15 = (bf16[384,128]{1,0:T(8,128)(2,1)S(1)}, bf16[384,128]{1,0:T(8,128)(2,1)S(1)}, u32[]{:S(2)}, u32[]{:S(2)}) collective-permute-start(bf16[384,128]{1,0:T(8,128)(2,1)S(1)} %get-tuple-element.42), channel_id=1, source_target_pairs={{0,16},{8,24},{16,0},{24,8},{1,17},{9,25},{17,1},{25,9},{2,18},{10... | collective-permute-start | bytes 294920 | tf_op jit(solution)/shard_map/ppermute | solution.py:35
  33.4 7.6 %collective-permute-start.16 = (bf16[384,128]{1,0:T(8,128)(2,1)S(1)}, bf16[384,128]{1,0:T(8,128)(2,1)S(1)}, u32[]{:S(2)}, u32[]{:S(2)}) collective-permute-start(bf16[384,128]{1,0:T(8,128)(2,1)S(1)} %get-tuple-element.43), channel_id=1, source_target_pairs={{0,24},{8,16},{16,8},{24,0},{1,25},{9,17},{17,9},{25,1},{2,26},{10... | collective-permute-start | bytes 294920 | tf_op jit(solution)/shard_map/ppermute | solution.py:35
  37.4 8.4 %collective-permute-start.17 = (bf16[384,128]{1,0:T(8,128)(2,1)S(1)}, bf16[384,128]{1,0:T(8,128)(2,1)S(1)}, u32[]{:S(2)}, u32[]{:S(2)}) collective-permute-start(bf16[384,128]{1,0:T(8,128)(2,1)S(1)} %get-tuple-element.53), channel_id=1, source_target_pairs={{0,8},{8,0},{16,24},{24,16},{1,9},{9,1},{17,25},{25,17},{2,10},{10... | collective-permute-start | bytes 294920 | tf_op jit(solution)/shard_map/ppermute | solution.py:35
  38.8 7.0 %collective-permute-start.18 = (bf16[384,128]{1,0:T(8,128)(2,1)S(1)}, bf16[384,128]{1,0:T(8,128)(2,1)S(1)}, u32[]{:S(2)}, u32[]{:S(2)}) collective-permute-start(bf16[384,128]{1,0:T(8,128)(2,1)S(1)} %get-tuple-element.54), channel_id=1, source_target_pairs={{0,16},{8,24},{16,0},{24,8},{1,17},{9,25},{17,1},{25,9},{2,18},{10... | collective-permute-start | bytes 294920 | tf_op jit(solution)/shard_map/ppermute | solution.py:35
  40.4 5.5 %collective-permute-start.19 = (bf16[384,128]{1,0:T(8,128)(2,1)S(1)}, bf16[384,128]{1,0:T(8,128)(2,1)S(1)}, u32[]{:S(2)}, u32[]{:S(2)}) collective-permute-start(bf16[384,128]{1,0:T(8,128)(2,1)S(1)} %get-tuple-element.55), channel_id=1, source_target_pairs={{0,24},{8,16},{16,8},{24,0},{1,25},{9,17},{17,9},{25,1},{2,26},{10... | collective-permute-start | bytes 294920 | tf_op jit(solution)/shard_map/ppermute | solution.py:35
  41.0 1.2 %copy-start.1 = (bf16[1,3456,128]{2,1,0:T(8,128)(2,1)S(1)}, bf16[1,3456,128]{2,1,0:T(8,128)(2,1)}, u32[]{:S(2)}) copy-start(bf16[1,3456,128]{2,1,0:T(8,128)(2,1)} %param.6) | copy-start | bytes 2654212
  47.7 1.5 %collective-permute-start.20 = (bf16[2,432,128]{2,1,0:T(8,128)(2,1)S(1)}, bf16[2,432,128]{2,1,0:T(8,128)(2,1)S(1)}, u32[]{:S(2)}, u32[]{:S(2)}) collective-permute-start(bf16[2,432,128]{2,1,0:T(8,128)(2,1)S(1)} %get-tuple-element.59), channel_id=1, source_target_pairs={{0,1},{1,0},{2,3},{3,2},{4,5},{5,4},{6,7},{7,6},{8,9},{9,8},{10,11... | collective-permute-start | bytes 663560 | tf_op jit(solution)/shard_map/ppermute | solution.py:35
  49.3 5.1 %collective-permute-start.21 = (bf16[2,432,128]{2,1,0:T(8,128)(2,1)S(1)}, bf16[2,432,128]{2,1,0:T(8,128)(2,1)S(1)}, u32[]{:S(2)}, u32[]{:S(2)}) collective-permute-start(bf16[2,432,128]{2,1,0:T(8,128)(2,1)S(1)} %get-tuple-element.60), channel_id=1, source_target_pairs={{0,1},{1,0},{2,3},{3,2},{4,5},{5,4},{6,7},{7,6},{8,9},{9,8},{10,11... | collective-permute-start | bytes 663560 | tf_op jit(solution)/shard_map/ppermute | solution.py:35
  50.3 11.7 %collective-permute-start.22 = (bf16[432,128]{1,0:T(8,128)(2,1)S(1)}, bf16[432,128]{1,0:T(8,128)(2,1)S(1)}, u32[]{:S(2)}, u32[]{:S(2)}) collective-permute-start(bf16[432,128]{1,0:T(8,128)(2,1)S(1)} %get-tuple-element.66), channel_id=1, source_target_pairs={{0,4},{1,5},{2,6},{3,7},{4,0},{5,1},{6,2},{7,3},{8,12},{9,13},{10,... | collective-permute-start | bytes 331784 | tf_op jit(solution)/shard_map/ppermute | solution.py:35
  53.0 9.0 %collective-permute-start.23 = (bf16[432,128]{1,0:T(8,128)(2,1)S(1)}, bf16[432,128]{1,0:T(8,128)(2,1)S(1)}, u32[]{:S(2)}, u32[]{:S(2)}) collective-permute-start(bf16[432,128]{1,0:T(8,128)(2,1)S(1)} %get-tuple-element.67), channel_id=1, source_target_pairs={{0,6},{1,7},{2,4},{3,5},{4,2},{5,3},{6,0},{7,1},{8,14},{9,15},{10,... | collective-permute-start | bytes 331784 | tf_op jit(solution)/shard_map/ppermute | solution.py:35
  54.9 8.2 %collective-permute-start.24 = (bf16[432,128]{1,0:T(8,128)(2,1)S(1)}, bf16[432,128]{1,0:T(8,128)(2,1)S(1)}, u32[]{:S(2)}, u32[]{:S(2)}) collective-permute-start(bf16[432,128]{1,0:T(8,128)(2,1)S(1)} %get-tuple-element.68), channel_id=1, source_target_pairs={{0,2},{1,3},{2,0},{3,1},{4,6},{5,7},{6,4},{7,5},{8,10},{9,11},{10,... | collective-permute-start | bytes 331784 | tf_op jit(solution)/shard_map/ppermute | solution.py:35

commit v4 on v3

--- a/solution.py
+++ b/solution.py
@@ -176,26 +176,7 @@
                         put_rows(spread, k * frames + f, a, pieces)
 
 
-def cut_kernel(parts, ids, gain, own, *refs):
-    pieces, sems = refs[:parts], refs[parts]
-    taps, quarter = own.shape[0], pieces[0].shape[1]
-    copies = []
-    for j in range(parts):
-        rows = pl.ds(pl.multiple_of((ids[1] * parts + j) * quarter, quarter), quarter)
-        copies.append(pltpu.make_async_copy(own.at[:, rows, :], pieces[j].at[0:taps], sems.at[j]))
-    for copy in copies:
-        copy.start()
-    wide = full(gain[...], quarter)
-    high = wide.astype(BF).astype(F32)
-    middle = (wide - high).astype(BF).astype(F32)
-    low = wide - high - middle
-    row = lax.broadcasted_iota(jnp.int32, wide.shape, 0)
-    pieces[0][taps] = jnp.where(row == 0, high, jnp.where(row == 1, middle, low)).astype(BF)
-    for copy in copies:
-        copy.wait()
-
-
-def forward_kernel(sections, dims, ids, x_ref, gain, *refs):
+def forward_kernel(sections, dims, ids, x_ref, *refs):
     frames, rows, cols, chans = dims
     plane = rows * cols
     n_chunk = (len(refs) - 9 - sections) // sections
@@ -203,12 +184,12 @@
     refs = refs[sections * n_chunk :]
     outs, stats, every = refs[:3]
     sends = refs[3 : 3 + sections]
-    spread, product, inputs, gain_rows, gain_sem, sems = refs[3 + sections :]
+    spread, product, inputs, gains, gain_sem, sems = refs[3 + sections :]
     place = ids[0]
     taps = every.shape[1]
     copies = [
-        pltpu.make_async_copy(chunks[k][0].at[taps], gain_rows.at[k - 1], gain_sem.at[k - 1])
-        for k in range(1, sections)
+        pltpu.make_async_copy(chunks[k][0].at[taps], gains.at[k], gain_sem.at[k])
+        for k in range(sections)
     ]
     for copy in copies:
         copy.start()
@@ -216,10 +197,9 @@
     for k in range(sections):
         for copy in copies_of(chunks[k], piece_ids(ids, n_chunk), every.at[k], sems.at[k]):
             copy.start()
-    stats[place, 16:24] = full(gain[...], 8)
-    for k in range(1, sections):
-        copies[k - 1].wait()
-        parts = gain_rows[k - 1].astype(F32)
+    for k in range(sections):
+        copies[k].wait()
+        parts = gains[k].astype(F32)
         stats[place ^ k, 16:24] = full(parts[0:1] + parts[1:2] + parts[2:3], 8)
     x = x_ref[...]
     for unit in range(sections):
@@ -241,15 +221,16 @@
         sends[k][...] = inputs[place ^ k]
 
 
-def turn_kernel(dims, n, gain, *refs):
+def turn_kernel(dims, n, ids, unit_stats, *refs):
     frames, rows, cols, chans = dims
     plane, points = rows * cols, frames * rows * cols
     xs, (turned, stats) = refs[:n], refs[n:]
+    gain = unit_stats[ids[0], 16:24]
     for k in range(n):
         x32 = xs[k][...].astype(F32)
         mean, rstd = statistics(x32, chans // GROUPS)
-        stats[k, 0:8], stats[k, 8:16] = mean, rstd
-        _, scaled, gate = norm_parts(x32, full(mean, points), full(rstd, points), full(gain[...], points))
+        stats[k, 0:8], stats[k, 8:16], stats[k, 16:24] = mean, rstd, gain
+        _, scaled, gate = norm_parts(x32, full(mean, points), full(rstd, points), full(gain, points))
         act = (scaled * gate).astype(BF).astype(F32)
         for f in range(frames):
             frame = act[f * plane : (f + 1) * plane]
@@ -258,21 +239,30 @@
                 turned[at * chans : (at + 1) * chans, pl.ds((f * n + k) * plane, plane)] = piece.T.astype(BF)
 
 
-def home_forward_kernel(dims, n, ids, stats, gain, own, *refs):
+def home_forward_kernel(dims, n, first, last, ids, stats, own, *refs):
     frames, rows, cols, chans = dims
     plane = rows * cols
-    xs, (seg, spread) = refs[:n], refs[n:]
+    count = last - first
+    xs, refs = refs[:count], refs[count:]
+    done = refs[:first] if last == n else ()
+    outs, spread = refs[len(done) : -1], refs[-1]
+    for k in range(len(done)):
+        outs[0][lax.rem(ids[0] ^ k, n)] = done[k][...]
     values = [ref[...].astype(F32) for ref in xs]
-    known = [(stats[k, 0:8], stats[k, 8:16]) for k in range(n)]
-    spread_forward(dims, values, known, gain[...], spread)
-    lhs = spread[...].reshape(n * frames * plane, 9 * chans)
+    known = [(stats[first + i, 0:8], stats[first + i, 8:16]) for i in range(count)]
+    spread_forward(dims, values, known, stats[0, 16:17], spread)
+    lhs = spread[...].reshape(count * frames * plane, 9 * chans)
     product = jnp.dot(lhs, forward_matrix(own[...]), preferred_element_type=F32)
-    for k in range(n):
-        at = (ids[0] ^ k) % n
+    for i in range(count):
+        at = lax.rem(ids[0] ^ (first + i), n)
         for f in range(frames):
             spot = slice(f * plane, (f + 1) * plane)
-            joined = join_cols(product[(k * frames + f) * plane : (k * frames + f + 1) * plane], cols, chans, (-1, 0, 1))
-            seg[at, spot] = (values[k][spot] + joined).astype(BF)
+            joined = join_cols(product[(i * frames + f) * plane : (i * frames + f + 1) * plane], cols, chans, (-1, 0, 1))
+            result = (values[i][spot] + joined).astype(BF)
+            if last == n:
+                outs[0][at, spot] = result
+            else:
+                outs[i][spot] = result
 
 
 def unit_backward(dims, x32, grad, stat, gain, multiply, spread):
@@ -324,7 +314,7 @@
         sends[k][...] = grads[place ^ k]
 
 
-def home_backward_kernel(dims, n, first, last, ids, stats, gain, own, *refs):
+def home_backward_kernel(dims, n, first, last, ids, stats, own, *refs):
     count = last - first
     xs, grads = refs[:count], refs[count : 2 * count]
     refs = refs[2 * count :]
@@ -339,7 +329,7 @@
             xs[i][...].astype(F32),
             grads[i][...],
             stats[first + i],
-            gain[...],
+            stats[0, 16:17],
             lambda lhs: times_transposed(lhs, own[...]),
             spread,
         )
@@ -395,7 +385,7 @@
 def half_kernel(dims, n, far, levels, ids, turned, *refs):
     chans = dims[3]
     if far:
-        put_right(dims, n, refs[:n], refs[n])
+        put_right(dims, n, refs[:n][::-1], refs[n])
         refs = refs[n:]
     right, keep, send, term = refs
     upper = ids[2] >= levels // 2
@@ -432,6 +422,18 @@
     for ref in refs[:-1]:
         total = total + ref[...].astype(F32)
     refs[-1][...] = total * scale
+
+
+def with_gains(piece, gains):
+    taps, rows, chans = piece.shape
+    high = lax.reduce_precision(gains, 8, 7)
+    middle = lax.reduce_precision(gains - high, 8, 7)
+    low = gains - high - middle
+    shape = (taps + 1, rows, chans)
+    row = lax.broadcasted_iota(jnp.int32, shape, 1)
+    extra = jnp.where(row == 0, high[None], jnp.where(row == 1, middle[None], low[None])).astype(BF)
+    padded = lax.pad(piece, jnp.zeros((), BF), ((0, 1, 0), (0, 0, 0), (0, 0, 0)))
+    return jnp.where(lax.broadcasted_iota(jnp.int32, shape, 0) < taps, padded, extra)
 
 
 def gather_chunks(mine, sections, ride):
@@ -467,14 +469,9 @@
     video = video.reshape(micro, points, chans)
     cot = cotangent.reshape(micro, points, chans)
     kernel_rows = weights.reshape(27, chans, chans)
-    gain_rows = jnp.broadcast_to(gains, (8, chans))
-    mine = call(
-        functools.partial(cut_kernel, parts),
-        [jax.ShapeDtypeStruct((27 + (j == 0), quarter, chans), BF) for j in range(parts)],
-        [SM, VM, ANY],
-        [VM] * parts,
-        [pltpu.SemaphoreType.DMA((parts,))],
-    )(ids, gain_rows, kernel_rows)
+    cut = kernel_rows.reshape(27, n_chunk, quarter, chans)
+    mine = [lax.dynamic_index_in_dim(cut, core * parts + j, 1, False) for j in range(parts)]
+    mine[0] = with_gains(mine[0], gains)
     x = lax.dynamic_index_in_dim(video, lax.rem(place, micro), 0, False)
     grad = lax.dynamic_index_in_dim(cot, lax.rem(place, micro), 0, False)
     got, (x, grad) = gather_chunks(mine, sections, (x, grad))
@@ -499,18 +496,18 @@
             jax.ShapeDtypeStruct((sections, 27, chans, chans), BF),
         ]
         + [act_shape] * sections,
-        [SM, VM, VM] + [ANY] * len(flat),
+        [SM, VM] + [ANY] * len(flat),
         [VM] * (3 + sections),
         [
             spread(1),
             product,
             pltpu.VMEM((sections, points, chans), BF),
-            pltpu.VMEM((sections - 1, quarter, chans), BF),
-            pltpu.SemaphoreType.DMA((sections - 1,)),
+            pltpu.VMEM((sections, quarter, chans), BF),
+            pltpu.SemaphoreType.DMA((sections,)),
             pltpu.SemaphoreType.DMA((sections,)),
         ],
         flops=4 * sections * unit_flops,
-    )(ids, x, gain_rows, *flat)
+    )(ids, x, *flat)
     xs_home = [xsends[0]] + [swap(xsends[k], "pipe", k) for k in range(1, n)]
 
     gsends = call(
@@ -525,35 +522,36 @@
 
     turned, home_stats = call(
         functools.partial(turn_kernel, dims, n),
-        [jax.ShapeDtypeStruct((3 * chans, n * points), BF), jax.ShapeDtypeStruct((n, 16, chans), F32)],
-        [VM] * (1 + n),
+        [jax.ShapeDtypeStruct((3 * chans, n * points), BF), jax.ShapeDtypeStruct((n, 24, chans), F32)],
+        [SM] + [VM] * (1 + n),
         [VM] * 2,
         flops=n * unit_flops,
-    )(gain_rows, *xs_home)
-
-    def home_forward(ids):
+    )(ids, stats, *xs_home)
+
+    def home_forward(first, last, done, ids):
+        count = last - first
         return call(
-            functools.partial(home_forward_kernel, dims, n),
-            jax.ShapeDtypeStruct((micro, points, chans), BF),
-            [SM, VM, VM, VM] + [VM] * n,
-            VM,
-            [spread(n)],
-            flops=4 * n * unit_flops,
-        )(ids, home_stats, gain_rows, kernel_rows, *xs_home)
+            functools.partial(home_forward_kernel, dims, n, first, last),
+            [jax.ShapeDtypeStruct((micro, points, chans), BF)] if last == n else [act_shape] * count,
+            [SM, VM, VM] + [VM] * (count + len(done)),
+            [VM] * (1 if last == n else count),
+            [spread(count)],
+            flops=4 * count * unit_flops,
+        )(ids, home_stats, kernel_rows, *xs_home[first:last], *done)
 
     def home_backward(first, last, done, ids):
         count = last - first
         return call(
             functools.partial(home_backward_kernel, dims, n, first, last),
             [jax.ShapeDtypeStruct((micro, points, chans), BF)] if last == n else [act_shape] * count,
-            [SM, VM, VM, VM] + [VM] * (2 * count + len(done)),
+            [SM, VM, VM] + [VM] * (2 * count + len(done)),
             [VM] * (1 if last == n else count),
             [spread(1)],
             flops=4 * count * unit_flops,
-        )(ids, home_stats, gain_rows, kernel_rows, *xs_home[first:last], *grads_home[first:last], *done)
-
-    seg = home_forward(ids)
-    turned, seg = lax.optimization_barrier((turned, seg))
+        )(ids, home_stats, kernel_rows, *xs_home[first:last], *grads_home[first:last], *done)
+
+    seg_early = home_forward(0, n // 2, (), ids)
+    turned, *seg_early = lax.optimization_barrier((turned, *seg_early))
 
     size = 27 * chans // ranks
     levels = ranks // 2
@@ -577,7 +575,7 @@
             [VM] * 3,
             [term],
             flops=n * unit_flops // 2,
-        )(ids, turned, *grads_home)
+        )(ids, turned, *grads_home[::-1])
         got = swap(send, "dp", 1)
         near_keep, near_send = call(
             functools.partial(half_kernel, dims, n, False, levels),
@@ -611,6 +609,7 @@
 
     late, own = lax.optimization_barrier((ids, own))
     (ing,) = home_backward(0, n, (), late)
+    (seg,) = home_forward(n // 2, n, seg_early, late)
 
     scale = 1.0 / math.sqrt(micro * clips * ranks * points)
     share = call(

time: 64.1 us -> 62.8 us (0.980)
  waiting for transfers between devices: 15.5 us -> 13.9 us
  local copies, waits for them, and re-layouts: 3.06 us -> 2.03 us
  other arithmetic: 0.08 us -> 0.86 us
    ppermute x25, waiting for transfers between devices: 15.5 us -> 13.9 us  [swap(): return lax.ppermute(value, axis, [(i, i ^ bits) for i in range(count)])]
    unnamed x4 -> x2, local copies, waits for them, and re-layouts: 1.45 us -> 0.01 us
    squeeze x0 -> x1, local copies, waits for them, and re-layouts: none -> 1.08 us  [body(): lax.dynamic_index_in_dim(cut, core * parts + j, 1, False)]
    broadcast_in_dim x0 -> x1, other arithmetic: none -> 0.66 us  [with_gains(): jnp.where(row == 0, high[None], jnp.where(row == 1, middle[None], low[Non...]
    broadcast_in_dim x1 -> x0, local copies, waits for them, and re-layouts: 0.66 us -> none  [body(): gain_rows = jnp.broadcast_to(gains, (8, chans))]
  transfers between devices with their start and end apart: 25 -> 25, of which waited for: 11 -> 13; matrix products, arithmetic and copies ran while one was open for 1% -> 2% of each run, Pallas kernels for 23% -> 25%
where the time goes in v4:
time: 62.8 us; the launch traced here: 62.7 us
  Pallas kernels  23.7 us (38%)
  starting transfers between devices  21.3 us (34%)
  waiting for transfers between devices  13.9 us (22%)
  local copies, waits for them, and re-layouts  2.03 us (3%)
  other arithmetic  0.86 us (1%)
  between operations  0.78 us (1%)
    ppermute x25, starting transfers between devices, swap(): return lax.ppermute(value, axis, [(i, i ^ bits) for i in range(count)])  21.3 us
    ppermute x25, waiting for transfers between devices, swap(): return lax.ppermute(value, axis, [(i, i ^ bits) for i in range(count)])  13.9 us
    pallas_call x1, Pallas kernels, body(): call(functools.partial(forward_kernel, sections, dims), [jax.ShapeDtypeSt...  5.37 us
    pallas_call x2, Pallas kernels, home_forward(): call(functools.partial(home_forward_kernel, dims, n, first, last), [jax.S...  4.38 us
    pallas_call x1, Pallas kernels, home_backward(): call(functools.partial(home_backward_kernel, dims, n, first, last), [jax....  3.96 us
    pallas_call x1, Pallas kernels, body(): call(functools.partial(backward_kernel, sections, dims), [act_shape] * se...  3.43 us
    pallas_call x1, Pallas kernels, body(): call(functools.partial(half_kernel, dims, n, True, levels), [right_shape]...  1.83 us
    pallas_call x1, Pallas kernels, body(): call(functools.partial(turn_kernel, dims, n), [jax.ShapeDtypeStruct((3 *...  1.42 us
  transfers between devices with their start and end apart: 25, of which 13 were waited for; matrix products, arithmetic and copies ran while one was open for 2% of the time, Pallas kernels for 25%

profile of v4, /device:TPU:0, one launch (start us, length us, event | category | flops | bytes accessed | tf_op | source)
XLA Modules:
  0.0 62.7 jit_solution(14301538762806703612)
XLA Ops:
  0.7 0.7 %reduce-precision_bitcast_fusion.1 = (bf16[128]{0:T(256)(128)(2,1)S(1)}, bf16[128]{0:T(256)(128)(2,1)S(1)}, bf16[128]{0:T(256)(128)(2,1)S(1)}) fusion(f32[1,128]{1,0:T(1,128)} %param.7), kind=kLoop, calls=%fused_computation.9 | loop fusion | flops 896 | bytes 1280 | tf_op jit(solution)/shard_map/jit(_where)/broadcast_in_dim | solution.py:434
  1.3 1.1 %dynamic-slice_bitcast_fusion = (bf16[27,32,128]{2,1,0:T(8,128)(2,1)S(1)}, bf16[27,32,128]{2,1,0:T(8,128)(2,1)S(1)}) fusion(bf16[27,4,32,128]{3,2,1,0:T(8,128)(2,1)} %bitcast.32, s32[]{:T(128)S(6)} %select_n.29, s32[]{:T(128)S(6)} %select_n.24), kind=kLoop, calls=%fused_computation.2 | loop fusion | bytes 884744 | tf_op jit(solution)/shard_map/jit(dynamic_index_in_dim)/squeeze | solution.py:473
  2.4 0.1 fusion.refs_0_
  2.5 3.0 %collective-permute-start = (bf16[28,32,128]{2,1,0:T(8,128)(2,1)S(1)}, bf16[28,32,128]{2,1,0:T(8,128)(2,1)S(1)}, u32[]{:S(2)}, u32[]{:S(2)}) collective-permute-start(bf16[28,32,128]{2,1,0:T(8,128)(2,1)S(1)} %fusion.refs_0_), channel_id=1, source_target_pairs={{0,8},{8,0},{16,24},{24,16},{1,9},{9,1},{17,25},{25,17},{2,10},{10... | collective-permute-start | bytes 688136 | tf_op jit(solution)/shard_map/ppermute | solution.py:35
  5.5 1.5 %collective-permute-start.7 = (bf16[27,32,128]{2,1,0:T(8,128)(2,1)S(1)}, bf16[27,32,128]{2,1,0:T(8,128)(2,1)S(1)}, u32[]{:S(2)}, u32[]{:S(2)}) collective-permute-start(bf16[27,32,128]{2,1,0:T(8,128)(2,1)S(1)} %get-tuple-element.74.refs_1_), channel_id=1, source_target_pairs={{0,16},{8,24},{16,0},{24,8},{1,17},{9,25},{17,1},{25,9},{2,18},{10... | collective-permute-start | bytes 663560 | tf_op jit(solution)/shard_map/ppermute | solution.py:35
  7.1 0.5 collective-permute-start.3
  7.6 0.0 collective-permute-start.2
  7.6 0.1 collective-permute-start.6
  7.6 1.0 %dynamic-slice_bitcast_fusion.2 = (bf16[384,128]{1,0:T(8,128)(2,1)S(1)}, bf16[384,128]{1,0:T(8,128)(2,1)S(1)}) fusion(bf16[4,384,128]{2,1,0:T(8,128)(2,1)} %bitcast.37, s32[]{:T(128)S(6)} %select_n.28, bf16[4,384,128]{2,1,0:T(8,128)(2,1)} %bitcast.38), kind=kLoop, calls=%fused_computation.4 | loop fusion | bytes 393220 | tf_op jit(solution)/shard_map/jit(dynamic_index_in_dim)/squeeze | solution.py:476
  8.6 3.4 %collective-permute-done.refs_4_ = bf16[28,32,128]{2,1,0:T(8,128)(2,1)S(1)} collective-permute-done((bf16[28,32,128]{2,1,0:T(8,128)(2,1)S(1)}, bf16[28,32,128]{2,1,0:T(8,128)(2,1)S(1)}, u32[]{:S(2)}, u32[]{:S(2)}) %collective-permute-start) | collective-permute-done | bytes 229408 | tf_op jit(solution)/shard_map/ppermute | solution.py:35
  12.0 0.0 collective-permute-start.1
  12.0 1.9 %collective-permute-done.7.refs_9_ = bf16[27,32,128]{2,1,0:T(8,128)(2,1)S(1)} collective-permute-done((bf16[27,32,128]{2,1,0:T(8,128)(2,1)S(1)}, bf16[27,32,128]{2,1,0:T(8,128)(2,1)S(1)}, u32[]{:S(2)}, u32[]{:S(2)}) %collective-permute-start.7) | collective-permute-done | bytes 221216 | tf_op jit(solution)/shard_map/ppermute | solution.py:35
  13.9 1.5 %collective-permute-start.10 = (bf16[28,32,128]{2,1,0:T(8,128)(2,1)S(1)}, bf16[28,32,128]{2,1,0:T(8,128)(2,1)S(1)}, u32[]{:S(2)}, u32[]{:S(2)}) collective-permute-start(bf16[28,32,128]{2,1,0:T(8,128)(2,1)S(1)} %collective-permute-done.refs_4_), channel_id=1, source_target_pairs={{0,16},{8,24},{16,0},{24,8},{1,17},{9,25},{17,1},{25,9},{2,18},{10... | collective-permute-start | bytes 688136 | tf_op jit(solution)/shard_map/ppermute | solution.py:35
  15.4 0.5 collective-permute-done.3.refs_5_
  15.9 1.7 %collective-permute-start.11 = (bf16[27,32,128]{2,1,0:T(8,128)(2,1)S(1)}, bf16[27,32,128]{2,1,0:T(8,128)(2,1)S(1)}, u32[]{:S(2)}, u32[]{:S(2)}) collective-permute-start(bf16[27,32,128]{2,1,0:T(8,128)(2,1)S(1)} %collective-permute-done.7.refs_9_), channel_id=1, source_target_pairs={{0,8},{8,0},{16,24},{24,16},{1,9},{9,1},{17,25},{25,17},{2,10},{10... | collective-permute-start | bytes 663560 | tf_op jit(solution)/shard_map/ppermute | solution.py:35
  17.6 0.0 collective-permute-done.2.refs_3_
  17.6 0.0 collective-permute-start.9
  17.6 1.2 %collective-permute-done.6.refs_8_ = bf16[28,32,128]{2,1,0:T(8,128)(2,1)S(1)} collective-permute-done((bf16[28,32,128]{2,1,0:T(8,128)(2,1)S(1)}, bf16[28,32,128]{2,1,0:T(8,128)(2,1)S(1)}, u32[]{:S(2)}, u32[]{:S(2)}) %collective-permute-start.6) | collective-permute-done | bytes 229408 | tf_op jit(solution)/shard_map/ppermute | solution.py:35
  18.8 0.0 collective-permute-start.8
  18.8 0.0 collective-permute-done.1.refs_2_
  18.8 0.5 collective-permute-start.4
  19.3 2.9 %collective-permute-done.10.refs_12_ = bf16[28,32,128]{2,1,0:T(8,128)(2,1)S(1)} collective-permute-done((bf16[28,32,128]{2,1,0:T(8,128)(2,1)S(1)}, bf16[28,32,128]{2,1,0:T(8,128)(2,1)S(1)}, u32[]{:S(2)}, u32[]{:S(2)}) %collective-permute-start.10) | collective-permute-done | bytes 229408 | tf_op jit(solution)/shard_map/ppermute | solution.py:35
  22.3 0.0 collective-permute-start.12
  22.3 0.2 collective-permute-done.11.refs_13_
  22.5 0.3 collective-permute-start.5
  22.8 0.0 collective-permute-done.9.refs_11_
  22.8 0.2 collective-permute-start.13
  23.0 0.1 pad_add_fusion.ids
  23.1 1.1 %collective-permute-done.5.refs_7_ = bf16[27,32,128]{2,1,0:T(8,128)(2,1)} collective-permute-done((bf16[27,32,128]{2,1,0:T(8,128)(2,1)S(1)}, bf16[27,32,128]{2,1,0:T(8,128)(2,1)}, u32[]{:S(2)}, u32[]{:S(2)}) %collective-permute-start.5) | collective-permute-done | bytes 221216 | tf_op jit(solution)/shard_map/ppermute | solution.py:35
  24.2 0.0 collective-permute-done.8.refs_10_
  24.2 0.0 collective-permute-done.4.refs_6_
  24.2 0.3 collective-permute-done.13.refs_15_
  24.5 0.0 collective-permute-done.12.refs_14_
  24.5 5.4 %shard_map.67 = (bf16[4,384,128]{2,1,0:T(8,128)(2,1)S(1)}, f32[4,24,128]{2,1,0:T(8,128)S(1)}, bf16[4,27,128,128]{3,2,1,0:T(8,128)(2,1)S(1)}, bf16[384,128]{1,0:T...) custom-call(s32[3]{0:T(128)S(1)} %pad_add_fusion.ids, ...), custom_call_target="tpu_custom_call" | custom-call | flops 5435817984 | tf_op jit(solution)/shard_map/pallas_call | solution.py:491
  29.9 1.7 %collective-permute-start.14 = (bf16[384,128]{1,0:T(8,128)(2,1)S(1)}, bf16[384,128]{1,0:T(8,128)(2,1)S(1)}, u32[]{:S(2)}, u32[]{:S(2)}) collective-permute-start(bf16[384,128]{1,0:T(8,128)(2,1)S(1)} %get-tuple-element.41), channel_id=1, source_target_pairs={{0,8},{8,0},{16,24},{24,16},{1,9},{9,1},{17,25},{25,17},{2,10},{10... | collective-permute-start | bytes 294920 | tf_op jit(solution)/shard_map/ppermute | solution.py:35
  31.6 1.8 %collective-permute-start.15 = (bf16[384,128]{1,0:T(8,128)(2,1)S(1)}, bf16[384,128]{1,0:T(8,128)(2,1)S(1)}, u32[]{:S(2)}, u32[]{:S(2)}) collective-permute-start(bf16[384,128]{1,0:T(8,128)(2,1)S(1)} %get-tuple-element.42), channel_id=1, source_target_pairs={{0,16},{8,24},{16,0},{24,8},{1,17},{9,25},{17,1},{25,9},{2,18},{10... | collective-permute-start | bytes 294920 | tf_op jit(solution)/shard_map/ppermute | solution.py:35
  33.4 0.1 collective-permute-start.16
  33.4 3.4 %shard_map.70 = (bf16[384,128]{1,0:T(8,128)(2,1)S(1)}, bf16[384,128]{1,0:T(8,128)(2,1)S(1)}, bf16[384,128]{1,0:T(8,128)(2,1)S(1)}, bf16[384,128]{1,0:T(8,128)(2,1)S(1)}) custom-call(s32[3]{0:T(128)S(1)} %pad_add_fusion.ids, bf16[4,384,128]{2,1,0:T(8,128)(2,1)S(1)} %get-tuple-element.49.outs, bf16[384,128]{1,0:T(8,128)(2,1)S(1)} %get-tuple-element.50.grad_ref, ...), custom_call_target="tpu_custom_call" | custom-call | flops 4076863488 | tf_op jit(solution)/shard_map/pallas_call | solution.py:513
  36.9 2.9 %collective-permute-start.17 = (bf16[384,128]{1,0:T(8,128)(2,1)S(1)}, bf16[384,128]{1,0:T(8,128)(2,1)S(1)}, u32[]{:S(2)}, u32[]{:S(2)}) collective-permute-start(bf16[384,128]{1,0:T(8,128)(2,1)S(1)} %get-tuple-element.52), channel_id=1, source_target_pairs={{0,24},{8,16},{16,8},{24,0},{1,25},{9,17},{17,9},{25,1},{2,26},{10... | collective-permute-start | bytes 294920 | tf_op jit(solution)/shard_map/ppermute | solution.py:35
  39.8 0.3 collective-permute-start.18
  40.1 0.0 collective-permute-done.14.refs_1_
  40.1 0.4 collective-permute-start.19
  40.4 0.0 collective-permute-done.15.refs_2_.refs_0_
  40.5 0.0 collective-permute-done.16.refs_3_.refs_1_
  40.5 1.4 %shard_map.68 = (bf16[384,1536]{1,0:T(8,128)(2,1)S(1)}, f32[4,24,128]{2,1,0:T(8,128)S(1)}) custom-call(s32[3]{0:T(128)S(1)} %pad_add_fusion.ids, f32[4,24,128]{2,1,0:T(8,128)S(1)} %get-tuple-element.39.unit_stats.stats, bf16[384,128]{1,0:T(8,128)(2,1)S(1)} %get-tuple-element.40.refs_0_, bf16[384,128]{1,0:T(8,128)(2,1)S(1)} %collective-permute-done.14.refs_1_, ...), custom_call_target="tpu_custom_call" | custom-call | flops 1358954496 | tf_op jit(solution)/shard_map/pallas_call | solution.py:523
  41.9 1.8 %shard_map.69 = (bf16[384,128]{1,0:T(8,128)(2,1)S(1)}, bf16[384,128]{1,0:T(8,128)(2,1)S(1)}) custom-call(s32[3]{0:T(128)S(1)} %pad_add_fusion.ids, f32[4,24,128]{2,1,0:T(8,128)S(1)} %get-tuple-element.45.stats, bf16[27,128,128]{2,1,0:T(8,128)(2,1)S(1)} %bitcast.33, bf16[384,128]{1,0:T(8,128)(2,1)S(1)} %get-tuple-element.40.refs_0_, ...), custom_call_target="tpu_custom_call" | custom-call | flops 2717908992 | tf_op jit(solution)/shard_map/pallas_call | solution.py:533
  43.7 0.0 collective-permute-done.17.refs_0_.refs_7_
  43.7 0.8 %collective-permute-done.18.refs_1_.refs_6_ = bf16[384,128]{1,0:T(8,128)(2,1)S(1)} collective-permute-done((bf16[384,128]{1,0:T(8,128)(2,1)S(1)}, bf16[384,128]{1,0:T(8,128)(2,1)S(1)}, u32[]{:S(2)}, u32[]{:S(2)}) %collective-permute-start.18) | collective-permute-done | bytes 98336 | tf_op jit(solution)/shard_map/ppermute | solution.py:35
  44.6 0.1 collective-permute-done.19.refs_2_.refs_5_
  44.7 1.8 %shard_map.71 = (bf16[3072,384]{1,0:T(8,128)(2,1)S(1)}, bf16[2,432,128]{2,1,0:T(8,128)(2,1)S(1)}, bf16[2,432,128]{2,1,0:T(8,128)(2,1)S(1)}) custom-call(s32[3]{0:T(128)S(1)} %pad_add_fusion.ids, bf16[384,1536]{1,0:T(8,128)(2,1)S(1)} %get-tuple-element.48.turned, bf16[384,128]{1,0:T(8,128)(2,1)S(1)} %collective-permute-done.17.refs_0_.refs_7_, ...), custom_call_target="tpu_custom_call" | custom-call | flops 679477248 | tf_op jit(solution)/shard_map/pallas_call | solution.py:571
  46.5 0.1 collective-permute-start.20
  46.6 1.3 %shard_map.72 = (bf16[2,432,128]{2,1,0:T(8,128)(2,1)S(1)}, bf16[2,432,128]{2,1,0:T(8,128)(2,1)S(1)}) custom-call(s32[3]{0:T(128)S(1)} %pad_add_fusion.ids, bf16[384,1536]{1,0:T(8,128)(2,1)S(1)} %get-tuple-element.48.turned, bf16[3072,384]{1,0:T(8,128)(2,1)S(1)} %get-tuple-element.56.refs_0_), custom_call_target="tpu_custom_call" | custom-call | flops 679477248 | tf_op jit(solution)/shard_map/pallas_call | solution.py:580
  48.0 0.1 collective-permute-done.20.got
  48.1 0.5 collective-permute-start.21
  48.5 0.6 shard_map.76
  49.1 2.7 %collective-permute-start.22 = (bf16[432,128]{1,0:T(8,128)(2,1)S(1)}, bf16[432,128]{1,0:T(8,128)(2,1)S(1)}, u32[]{:S(2)}, u32[]{:S(2)}) collective-permute-start(bf16[432,128]{1,0:T(8,128)(2,1)S(1)} %get-tuple-element.68), channel_id=1, source_target_pairs={{0,4},{1,5},{2,6},{3,7},{4,0},{5,1},{6,2},{7,3},{8,12},{9,13},{10,... | collective-permute-start | bytes 331784 | tf_op jit(solution)/shard_map/ppermute | solution.py:35
  51.8 1.3 %collective-permute-start.23 = (bf16[432,128]{1,0:T(8,128)(2,1)S(1)}, bf16[432,128]{1,0:T(8,128)(2,1)S(1)}, u32[]{:S(2)}, u32[]{:S(2)}) collective-permute-start(bf16[432,128]{1,0:T(8,128)(2,1)S(1)} %get-tuple-element.69), channel_id=1, source_target_pairs={{0,6},{1,7},{2,4},{3,5},{4,2},{5,3},{6,0},{7,1},{8,14},{9,15},{10,... | collective-permute-start | bytes 331784 | tf_op jit(solution)/shard_map/ppermute | solution.py:35
  53.1 0.6 shard_map.73
  53.8 0.3 collective-permute-start.24
  54.1 4.0 %shard_map.75 = bf16[4,384,128]{2,1,0:T(8,128)(2,1)} custom-call(s32[3]{0:T(128)S(1)} %pad_add_fusion.ids, f32[4,24,128]{2,1,0:T(8,128)S(1)} %get-tuple-element.45.stats, bf16[27,128,128]{2,1,0:T(8,128)(2,1)S(1)} %bitcast.34, bf16[384,128]{1,0:T(8,128)(2,1)S(1)} %get-tuple-element.40.refs_0_, bf16[384,128]{1,0:T(8,128)(2,1)S(1)} %collective-permute-done.14.refs_1_, ...), custom_call_target="tpu_custom_call" | custom-call | flops 5435817984 | tf_op jit(solution)/shard_map/pallas_call | solution.py:544
  58.0 2.6 %shard_map.74 = bf16[4,384,128]{2,1,0:T(8,128)(2,1)} custom-call(s32[3]{0:T(128)S(1)} %pad_add_fusion.ids, f32[4,24,128]{2,1,0:T(8,128)S(1)} %get-tuple-element.45.stats, bf16[27,128,128]{2,1,0:T(8,128)(2,1)S(1)} %bitcast.35, bf16[384,128]{1,0:T(8,128)(2,1)S(1)} %collective-permute-done.15.refs_2_.refs_0_, ...), custom_call_target="tpu_custom_call" | custom-call | flops 2717908992 | tf_op jit(solution)/shard_map/pallas_call | solution.py:533
  60.6 0.2 collective-permute-done.22.refs_0_
  60.8 1.1 %collective-permute-done.24.refs_2_ = bf16[432,128]{1,0:T(8,128)(2,1)S(1)} collective-permute-done((bf16[432,128]{1,0:T(8,128)(2,1)S(1)}, bf16[432,128]{1,0:T(8,128)(2,1)S(1)}, u32[]{:S(2)}, u32[]{:S(2)}) %collective-permute-start.24) | collective-permute-done | bytes 110624 | tf_op jit(solution)/shard_map/ppermute | solution.py:35
  61.9 0.7 %shard_map.77 = f32[432,128]{1,0:T(8,128)} custom-call(f32[432,128]{1,0:T(8,128)S(1)} %get-tuple-element.65.own, bf16[432,128]{1,0:T(8,128)(2,1)S(1)} %collective-permute-done.22.refs_0_, bf16[432,128]{1,0:T(8,128)(2,1)S(1)} %collective-permute-done.23.refs_1_, bf16[432,128]{1,0:T(8,128)(2,1)S(1)} %collective-permute-done.24.refs_2_), custom_call_target="tpu_custom_call" | custom-call | tf_op jit(solution)/shard_map/pallas_call | solution.py:615
  (6 shorter events, 0.0 us)
Async XLA Ops:
  2.5 9.4 %collective-permute-start = (bf16[28,32,128]{2,1,0:T(8,128)(2,1)S(1)}, bf16[28,32,128]{2,1,0:T(8,128)(2,1)S(1)}, u32[]{:S(2)}, u32[]{:S(2)}) collective-permute-start(bf16[28,32,128]{2,1,0:T(8,128)(2,1)S(1)} %fusion.refs_0_), channel_id=1, source_target_pairs={{0,8},{8,0},{16,24},{24,16},{1,9},{9,1},{17,25},{25,17},{2,10},{10... | collective-permute-start | bytes 688136 | tf_op jit(solution)/shard_map/ppermute | solution.py:35
  5.5 8.4 %collective-permute-start.7 = (bf16[27,32,128]{2,1,0:T(8,128)(2,1)S(1)}, bf16[27,32,128]{2,1,0:T(8,128)(2,1)S(1)}, u32[]{:S(2)}, u32[]{:S(2)}) collective-permute-start(bf16[27,32,128]{2,1,0:T(8,128)(2,1)S(1)} %get-tuple-element.74.refs_1_), channel_id=1, source_target_pairs={{0,16},{8,24},{16,0},{24,8},{1,17},{9,25},{17,1},{25,9},{2,18},{10... | collective-permute-start | bytes 663560 | tf_op jit(solution)/shard_map/ppermute | solution.py:35
  7.1 8.8 %collective-permute-start.3 = (bf16[27,32,128]{2,1,0:T(8,128)(2,1)S(1)}, bf16[27,32,128]{2,1,0:T(8,128)(2,1)S(1)}, u32[]{:S(2)}, u32[]{:S(2)}) collective-permute-start(bf16[27,32,128]{2,1,0:T(8,128)(2,1)S(1)} %get-tuple-element.74.refs_1_), channel_id=1, source_target_pairs={{0,8},{8,0},{16,24},{24,16},{1,9},{9,1},{17,25},{25,17},{2,10},{10... | collective-permute-start | bytes 663560 | tf_op jit(solution)/shard_map/ppermute | solution.py:35
  7.6 10.0 %collective-permute-start.2 = (bf16[27,32,128]{2,1,0:T(8,128)(2,1)S(1)}, bf16[27,32,128]{2,1,0:T(8,128)(2,1)S(1)}, u32[]{:S(2)}, u32[]{:S(2)}) collective-permute-start(bf16[27,32,128]{2,1,0:T(8,128)(2,1)S(1)} %get-tuple-element.74.refs_1_), channel_id=1, source_target_pairs={{0,1},{1,0},{2,3},{3,2},{4,5},{5,4},{6,7},{7,6},{8,9},{9,8},{10,11... | collective-permute-start | bytes 663560 | tf_op jit(solution)/shard_map/ppermute | solution.py:35
  7.6 11.2 %collective-permute-start.6 = (bf16[28,32,128]{2,1,0:T(8,128)(2,1)S(1)}, bf16[28,32,128]{2,1,0:T(8,128)(2,1)S(1)}, u32[]{:S(2)}, u32[]{:S(2)}) collective-permute-start(bf16[28,32,128]{2,1,0:T(8,128)(2,1)S(1)} %fusion.refs_0_), channel_id=1, source_target_pairs={{0,16},{8,24},{16,0},{24,8},{1,17},{9,25},{17,1},{25,9},{2,18},{10... | collective-permute-start | bytes 688136 | tf_op jit(solution)/shard_map/ppermute | solution.py:35
  12.0 6.8 %collective-permute-start.1 = (bf16[28,32,128]{2,1,0:T(8,128)(2,1)S(1)}, bf16[28,32,128]{2,1,0:T(8,128)(2,1)S(1)}, u32[]{:S(2)}, u32[]{:S(2)}) collective-permute-start(bf16[28,32,128]{2,1,0:T(8,128)(2,1)S(1)} %fusion.refs_0_), channel_id=1, source_target_pairs={{0,1},{1,0},{2,3},{3,2},{4,5},{5,4},{6,7},{7,6},{8,9},{9,8},{10,11... | collective-permute-start | bytes 688136 | tf_op jit(solution)/shard_map/ppermute | solution.py:35
  13.9 8.4 %collective-permute-start.10 = (bf16[28,32,128]{2,1,0:T(8,128)(2,1)S(1)}, bf16[28,32,128]{2,1,0:T(8,128)(2,1)S(1)}, u32[]{:S(2)}, u32[]{:S(2)}) collective-permute-start(bf16[28,32,128]{2,1,0:T(8,128)(2,1)S(1)} %collective-permute-done.refs_4_), channel_id=1, source_target_pairs={{0,16},{8,24},{16,0},{24,8},{1,17},{9,25},{17,1},{25,9},{2,18},{10... | collective-permute-start | bytes 688136 | tf_op jit(solution)/shard_map/ppermute | solution.py:35
  15.9 6.6 %collective-permute-start.11 = (bf16[27,32,128]{2,1,0:T(8,128)(2,1)S(1)}, bf16[27,32,128]{2,1,0:T(8,128)(2,1)S(1)}, u32[]{:S(2)}, u32[]{:S(2)}) collective-permute-start(bf16[27,32,128]{2,1,0:T(8,128)(2,1)S(1)} %collective-permute-done.7.refs_9_), channel_id=1, source_target_pairs={{0,8},{8,0},{16,24},{24,16},{1,9},{9,1},{17,25},{25,17},{2,10},{10... | collective-permute-start | bytes 663560 | tf_op jit(solution)/shard_map/ppermute | solution.py:35
  17.6 5.1 %collective-permute-start.9 = (bf16[27,32,128]{2,1,0:T(8,128)(2,1)S(1)}, bf16[27,32,128]{2,1,0:T(8,128)(2,1)S(1)}, u32[]{:S(2)}, u32[]{:S(2)}) collective-permute-start(bf16[27,32,128]{2,1,0:T(8,128)(2,1)S(1)} %collective-permute-done.7.refs_9_), channel_id=1, source_target_pairs={{0,1},{1,0},{2,3},{3,2},{4,5},{5,4},{6,7},{7,6},{8,9},{9,8},{10,11... | collective-permute-start | bytes 663560 | tf_op jit(solution)/shard_map/ppermute | solution.py:35
  18.8 5.4 %collective-permute-start.8 = (bf16[28,32,128]{2,1,0:T(8,128)(2,1)S(1)}, bf16[28,32,128]{2,1,0:T(8,128)(2,1)S(1)}, u32[]{:S(2)}, u32[]{:S(2)}) collective-permute-start(bf16[28,32,128]{2,1,0:T(8,128)(2,1)S(1)} %collective-permute-done.6.refs_8_), channel_id=1, source_target_pairs={{0,1},{1,0},{2,3},{3,2},{4,5},{5,4},{6,7},{7,6},{8,9},{9,8},{10,11... | collective-permute-start | bytes 688136 | tf_op jit(solution)/shard_map/ppermute | solution.py:35
  18.8 5.4 %collective-permute-start.4 = (bf16[28,32,128]{2,1,0:T(8,128)(2,1)S(1)}, bf16[28,32,128]{2,1,0:T(8,128)(2,1)S(1)}, u32[]{:S(2)}, u32[]{:S(2)}) collective-permute-start(bf16[28,32,128]{2,1,0:T(8,128)(2,1)S(1)} %collective-permute-done.refs_4_), channel_id=1, source_target_pairs={{0,1},{1,0},{2,3},{3,2},{4,5},{5,4},{6,7},{7,6},{8,9},{9,8},{10,11... | collective-permute-start | bytes 688136 | tf_op jit(solution)/shard_map/ppermute | solution.py:35
  22.3 2.3 %collective-permute-start.12 = (bf16[28,32,128]{2,1,0:T(8,128)(2,1)S(1)}, bf16[28,32,128]{2,1,0:T(8,128)(2,1)S(1)}, u32[]{:S(2)}, u32[]{:S(2)}) collective-permute-start(bf16[28,32,128]{2,1,0:T(8,128)(2,1)S(1)} %collective-permute-done.10.refs_12_), channel_id=1, source_target_pairs={{0,1},{1,0},{2,3},{3,2},{4,5},{5,4},{6,7},{7,6},{8,9},{9,8},{10,11... | collective-permute-start | bytes 688136 | tf_op jit(solution)/shard_map/ppermute | solution.py:35
  22.5 1.7 %collective-permute-start.5 = (bf16[27,32,128]{2,1,0:T(8,128)(2,1)S(1)}, bf16[27,32,128]{2,1,0:T(8,128)(2,1)}, u32[]{:S(2)}, u32[]{:S(2)}) collective-permute-start(bf16[27,32,128]{2,1,0:T(8,128)(2,1)S(1)} %collective-permute-done.3.refs_5_), channel_id=1, source_target_pairs={{0,1},{1,0},{2,3},{3,2},{4,5},{5,4},{6,7},{7,6},{8,9},{9,8},{10,11... | collective-permute-start | bytes 663560 | tf_op jit(solution)/shard_map/ppermute | solution.py:35
  22.8 1.7 %collective-permute-start.13 = (bf16[27,32,128]{2,1,0:T(8,128)(2,1)S(1)}, bf16[27,32,128]{2,1,0:T(8,128)(2,1)}, u32[]{:S(2)}, u32[]{:S(2)}) collective-permute-start(bf16[27,32,128]{2,1,0:T(8,128)(2,1)S(1)} %collective-permute-done.11.refs_13_), channel_id=1, source_target_pairs={{0,1},{1,0},{2,3},{3,2},{4,5},{5,4},{6,7},{7,6},{8,9},{9,8},{10,11... | collective-permute-start | bytes 663560 | tf_op jit(solution)/shard_map/ppermute | solution.py:35
  29.9 10.2 %collective-permute-start.14 = (bf16[384,128]{1,0:T(8,128)(2,1)S(1)}, bf16[384,128]{1,0:T(8,128)(2,1)S(1)}, u32[]{:S(2)}, u32[]{:S(2)}) collective-permute-start(bf16[384,128]{1,0:T(8,128)(2,1)S(1)} %get-tuple-element.41), channel_id=1, source_target_pairs={{0,8},{8,0},{16,24},{24,16},{1,9},{9,1},{17,25},{25,17},{2,10},{10... | collective-permute-start | bytes 294920 | tf_op jit(solution)/shard_map/ppermute | solution.py:35
  31.6 8.8 %collective-permute-start.15 = (bf16[384,128]{1,0:T(8,128)(2,1)S(1)}, bf16[384,128]{1,0:T(8,128)(2,1)S(1)}, u32[]{:S(2)}, u32[]{:S(2)}) collective-permute-start(bf16[384,128]{1,0:T(8,128)(2,1)S(1)} %get-tuple-element.42), channel_id=1, source_target_pairs={{0,16},{8,24},{16,0},{24,8},{1,17},{9,25},{17,1},{25,9},{2,18},{10... | collective-permute-start | bytes 294920 | tf_op jit(solution)/shard_map/ppermute | solution.py:35
  33.4 7.1 %collective-permute-start.16 = (bf16[384,128]{1,0:T(8,128)(2,1)S(1)}, bf16[384,128]{1,0:T(8,128)(2,1)S(1)}, u32[]{:S(2)}, u32[]{:S(2)}) collective-permute-start(bf16[384,128]{1,0:T(8,128)(2,1)S(1)} %get-tuple-element.43), channel_id=1, source_target_pairs={{0,24},{8,16},{16,8},{24,0},{1,25},{9,17},{17,9},{25,1},{2,26},{10... | collective-permute-start | bytes 294920 | tf_op jit(solution)/shard_map/ppermute | solution.py:35
  36.9 6.8 %collective-permute-start.17 = (bf16[384,128]{1,0:T(8,128)(2,1)S(1)}, bf16[384,128]{1,0:T(8,128)(2,1)S(1)}, u32[]{:S(2)}, u32[]{:S(2)}) collective-permute-start(bf16[384,128]{1,0:T(8,128)(2,1)S(1)} %get-tuple-element.52), channel_id=1, source_target_pairs={{0,24},{8,16},{16,8},{24,0},{1,25},{9,17},{17,9},{25,1},{2,26},{10... | collective-permute-start | bytes 294920 | tf_op jit(solution)/shard_map/ppermute | solution.py:35
  39.8 4.8 %collective-permute-start.18 = (bf16[384,128]{1,0:T(8,128)(2,1)S(1)}, bf16[384,128]{1,0:T(8,128)(2,1)S(1)}, u32[]{:S(2)}, u32[]{:S(2)}) collective-permute-start(bf16[384,128]{1,0:T(8,128)(2,1)S(1)} %get-tuple-element.53), channel_id=1, source_target_pairs={{0,16},{8,24},{16,0},{24,8},{1,17},{9,25},{17,1},{25,9},{2,18},{10... | collective-permute-start | bytes 294920 | tf_op jit(solution)/shard_map/ppermute | solution.py:35
  40.1 4.6 %collective-permute-start.19 = (bf16[384,128]{1,0:T(8,128)(2,1)S(1)}, bf16[384,128]{1,0:T(8,128)(2,1)S(1)}, u32[]{:S(2)}, u32[]{:S(2)}) collective-permute-start(bf16[384,128]{1,0:T(8,128)(2,1)S(1)} %get-tuple-element.54), channel_id=1, source_target_pairs={{0,8},{8,0},{16,24},{24,16},{1,9},{9,1},{17,25},{25,17},{2,10},{10... | collective-permute-start | bytes 294920 | tf_op jit(solution)/shard_map/ppermute | solution.py:35
  40.5 1.4 %copy-start = (bf16[1,3456,128]{2,1,0:T(8,128)(2,1)S(1)}, bf16[1,3456,128]{2,1,0:T(8,128)(2,1)}, u32[]{:S(2)}) copy-start(bf16[1,3456,128]{2,1,0:T(8,128)(2,1)} %param.6) | copy-start | bytes 2654212
  46.5 1.5 %collective-permute-start.20 = (bf16[2,432,128]{2,1,0:T(8,128)(2,1)S(1)}, bf16[2,432,128]{2,1,0:T(8,128)(2,1)S(1)}, u32[]{:S(2)}, u32[]{:S(2)}) collective-permute-start(bf16[2,432,128]{2,1,0:T(8,128)(2,1)S(1)} %get-tuple-element.59), channel_id=1, source_target_pairs={{0,1},{1,0},{2,3},{3,2},{4,5},{5,4},{6,7},{7,6},{8,9},{9,8},{10,11... | collective-permute-start | bytes 663560 | tf_op jit(solution)/shard_map/ppermute | solution.py:35
  48.1 5.1 %collective-permute-start.21 = (bf16[2,432,128]{2,1,0:T(8,128)(2,1)S(1)}, bf16[2,432,128]{2,1,0:T(8,128)(2,1)S(1)}, u32[]{:S(2)}, u32[]{:S(2)}) collective-permute-start(bf16[2,432,128]{2,1,0:T(8,128)(2,1)S(1)} %get-tuple-element.60), channel_id=1, source_target_pairs={{0,1},{1,0},{2,3},{3,2},{4,5},{5,4},{6,7},{7,6},{8,9},{9,8},{10,11... | collective-permute-start | bytes 663560 | tf_op jit(solution)/shard_map/ppermute | solution.py:35
  49.1 11.7 %collective-permute-start.22 = (bf16[432,128]{1,0:T(8,128)(2,1)S(1)}, bf16[432,128]{1,0:T(8,128)(2,1)S(1)}, u32[]{:S(2)}, u32[]{:S(2)}) collective-permute-start(bf16[432,128]{1,0:T(8,128)(2,1)S(1)} %get-tuple-element.68), channel_id=1, source_target_pairs={{0,4},{1,5},{2,6},{3,7},{4,0},{5,1},{6,2},{7,3},{8,12},{9,13},{10,... | collective-permute-start | bytes 331784 | tf_op jit(solution)/shard_map/ppermute | solution.py:35
  51.8 9.0 %collective-permute-start.23 = (bf16[432,128]{1,0:T(8,128)(2,1)S(1)}, bf16[432,128]{1,0:T(8,128)(2,1)S(1)}, u32[]{:S(2)}, u32[]{:S(2)}) collective-permute-start(bf16[432,128]{1,0:T(8,128)(2,1)S(1)} %get-tuple-element.69), channel_id=1, source_target_pairs={{0,6},{1,7},{2,4},{3,5},{4,2},{5,3},{6,0},{7,1},{8,14},{9,15},{10,... | collective-permute-start | bytes 331784 | tf_op jit(solution)/shard_map/ppermute | solution.py:35
  53.8 8.2 %collective-permute-start.24 = (bf16[432,128]{1,0:T(8,128)(2,1)S(1)}, bf16[432,128]{1,0:T(8,128)(2,1)S(1)}, u32[]{:S(2)}, u32[]{:S(2)}) collective-permute-start(bf16[432,128]{1,0:T(8,128)(2,1)S(1)} %get-tuple-element.70), channel_id=1, source_target_pairs={{0,2},{1,3},{2,0},{3,1},{4,6},{5,7},{6,4},{7,5},{8,10},{9,11},{10,... | collective-permute-start | bytes 331784 | tf_op jit(solution)/shard_map/ppermute | solution.py:35

commit v5 on v4

--- a/solution.py
+++ b/solution.py
@@ -179,27 +179,19 @@
 def forward_kernel(sections, dims, ids, x_ref, *refs):
     frames, rows, cols, chans = dims
     plane = rows * cols
-    n_chunk = (len(refs) - 9 - sections) // sections
+    n_chunk = (len(refs) - 7 - sections) // sections
     chunks = [refs[k * n_chunk : (k + 1) * n_chunk] for k in range(sections)]
     refs = refs[sections * n_chunk :]
     outs, stats, every = refs[:3]
     sends = refs[3 : 3 + sections]
-    spread, product, inputs, gains, gain_sem, sems = refs[3 + sections :]
+    spread, product, inputs, sems = refs[3 + sections :]
     place = ids[0]
     taps = every.shape[1]
-    copies = [
-        pltpu.make_async_copy(chunks[k][0].at[taps], gains.at[k], gain_sem.at[k])
-        for k in range(sections)
-    ]
-    for copy in copies:
-        copy.start()
-
     for k in range(sections):
         for copy in copies_of(chunks[k], piece_ids(ids, n_chunk), every.at[k], sems.at[k]):
             copy.start()
     for k in range(sections):
-        copies[k].wait()
-        parts = gains[k].astype(F32)
+        parts = chunks[k][0][taps].astype(F32)
         stats[place ^ k, 16:24] = full(parts[0:1] + parts[1:2] + parts[2:3], 8)
     x = x_ref[...]
     for unit in range(sections):
@@ -496,14 +488,12 @@
             jax.ShapeDtypeStruct((sections, 27, chans, chans), BF),
         ]
         + [act_shape] * sections,
-        [SM, VM] + [ANY] * len(flat),
+        [SM, VM] + [ANY if i % n_chunk else VM for i in range(len(flat))],
         [VM] * (3 + sections),
         [
             spread(1),
             product,
             pltpu.VMEM((sections, points, chans), BF),
-            pltpu.VMEM((sections, quarter, chans), BF),
-            pltpu.SemaphoreType.DMA((sections,)),
             pltpu.SemaphoreType.DMA((sections,)),
         ],
         flops=4 * sections * unit_flops,

time: 62.8 us -> 62.7 us (level)
  no operation moved by 1% of the time
where the time goes in v5:
time: 62.7 us; the launch traced here: 62.6 us
  Pallas kernels  23.6 us (38%)
  starting transfers between devices  21.4 us (34%)
  waiting for transfers between devices  13.9 us (22%)
  local copies, waits for them, and re-layouts  2.03 us (3%)
  other arithmetic  0.86 us (1%)
  between operations  0.78 us (1%)
    ppermute x25, starting transfers between devices, swap(): return lax.ppermute(value, axis, [(i, i ^ bits) for i in range(count)])  21.4 us
    ppermute x25, waiting for transfers between devices, swap(): return lax.ppermute(value, axis, [(i, i ^ bits) for i in range(count)])  13.9 us
    pallas_call x1, Pallas kernels, body(): call(functools.partial(forward_kernel, sections, dims), [jax.ShapeDtypeSt...  5.26 us
    pallas_call x2, Pallas kernels, home_forward(): call(functools.partial(home_forward_kernel, dims, n, first, last), [jax.S...  4.38 us
    pallas_call x1, Pallas kernels, home_backward(): call(functools.partial(home_backward_kernel, dims, n, first, last), [jax....  3.96 us
    pallas_call x1, Pallas kernels, body(): call(functools.partial(backward_kernel, sections, dims), [act_shape] * se...  3.43 us
    pallas_call x1, Pallas kernels, body(): call(functools.partial(half_kernel, dims, n, True, levels), [right_shape]...  1.83 us
    pallas_call x1, Pallas kernels, body(): call(functools.partial(turn_kernel, dims, n), [jax.ShapeDtypeStruct((3 *...  1.42 us
  transfers between devices with their start and end apart: 25, of which 13 were waited for; matrix products, arithmetic and copies ran while one was open for 2% of the time, Pallas kernels for 25%

profile of v5, /device:TPU:0, one launch (start us, length us, event | category | flops | bytes accessed | tf_op | source)
XLA Modules:
  0.0 62.6 jit_solution(2950797127874339586)
XLA Ops:
  0.7 0.7 %reduce-precision_bitcast_fusion.1 = (bf16[128]{0:T(256)(128)(2,1)S(1)}, bf16[128]{0:T(256)(128)(2,1)S(1)}, bf16[128]{0:T(256)(128)(2,1)S(1)}) fusion(f32[1,128]{1,0:T(1,128)} %param.7), kind=kLoop, calls=%fused_computation.9 | loop fusion | flops 896 | bytes 1280 | tf_op jit(solution)/shard_map/jit(_where)/broadcast_in_dim | solution.py:426
  1.3 1.1 %dynamic-slice_bitcast_fusion = (bf16[27,32,128]{2,1,0:T(8,128)(2,1)S(1)}, bf16[27,32,128]{2,1,0:T(8,128)(2,1)S(1)}) fusion(bf16[27,4,32,128]{3,2,1,0:T(8,128)(2,1)} %bitcast.32, s32[]{:T(128)S(6)} %select_n.29, s32[]{:T(128)S(6)} %select_n.24), kind=kLoop, calls=%fused_computation.2 | loop fusion | bytes 884744 | tf_op jit(solution)/shard_map/jit(dynamic_index_in_dim)/squeeze | solution.py:465
  2.4 0.1 fusion.refs_0_
  2.5 3.0 %collective-permute-start = (bf16[28,32,128]{2,1,0:T(8,128)(2,1)S(1)}, bf16[28,32,128]{2,1,0:T(8,128)(2,1)S(1)}, u32[]{:S(2)}, u32[]{:S(2)}) collective-permute-start(bf16[28,32,128]{2,1,0:T(8,128)(2,1)S(1)} %fusion.refs_0_), channel_id=1, source_target_pairs={{0,8},{8,0},{16,24},{24,16},{1,9},{9,1},{17,25},{25,17},{2,10},{10... | collective-permute-start | bytes 688136 | tf_op jit(solution)/shard_map/ppermute | solution.py:35
  5.5 1.5 %collective-permute-start.7 = (bf16[27,32,128]{2,1,0:T(8,128)(2,1)S(1)}, bf16[27,32,128]{2,1,0:T(8,128)(2,1)S(1)}, u32[]{:S(2)}, u32[]{:S(2)}) collective-permute-start(bf16[27,32,128]{2,1,0:T(8,128)(2,1)S(1)} %get-tuple-element.74.refs_1_), channel_id=1, source_target_pairs={{0,16},{8,24},{16,0},{24,8},{1,17},{9,25},{17,1},{25,9},{2,18},{10... | collective-permute-start | bytes 663560 | tf_op jit(solution)/shard_map/ppermute | solution.py:35
  7.1 0.5 collective-permute-start.3
  7.6 0.0 collective-permute-start.2
  7.6 0.1 collective-permute-start.6
  7.6 1.0 %dynamic-slice_bitcast_fusion.2 = (bf16[384,128]{1,0:T(8,128)(2,1)S(1)}, bf16[384,128]{1,0:T(8,128)(2,1)S(1)}) fusion(bf16[4,384,128]{2,1,0:T(8,128)(2,1)} %bitcast.37, s32[]{:T(128)S(6)} %select_n.28, bf16[4,384,128]{2,1,0:T(8,128)(2,1)} %bitcast.38), kind=kLoop, calls=%fused_computation.4 | loop fusion | bytes 393220 | tf_op jit(solution)/shard_map/jit(dynamic_index_in_dim)/squeeze | solution.py:468
  8.6 3.4 %collective-permute-done.refs_4_ = bf16[28,32,128]{2,1,0:T(8,128)(2,1)S(1)} collective-permute-done((bf16[28,32,128]{2,1,0:T(8,128)(2,1)S(1)}, bf16[28,32,128]{2,1,0:T(8,128)(2,1)S(1)}, u32[]{:S(2)}, u32[]{:S(2)}) %collective-permute-start) | collective-permute-done | bytes 229408 | tf_op jit(solution)/shard_map/ppermute | solution.py:35
  12.0 0.0 collective-permute-start.1
  12.0 1.9 %collective-permute-done.7.refs_9_ = bf16[27,32,128]{2,1,0:T(8,128)(2,1)S(1)} collective-permute-done((bf16[27,32,128]{2,1,0:T(8,128)(2,1)S(1)}, bf16[27,32,128]{2,1,0:T(8,128)(2,1)S(1)}, u32[]{:S(2)}, u32[]{:S(2)}) %collective-permute-start.7) | collective-permute-done | bytes 221216 | tf_op jit(solution)/shard_map/ppermute | solution.py:35
  13.9 1.5 %collective-permute-start.10 = (bf16[28,32,128]{2,1,0:T(8,128)(2,1)S(1)}, bf16[28,32,128]{2,1,0:T(8,128)(2,1)S(1)}, u32[]{:S(2)}, u32[]{:S(2)}) collective-permute-start(bf16[28,32,128]{2,1,0:T(8,128)(2,1)S(1)} %collective-permute-done.refs_4_), channel_id=1, source_target_pairs={{0,16},{8,24},{16,0},{24,8},{1,17},{9,25},{17,1},{25,9},{2,18},{10... | collective-permute-start | bytes 688136 | tf_op jit(solution)/shard_map/ppermute | solution.py:35
  15.4 0.5 collective-permute-done.3.refs_5_
  15.9 1.7 %collective-permute-start.11 = (bf16[27,32,128]{2,1,0:T(8,128)(2,1)S(1)}, bf16[27,32,128]{2,1,0:T(8,128)(2,1)S(1)}, u32[]{:S(2)}, u32[]{:S(2)}) collective-permute-start(bf16[27,32,128]{2,1,0:T(8,128)(2,1)S(1)} %collective-permute-done.7.refs_9_), channel_id=1, source_target_pairs={{0,8},{8,0},{16,24},{24,16},{1,9},{9,1},{17,25},{25,17},{2,10},{10... | collective-permute-start | bytes 663560 | tf_op jit(solution)/shard_map/ppermute | solution.py:35
  17.6 0.0 collective-permute-done.2.refs_3_
  17.6 0.0 collective-permute-start.9
  17.6 1.2 %collective-permute-done.6.refs_8_ = bf16[28,32,128]{2,1,0:T(8,128)(2,1)S(1)} collective-permute-done((bf16[28,32,128]{2,1,0:T(8,128)(2,1)S(1)}, bf16[28,32,128]{2,1,0:T(8,128)(2,1)S(1)}, u32[]{:S(2)}, u32[]{:S(2)}) %collective-permute-start.6) | collective-permute-done | bytes 229408 | tf_op jit(solution)/shard_map/ppermute | solution.py:35
  18.8 0.0 collective-permute-start.8
  18.8 0.0 collective-permute-done.1.refs_2_
  18.8 0.5 collective-permute-start.4
  19.3 2.9 %collective-permute-done.10.refs_12_ = bf16[28,32,128]{2,1,0:T(8,128)(2,1)S(1)} collective-permute-done((bf16[28,32,128]{2,1,0:T(8,128)(2,1)S(1)}, bf16[28,32,128]{2,1,0:T(8,128)(2,1)S(1)}, u32[]{:S(2)}, u32[]{:S(2)}) %collective-permute-start.10) | collective-permute-done | bytes 229408 | tf_op jit(solution)/shard_map/ppermute | solution.py:35
  22.3 0.0 collective-permute-start.12
  22.3 0.2 collective-permute-done.11.refs_13_
  22.5 0.3 collective-permute-start.5
  22.8 0.0 collective-permute-done.9.refs_11_
  22.8 0.2 collective-permute-start.13
  23.0 0.1 pad_add_fusion.ids
  23.1 1.1 %collective-permute-done.5.refs_7_ = bf16[27,32,128]{2,1,0:T(8,128)(2,1)} collective-permute-done((bf16[27,32,128]{2,1,0:T(8,128)(2,1)S(1)}, bf16[27,32,128]{2,1,0:T(8,128)(2,1)}, u32[]{:S(2)}, u32[]{:S(2)}) %collective-permute-start.5) | collective-permute-done | bytes 221216 | tf_op jit(solution)/shard_map/ppermute | solution.py:35
  24.2 0.0 collective-permute-done.8.refs_10_
  24.2 0.0 collective-permute-done.4.refs_6_
  24.2 0.3 collective-permute-done.13.refs_15_
  24.5 0.0 collective-permute-done.12.refs_14_
  24.5 5.3 %shard_map.67 = (bf16[4,384,128]{2,1,0:T(8,128)(2,1)S(1)}, f32[4,24,128]{2,1,0:T(8,128)S(1)}, bf16[4,27,128,128]{3,2,1,0:T(8,128)(2,1)S(1)}, bf16[384,128]{1,0:T...) custom-call(s32[3]{0:T(128)S(1)} %pad_add_fusion.ids, ...), custom_call_target="tpu_custom_call" | custom-call | flops 5435817984 | tf_op jit(solution)/shard_map/pallas_call | solution.py:483
  29.8 1.7 %collective-permute-start.14 = (bf16[384,128]{1,0:T(8,128)(2,1)S(1)}, bf16[384,128]{1,0:T(8,128)(2,1)S(1)}, u32[]{:S(2)}, u32[]{:S(2)}) collective-permute-start(bf16[384,128]{1,0:T(8,128)(2,1)S(1)} %get-tuple-element.41), channel_id=1, source_target_pairs={{0,8},{8,0},{16,24},{24,16},{1,9},{9,1},{17,25},{25,17},{2,10},{10... | collective-permute-start | bytes 294920 | tf_op jit(solution)/shard_map/ppermute | solution.py:35
  31.5 1.8 %collective-permute-start.15 = (bf16[384,128]{1,0:T(8,128)(2,1)S(1)}, bf16[384,128]{1,0:T(8,128)(2,1)S(1)}, u32[]{:S(2)}, u32[]{:S(2)}) collective-permute-start(bf16[384,128]{1,0:T(8,128)(2,1)S(1)} %get-tuple-element.42), channel_id=1, source_target_pairs={{0,16},{8,24},{16,0},{24,8},{1,17},{9,25},{17,1},{25,9},{2,18},{10... | collective-permute-start | bytes 294920 | tf_op jit(solution)/shard_map/ppermute | solution.py:35
  33.3 0.0 collective-permute-start.16
  33.3 3.4 %shard_map.70 = (bf16[384,128]{1,0:T(8,128)(2,1)S(1)}, bf16[384,128]{1,0:T(8,128)(2,1)S(1)}, bf16[384,128]{1,0:T(8,128)(2,1)S(1)}, bf16[384,128]{1,0:T(8,128)(2,1)S(1)}) custom-call(s32[3]{0:T(128)S(1)} %pad_add_fusion.ids, bf16[4,384,128]{2,1,0:T(8,128)(2,1)S(1)} %get-tuple-element.49.outs, bf16[384,128]{1,0:T(8,128)(2,1)S(1)} %get-tuple-element.50.grad_ref, ...), custom_call_target="tpu_custom_call" | custom-call | flops 4076863488 | tf_op jit(solution)/shard_map/pallas_call | solution.py:503
  36.8 3.0 %collective-permute-start.17 = (bf16[384,128]{1,0:T(8,128)(2,1)S(1)}, bf16[384,128]{1,0:T(8,128)(2,1)S(1)}, u32[]{:S(2)}, u32[]{:S(2)}) collective-permute-start(bf16[384,128]{1,0:T(8,128)(2,1)S(1)} %get-tuple-element.52), channel_id=1, source_target_pairs={{0,24},{8,16},{16,8},{24,0},{1,25},{9,17},{17,9},{25,1},{2,26},{10... | collective-permute-start | bytes 294920 | tf_op jit(solution)/shard_map/ppermute | solution.py:35
  39.7 0.2 collective-permute-start.18
  40.0 0.0 collective-permute-done.14.refs_1_
  40.0 0.4 collective-permute-start.19
  40.4 0.0 collective-permute-done.15.refs_2_.refs_0_
  40.4 0.0 collective-permute-done.16.refs_3_.refs_1_
  40.4 1.4 %shard_map.68 = (bf16[384,1536]{1,0:T(8,128)(2,1)S(1)}, f32[4,24,128]{2,1,0:T(8,128)S(1)}) custom-call(s32[3]{0:T(128)S(1)} %pad_add_fusion.ids, f32[4,24,128]{2,1,0:T(8,128)S(1)} %get-tuple-element.39.unit_stats.stats, bf16[384,128]{1,0:T(8,128)(2,1)S(1)} %get-tuple-element.40.refs_0_, bf16[384,128]{1,0:T(8,128)(2,1)S(1)} %collective-permute-done.14.refs_1_, ...), custom_call_target="tpu_custom_call" | custom-call | flops 1358954496 | tf_op jit(solution)/shard_map/pallas_call | solution.py:513
  41.8 1.8 %shard_map.69 = (bf16[384,128]{1,0:T(8,128)(2,1)S(1)}, bf16[384,128]{1,0:T(8,128)(2,1)S(1)}) custom-call(s32[3]{0:T(128)S(1)} %pad_add_fusion.ids, f32[4,24,128]{2,1,0:T(8,128)S(1)} %get-tuple-element.45.stats, bf16[27,128,128]{2,1,0:T(8,128)(2,1)S(1)} %bitcast.33, bf16[384,128]{1,0:T(8,128)(2,1)S(1)} %get-tuple-element.40.refs_0_, ...), custom_call_target="tpu_custom_call" | custom-call | flops 2717908992 | tf_op jit(solution)/shard_map/pallas_call | solution.py:523
  43.7 0.0 collective-permute-done.17.refs_0_.refs_7_
  43.7 0.8 %collective-permute-done.18.refs_1_.refs_6_ = bf16[384,128]{1,0:T(8,128)(2,1)S(1)} collective-permute-done((bf16[384,128]{1,0:T(8,128)(2,1)S(1)}, bf16[384,128]{1,0:T(8,128)(2,1)S(1)}, u32[]{:S(2)}, u32[]{:S(2)}) %collective-permute-start.18) | collective-permute-done | bytes 98336 | tf_op jit(solution)/shard_map/ppermute | solution.py:35
  44.5 0.1 collective-permute-done.19.refs_2_.refs_5_
  44.6 1.8 %shard_map.71 = (bf16[3072,384]{1,0:T(8,128)(2,1)S(1)}, bf16[2,432,128]{2,1,0:T(8,128)(2,1)S(1)}, bf16[2,432,128]{2,1,0:T(8,128)(2,1)S(1)}) custom-call(s32[3]{0:T(128)S(1)} %pad_add_fusion.ids, bf16[384,1536]{1,0:T(8,128)(2,1)S(1)} %get-tuple-element.48.turned, bf16[384,128]{1,0:T(8,128)(2,1)S(1)} %collective-permute-done.17.refs_0_.refs_7_, ...), custom_call_target="tpu_custom_call" | custom-call | flops 679477248 | tf_op jit(solution)/shard_map/pallas_call | solution.py:561
  46.4 0.1 collective-permute-start.20
  46.5 1.3 %shard_map.72 = (bf16[2,432,128]{2,1,0:T(8,128)(2,1)S(1)}, bf16[2,432,128]{2,1,0:T(8,128)(2,1)S(1)}) custom-call(s32[3]{0:T(128)S(1)} %pad_add_fusion.ids, bf16[384,1536]{1,0:T(8,128)(2,1)S(1)} %get-tuple-element.48.turned, bf16[3072,384]{1,0:T(8,128)(2,1)S(1)} %get-tuple-element.56.refs_0_), custom_call_target="tpu_custom_call" | custom-call | flops 679477248 | tf_op jit(solution)/shard_map/pallas_call | solution.py:570
  47.9 0.1 collective-permute-done.20.got
  48.0 0.5 collective-permute-start.21
  48.4 0.6 shard_map.76
  49.0 2.7 %collective-permute-start.22 = (bf16[432,128]{1,0:T(8,128)(2,1)S(1)}, bf16[432,128]{1,0:T(8,128)(2,1)S(1)}, u32[]{:S(2)}, u32[]{:S(2)}) collective-permute-start(bf16[432,128]{1,0:T(8,128)(2,1)S(1)} %get-tuple-element.68), channel_id=1, source_target_pairs={{0,4},{1,5},{2,6},{3,7},{4,0},{5,1},{6,2},{7,3},{8,12},{9,13},{10,... | collective-permute-start | bytes 331784 | tf_op jit(solution)/shard_map/ppermute | solution.py:35
  51.7 1.3 %collective-permute-start.23 = (bf16[432,128]{1,0:T(8,128)(2,1)S(1)}, bf16[432,128]{1,0:T(8,128)(2,1)S(1)}, u32[]{:S(2)}, u32[]{:S(2)}) collective-permute-start(bf16[432,128]{1,0:T(8,128)(2,1)S(1)} %get-tuple-element.69), channel_id=1, source_target_pairs={{0,6},{1,7},{2,4},{3,5},{4,2},{5,3},{6,0},{7,1},{8,14},{9,15},{10,... | collective-permute-start | bytes 331784 | tf_op jit(solution)/shard_map/ppermute | solution.py:35
  53.0 0.6 shard_map.73
  53.7 0.3 collective-permute-start.24
  54.0 4.0 %shard_map.75 = bf16[4,384,128]{2,1,0:T(8,128)(2,1)} custom-call(s32[3]{0:T(128)S(1)} %pad_add_fusion.ids, f32[4,24,128]{2,1,0:T(8,128)S(1)} %get-tuple-element.45.stats, bf16[27,128,128]{2,1,0:T(8,128)(2,1)S(1)} %bitcast.34, bf16[384,128]{1,0:T(8,128)(2,1)S(1)} %get-tuple-element.40.refs_0_, bf16[384,128]{1,0:T(8,128)(2,1)S(1)} %collective-permute-done.14.refs_1_, ...), custom_call_target="tpu_custom_call" | custom-call | flops 5435817984 | tf_op jit(solution)/shard_map/pallas_call | solution.py:534
  57.9 2.6 %shard_map.74 = bf16[4,384,128]{2,1,0:T(8,128)(2,1)} custom-call(s32[3]{0:T(128)S(1)} %pad_add_fusion.ids, f32[4,24,128]{2,1,0:T(8,128)S(1)} %get-tuple-element.45.stats, bf16[27,128,128]{2,1,0:T(8,128)(2,1)S(1)} %bitcast.35, bf16[384,128]{1,0:T(8,128)(2,1)S(1)} %collective-permute-done.15.refs_2_.refs_0_, ...), custom_call_target="tpu_custom_call" | custom-call | flops 2717908992 | tf_op jit(solution)/shard_map/pallas_call | solution.py:523
  60.5 0.2 collective-permute-done.22.refs_0_
  60.7 1.1 %collective-permute-done.24.refs_2_ = bf16[432,128]{1,0:T(8,128)(2,1)S(1)} collective-permute-done((bf16[432,128]{1,0:T(8,128)(2,1)S(1)}, bf16[432,128]{1,0:T(8,128)(2,1)S(1)}, u32[]{:S(2)}, u32[]{:S(2)}) %collective-permute-start.24) | collective-permute-done | bytes 110624 | tf_op jit(solution)/shard_map/ppermute | solution.py:35
  61.8 0.7 %shard_map.77 = f32[432,128]{1,0:T(8,128)} custom-call(f32[432,128]{1,0:T(8,128)S(1)} %get-tuple-element.65.own, bf16[432,128]{1,0:T(8,128)(2,1)S(1)} %collective-permute-done.22.refs_0_, bf16[432,128]{1,0:T(8,128)(2,1)S(1)} %collective-permute-done.23.refs_1_, bf16[432,128]{1,0:T(8,128)(2,1)S(1)} %collective-permute-done.24.refs_2_), custom_call_target="tpu_custom_call" | custom-call | tf_op jit(solution)/shard_map/pallas_call | solution.py:605
  (6 shorter events, 0.0 us)
Async XLA Ops:
  2.5 9.4 %collective-permute-start = (bf16[28,32,128]{2,1,0:T(8,128)(2,1)S(1)}, bf16[28,32,128]{2,1,0:T(8,128)(2,1)S(1)}, u32[]{:S(2)}, u32[]{:S(2)}) collective-permute-start(bf16[28,32,128]{2,1,0:T(8,128)(2,1)S(1)} %fusion.refs_0_), channel_id=1, source_target_pairs={{0,8},{8,0},{16,24},{24,16},{1,9},{9,1},{17,25},{25,17},{2,10},{10... | collective-permute-start | bytes 688136 | tf_op jit(solution)/shard_map/ppermute | solution.py:35
  5.5 8.4 %collective-permute-start.7 = (bf16[27,32,128]{2,1,0:T(8,128)(2,1)S(1)}, bf16[27,32,128]{2,1,0:T(8,128)(2,1)S(1)}, u32[]{:S(2)}, u32[]{:S(2)}) collective-permute-start(bf16[27,32,128]{2,1,0:T(8,128)(2,1)S(1)} %get-tuple-element.74.refs_1_), channel_id=1, source_target_pairs={{0,16},{8,24},{16,0},{24,8},{1,17},{9,25},{17,1},{25,9},{2,18},{10... | collective-permute-start | bytes 663560 | tf_op jit(solution)/shard_map/ppermute | solution.py:35
  7.1 8.8 %collective-permute-start.3 = (bf16[27,32,128]{2,1,0:T(8,128)(2,1)S(1)}, bf16[27,32,128]{2,1,0:T(8,128)(2,1)S(1)}, u32[]{:S(2)}, u32[]{:S(2)}) collective-permute-start(bf16[27,32,128]{2,1,0:T(8,128)(2,1)S(1)} %get-tuple-element.74.refs_1_), channel_id=1, source_target_pairs={{0,8},{8,0},{16,24},{24,16},{1,9},{9,1},{17,25},{25,17},{2,10},{10... | collective-permute-start | bytes 663560 | tf_op jit(solution)/shard_map/ppermute | solution.py:35
  7.6 10.0 %collective-permute-start.2 = (bf16[27,32,128]{2,1,0:T(8,128)(2,1)S(1)}, bf16[27,32,128]{2,1,0:T(8,128)(2,1)S(1)}, u32[]{:S(2)}, u32[]{:S(2)}) collective-permute-start(bf16[27,32,128]{2,1,0:T(8,128)(2,1)S(1)} %get-tuple-element.74.refs_1_), channel_id=1, source_target_pairs={{0,1},{1,0},{2,3},{3,2},{4,5},{5,4},{6,7},{7,6},{8,9},{9,8},{10,11... | collective-permute-start | bytes 663560 | tf_op jit(solution)/shard_map/ppermute | solution.py:35
  7.6 11.2 %collective-permute-start.6 = (bf16[28,32,128]{2,1,0:T(8,128)(2,1)S(1)}, bf16[28,32,128]{2,1,0:T(8,128)(2,1)S(1)}, u32[]{:S(2)}, u32[]{:S(2)}) collective-permute-start(bf16[28,32,128]{2,1,0:T(8,128)(2,1)S(1)} %fusion.refs_0_), channel_id=1, source_target_pairs={{0,16},{8,24},{16,0},{24,8},{1,17},{9,25},{17,1},{25,9},{2,18},{10... | collective-permute-start | bytes 688136 | tf_op jit(solution)/shard_map/ppermute | solution.py:35
  12.0 6.8 %collective-permute-start.1 = (bf16[28,32,128]{2,1,0:T(8,128)(2,1)S(1)}, bf16[28,32,128]{2,1,0:T(8,128)(2,1)S(1)}, u32[]{:S(2)}, u32[]{:S(2)}) collective-permute-start(bf16[28,32,128]{2,1,0:T(8,128)(2,1)S(1)} %fusion.refs_0_), channel_id=1, source_target_pairs={{0,1},{1,0},{2,3},{3,2},{4,5},{5,4},{6,7},{7,6},{8,9},{9,8},{10,11... | collective-permute-start | bytes 688136 | tf_op jit(solution)/shard_map/ppermute | solution.py:35
  13.9 8.4 %collective-permute-start.10 = (bf16[28,32,128]{2,1,0:T(8,128)(2,1)S(1)}, bf16[28,32,128]{2,1,0:T(8,128)(2,1)S(1)}, u32[]{:S(2)}, u32[]{:S(2)}) collective-permute-start(bf16[28,32,128]{2,1,0:T(8,128)(2,1)S(1)} %collective-permute-done.refs_4_), channel_id=1, source_target_pairs={{0,16},{8,24},{16,0},{24,8},{1,17},{9,25},{17,1},{25,9},{2,18},{10... | collective-permute-start | bytes 688136 | tf_op jit(solution)/shard_map/ppermute | solution.py:35
  15.9 6.6 %collective-permute-start.11 = (bf16[27,32,128]{2,1,0:T(8,128)(2,1)S(1)}, bf16[27,32,128]{2,1,0:T(8,128)(2,1)S(1)}, u32[]{:S(2)}, u32[]{:S(2)}) collective-permute-start(bf16[27,32,128]{2,1,0:T(8,128)(2,1)S(1)} %collective-permute-done.7.refs_9_), channel_id=1, source_target_pairs={{0,8},{8,0},{16,24},{24,16},{1,9},{9,1},{17,25},{25,17},{2,10},{10... | collective-permute-start | bytes 663560 | tf_op jit(solution)/shard_map/ppermute | solution.py:35
  17.6 5.1 %collective-permute-start.9 = (bf16[27,32,128]{2,1,0:T(8,128)(2,1)S(1)}, bf16[27,32,128]{2,1,0:T(8,128)(2,1)S(1)}, u32[]{:S(2)}, u32[]{:S(2)}) collective-permute-start(bf16[27,32,128]{2,1,0:T(8,128)(2,1)S(1)} %collective-permute-done.7.refs_9_), channel_id=1, source_target_pairs={{0,1},{1,0},{2,3},{3,2},{4,5},{5,4},{6,7},{7,6},{8,9},{9,8},{10,11... | collective-permute-start | bytes 663560 | tf_op jit(solution)/shard_map/ppermute | solution.py:35
  18.8 5.4 %collective-permute-start.8 = (bf16[28,32,128]{2,1,0:T(8,128)(2,1)S(1)}, bf16[28,32,128]{2,1,0:T(8,128)(2,1)S(1)}, u32[]{:S(2)}, u32[]{:S(2)}) collective-permute-start(bf16[28,32,128]{2,1,0:T(8,128)(2,1)S(1)} %collective-permute-done.6.refs_8_), channel_id=1, source_target_pairs={{0,1},{1,0},{2,3},{3,2},{4,5},{5,4},{6,7},{7,6},{8,9},{9,8},{10,11... | collective-permute-start | bytes 688136 | tf_op jit(solution)/shard_map/ppermute | solution.py:35
  18.8 5.4 %collective-permute-start.4 = (bf16[28,32,128]{2,1,0:T(8,128)(2,1)S(1)}, bf16[28,32,128]{2,1,0:T(8,128)(2,1)S(1)}, u32[]{:S(2)}, u32[]{:S(2)}) collective-permute-start(bf16[28,32,128]{2,1,0:T(8,128)(2,1)S(1)} %collective-permute-done.refs_4_), channel_id=1, source_target_pairs={{0,1},{1,0},{2,3},{3,2},{4,5},{5,4},{6,7},{7,6},{8,9},{9,8},{10,11... | collective-permute-start | bytes 688136 | tf_op jit(solution)/shard_map/ppermute | solution.py:35
  22.3 2.3 %collective-permute-start.12 = (bf16[28,32,128]{2,1,0:T(8,128)(2,1)S(1)}, bf16[28,32,128]{2,1,0:T(8,128)(2,1)S(1)}, u32[]{:S(2)}, u32[]{:S(2)}) collective-permute-start(bf16[28,32,128]{2,1,0:T(8,128)(2,1)S(1)} %collective-permute-done.10.refs_12_), channel_id=1, source_target_pairs={{0,1},{1,0},{2,3},{3,2},{4,5},{5,4},{6,7},{7,6},{8,9},{9,8},{10,11... | collective-permute-start | bytes 688136 | tf_op jit(solution)/shard_map/ppermute | solution.py:35
  22.5 1.7 %collective-permute-start.5 = (bf16[27,32,128]{2,1,0:T(8,128)(2,1)S(1)}, bf16[27,32,128]{2,1,0:T(8,128)(2,1)}, u32[]{:S(2)}, u32[]{:S(2)}) collective-permute-start(bf16[27,32,128]{2,1,0:T(8,128)(2,1)S(1)} %collective-permute-done.3.refs_5_), channel_id=1, source_target_pairs={{0,1},{1,0},{2,3},{3,2},{4,5},{5,4},{6,7},{7,6},{8,9},{9,8},{10,11... | collective-permute-start | bytes 663560 | tf_op jit(solution)/shard_map/ppermute | solution.py:35
  22.8 1.7 %collective-permute-start.13 = (bf16[27,32,128]{2,1,0:T(8,128)(2,1)S(1)}, bf16[27,32,128]{2,1,0:T(8,128)(2,1)}, u32[]{:S(2)}, u32[]{:S(2)}) collective-permute-start(bf16[27,32,128]{2,1,0:T(8,128)(2,1)S(1)} %collective-permute-done.11.refs_13_), channel_id=1, source_target_pairs={{0,1},{1,0},{2,3},{3,2},{4,5},{5,4},{6,7},{7,6},{8,9},{9,8},{10,11... | collective-permute-start | bytes 663560 | tf_op jit(solution)/shard_map/ppermute | solution.py:35
  29.8 10.2 %collective-permute-start.14 = (bf16[384,128]{1,0:T(8,128)(2,1)S(1)}, bf16[384,128]{1,0:T(8,128)(2,1)S(1)}, u32[]{:S(2)}, u32[]{:S(2)}) collective-permute-start(bf16[384,128]{1,0:T(8,128)(2,1)S(1)} %get-tuple-element.41), channel_id=1, source_target_pairs={{0,8},{8,0},{16,24},{24,16},{1,9},{9,1},{17,25},{25,17},{2,10},{10... | collective-permute-start | bytes 294920 | tf_op jit(solution)/shard_map/ppermute | solution.py:35
  31.5 8.9 %collective-permute-start.15 = (bf16[384,128]{1,0:T(8,128)(2,1)S(1)}, bf16[384,128]{1,0:T(8,128)(2,1)S(1)}, u32[]{:S(2)}, u32[]{:S(2)}) collective-permute-start(bf16[384,128]{1,0:T(8,128)(2,1)S(1)} %get-tuple-element.42), channel_id=1, source_target_pairs={{0,16},{8,24},{16,0},{24,8},{1,17},{9,25},{17,1},{25,9},{2,18},{10... | collective-permute-start | bytes 294920 | tf_op jit(solution)/shard_map/ppermute | solution.py:35
  33.3 7.1 %collective-permute-start.16 = (bf16[384,128]{1,0:T(8,128)(2,1)S(1)}, bf16[384,128]{1,0:T(8,128)(2,1)S(1)}, u32[]{:S(2)}, u32[]{:S(2)}) collective-permute-start(bf16[384,128]{1,0:T(8,128)(2,1)S(1)} %get-tuple-element.43), channel_id=1, source_target_pairs={{0,24},{8,16},{16,8},{24,0},{1,25},{9,17},{17,9},{25,1},{2,26},{10... | collective-permute-start | bytes 294920 | tf_op jit(solution)/shard_map/ppermute | solution.py:35
  36.8 6.9 %collective-permute-start.17 = (bf16[384,128]{1,0:T(8,128)(2,1)S(1)}, bf16[384,128]{1,0:T(8,128)(2,1)S(1)}, u32[]{:S(2)}, u32[]{:S(2)}) collective-permute-start(bf16[384,128]{1,0:T(8,128)(2,1)S(1)} %get-tuple-element.52), channel_id=1, source_target_pairs={{0,24},{8,16},{16,8},{24,0},{1,25},{9,17},{17,9},{25,1},{2,26},{10... | collective-permute-start | bytes 294920 | tf_op jit(solution)/shard_map/ppermute | solution.py:35
  39.7 4.7 %collective-permute-start.18 = (bf16[384,128]{1,0:T(8,128)(2,1)S(1)}, bf16[384,128]{1,0:T(8,128)(2,1)S(1)}, u32[]{:S(2)}, u32[]{:S(2)}) collective-permute-start(bf16[384,128]{1,0:T(8,128)(2,1)S(1)} %get-tuple-element.53), channel_id=1, source_target_pairs={{0,16},{8,24},{16,0},{24,8},{1,17},{9,25},{17,1},{25,9},{2,18},{10... | collective-permute-start | bytes 294920 | tf_op jit(solution)/shard_map/ppermute | solution.py:35
  40.0 4.6 %collective-permute-start.19 = (bf16[384,128]{1,0:T(8,128)(2,1)S(1)}, bf16[384,128]{1,0:T(8,128)(2,1)S(1)}, u32[]{:S(2)}, u32[]{:S(2)}) collective-permute-start(bf16[384,128]{1,0:T(8,128)(2,1)S(1)} %get-tuple-element.54), channel_id=1, source_target_pairs={{0,8},{8,0},{16,24},{24,16},{1,9},{9,1},{17,25},{25,17},{2,10},{10... | collective-permute-start | bytes 294920 | tf_op jit(solution)/shard_map/ppermute | solution.py:35
  40.4 1.4 %copy-start = (bf16[1,3456,128]{2,1,0:T(8,128)(2,1)S(1)}, bf16[1,3456,128]{2,1,0:T(8,128)(2,1)}, u32[]{:S(2)}) copy-start(bf16[1,3456,128]{2,1,0:T(8,128)(2,1)} %param.6) | copy-start | bytes 2654212
  46.4 1.5 %collective-permute-start.20 = (bf16[2,432,128]{2,1,0:T(8,128)(2,1)S(1)}, bf16[2,432,128]{2,1,0:T(8,128)(2,1)S(1)}, u32[]{:S(2)}, u32[]{:S(2)}) collective-permute-start(bf16[2,432,128]{2,1,0:T(8,128)(2,1)S(1)} %get-tuple-element.59), channel_id=1, source_target_pairs={{0,1},{1,0},{2,3},{3,2},{4,5},{5,4},{6,7},{7,6},{8,9},{9,8},{10,11... | collective-permute-start | bytes 663560 | tf_op jit(solution)/shard_map/ppermute | solution.py:35
  48.0 5.1 %collective-permute-start.21 = (bf16[2,432,128]{2,1,0:T(8,128)(2,1)S(1)}, bf16[2,432,128]{2,1,0:T(8,128)(2,1)S(1)}, u32[]{:S(2)}, u32[]{:S(2)}) collective-permute-start(bf16[2,432,128]{2,1,0:T(8,128)(2,1)S(1)} %get-tuple-element.60), channel_id=1, source_target_pairs={{0,1},{1,0},{2,3},{3,2},{4,5},{5,4},{6,7},{7,6},{8,9},{9,8},{10,11... | collective-permute-start | bytes 663560 | tf_op jit(solution)/shard_map/ppermute | solution.py:35
  49.0 11.7 %collective-permute-start.22 = (bf16[432,128]{1,0:T(8,128)(2,1)S(1)}, bf16[432,128]{1,0:T(8,128)(2,1)S(1)}, u32[]{:S(2)}, u32[]{:S(2)}) collective-permute-start(bf16[432,128]{1,0:T(8,128)(2,1)S(1)} %get-tuple-element.68), channel_id=1, source_target_pairs={{0,4},{1,5},{2,6},{3,7},{4,0},{5,1},{6,2},{7,3},{8,12},{9,13},{10,... | collective-permute-start | bytes 331784 | tf_op jit(solution)/shard_map/ppermute | solution.py:35
  51.7 9.0 %collective-permute-start.23 = (bf16[432,128]{1,0:T(8,128)(2,1)S(1)}, bf16[432,128]{1,0:T(8,128)(2,1)S(1)}, u32[]{:S(2)}, u32[]{:S(2)}) collective-permute-start(bf16[432,128]{1,0:T(8,128)(2,1)S(1)} %get-tuple-element.69), channel_id=1, source_target_pairs={{0,6},{1,7},{2,4},{3,5},{4,2},{5,3},{6,0},{7,1},{8,14},{9,15},{10,... | collective-permute-start | bytes 331784 | tf_op jit(solution)/shard_map/ppermute | solution.py:35
  53.7 8.2 %collective-permute-start.24 = (bf16[432,128]{1,0:T(8,128)(2,1)S(1)}, bf16[432,128]{1,0:T(8,128)(2,1)S(1)}, u32[]{:S(2)}, u32[]{:S(2)}) collective-permute-start(bf16[432,128]{1,0:T(8,128)(2,1)S(1)} %get-tuple-element.70), channel_id=1, source_target_pairs={{0,2},{1,3},{2,0},{3,1},{4,6},{5,7},{6,4},{7,5},{8,10},{9,11},{10,... | collective-permute-start | bytes 331784 | tf_op jit(solution)/shard_map/ppermute | solution.py:35
